TPU v7x, 128 devices: a whole 4x4x4 slice. The times are simulated.
128 devices in a mesh: dp: 2 (over z_hi), blk: 8 (over z_lo, y), uly: 8 (over x, core).
Axes of the slice: x: 4, y: 4, z: 4 (z_hi: 2, z_lo: 2; z = z_hi * 2 + z_lo), core: 2. Of those that a mesh axis runs over, the one named last changes fastest.
Arguments:
- query_rows: bfloat16 [8192, 3072], P(('dp', 'blk', 'uly')), may hold values from -76 to 76
- key_rows: bfloat16 [8192, 3072], P(('dp', 'blk', 'uly')), may hold values from -8 to 8
- value_rows: bfloat16 [8192, 3072], P(('dp', 'blk', 'uly')), may hold values from -6 to 6
- out_grad: bfloat16 [8192, 5120], P(('dp', 'blk', 'uly')), may hold values from -24 to 24
- out_weight: bfloat16 [5120, 3072], P(('dp', 'blk'), 'uly'), may hold values from -2.5 to 2.5
Outputs:
- grad_query: bfloat16 [8192, 3072], P(('dp', 'blk', 'uly'))
- grad_key: bfloat16 [8192, 3072], P(('dp', 'blk', 'uly'))
- grad_value: bfloat16 [8192, 3072], P(('dp', 'blk', 'uly'))
- grad_weight: float32 [5120, 3072], P(('dp', 'blk'), 'uly')
All inputs are finite; a program needn't handle non-finite values.
Results may differ from a plain program's by a relative error of at most 0.0059.
Values may be sent and summed in bfloat16 or wider, within the bound.
No kernel may reach another device: no remote copies, remote signals or barrier semaphores. Data moves between devices by JAX's collectives and lax.ppermute only.
A program may use at most 128 MiB of HBM per device.

v0:
```python
import jax
import jax.numpy as jnp
from jax import lax
from jax.sharding import PartitionSpec as P

HD = 128


def shifted(block, axis, distance):
    devices = range(lax.axis_size(axis))
    route = [((i - distance) % len(devices), i) for i in devices]
    return lax.ppermute(block, axis, route)


def forward_block(softmax_state, queries, keys_now, values_now, score_scale):
    row_max, row_sum, weighted = softmax_state
    scores = (
        jnp.einsum("qhd,khd->hqk", queries, keys_now, preferred_element_type=jnp.float32)
        * score_scale
    )
    new_max = jnp.maximum(row_max, jnp.max(scores, axis=2))
    rescale = jnp.exp(row_max - new_max)
    weights = jnp.exp(scores - new_max[:, :, None])
    row_sum = row_sum * rescale + jnp.sum(weights, axis=2)
    update = jnp.einsum(
        "hqk,khd->qhd", weights, values_now.astype(jnp.float32), precision=lax.Precision.HIGHEST
    )
    weighted = weighted * jnp.transpose(rescale)[:, :, None] + update
    return (new_max, row_sum, weighted)


def backward_block(queries, grad_heads, log_total, row_dot, keys_now, values_now, score_scale):
    scores = (
        jnp.einsum("qhd,khd->hqk", queries, keys_now, preferred_element_type=jnp.float32)
        * score_scale
    )
    probs_full = jnp.exp(scores - log_total[:, :, None])
    probs_low = probs_full.astype(jnp.bfloat16)
    grad_probs = jnp.einsum(
        "qhd,khd->hqk", grad_heads, values_now, preferred_element_type=jnp.float32
    )
    grad_scores = (probs_full * (grad_probs - row_dot[:, :, None])).astype(jnp.bfloat16)
    value_part = jnp.einsum(
        "hqk,qhd->khd", probs_low, grad_heads, preferred_element_type=jnp.float32
    )
    key_part = (
        jnp.einsum("hqk,qhd->khd", grad_scores, queries, preferred_element_type=jnp.float32)
        * score_scale
    )
    query_part = (
        jnp.einsum("hqk,khd->qhd", grad_scores, keys_now, preferred_element_type=jnp.float32)
        * score_scale
    )
    return (query_part, key_part, value_part)


def finish_forward(row_max, row_sum, weighted, grad_heads):
    log_total = row_max + jnp.log(row_sum)
    attn_heads = weighted / jnp.transpose(row_sum)[:, :, None]
    row_dot = jnp.transpose(jnp.sum(grad_heads.astype(jnp.float32) * attn_heads, axis=2))
    return (log_total, attn_heads, row_dot)


def per_device(query_rows, key_rows, value_rows, out_grad, out_weight):
    blocks = lax.axis_size("blk")
    score_scale = HD ** (-0.5)
    local_q, local_k, local_v = (
        lax.all_to_all(query_rows, "uly", split_axis=1, concat_axis=0, tiled=True),
        lax.all_to_all(key_rows, "uly", split_axis=1, concat_axis=0, tiled=True),
        lax.all_to_all(value_rows, "uly", split_axis=1, concat_axis=0, tiled=True),
    )
    block_rows = local_q.shape[0]
    local_width = local_q.shape[1]
    local_heads = local_width // HD
    grad_block = lax.all_gather(out_grad, "uly", axis=0, tiled=True)
    columns = grad_block
    grad_attn = jnp.dot(
        columns,
        lax.all_gather(out_weight, ("dp", "blk"), axis=0, tiled=True),
        preferred_element_type=jnp.float32,
    ).astype(jnp.bfloat16)
    queries = local_q.reshape(block_rows, local_heads, HD)
    keys_home = local_k.reshape(block_rows, local_heads, HD)
    values_home = local_v.reshape(block_rows, local_heads, HD)
    grad_heads = grad_attn.reshape(block_rows, local_heads, HD)
    start_state = (
        jnp.full((local_heads, block_rows), -jnp.inf, jnp.float32),
        jnp.zeros((local_heads, block_rows), jnp.float32),
        jnp.zeros((block_rows, local_heads, HD), jnp.float32),
    )
    zero_grad = jnp.zeros((block_rows, local_heads, HD), jnp.float32)

    def forward_step(step_index, loop_state):
        softmax_state, keys_now, values_now = loop_state
        softmax_state = forward_block(softmax_state, queries, keys_now, values_now, score_scale)
        keys_now, values_now = shifted((keys_now, values_now), "blk", 1)
        return (softmax_state, keys_now, values_now)

    softmax_state, keys_last, values_last = lax.fori_loop(
        0, blocks - 1, forward_step, (start_state, keys_home, values_home)
    )
    row_max, row_sum, weighted = forward_block(
        softmax_state, queries, keys_last, values_last, score_scale
    )
    log_total, attn_heads, row_dot = finish_forward(row_max, row_sum, weighted, grad_heads)

    def pass_grads(key_grad, value_grad):
        return shifted((key_grad, value_grad), "blk", 1)

    def key_step(step_index, loop_state):
        query_grad, keys_now, values_now, key_grad, value_grad = loop_state
        query_part, key_part, value_part = backward_block(
            queries, grad_heads, log_total, row_dot, keys_now, values_now, score_scale
        )
        keys_now, values_now = shifted((keys_now, values_now), "blk", 1)
        key_grad, value_grad = pass_grads(key_grad + key_part, value_grad + value_part)
        return (query_grad + query_part, keys_now, values_now, key_grad, value_grad)

    query_grad, keys_now, values_now, key_grad, value_grad = lax.fori_loop(
        0, blocks - 1, key_step, (zero_grad, keys_home, values_home, zero_grad, zero_grad)
    )
    query_part, key_part, value_part = backward_block(
        queries, grad_heads, log_total, row_dot, keys_now, values_now, score_scale
    )
    query_grad = query_grad + query_part
    key_grad, value_grad = pass_grads(key_grad + key_part, value_grad + value_part)
    query_low = query_grad.astype(jnp.bfloat16).reshape(block_rows, local_width)
    key_low = key_grad.astype(jnp.bfloat16).reshape(block_rows, local_width)
    value_low = value_grad.astype(jnp.bfloat16).reshape(block_rows, local_width)
    grad_query, grad_key, grad_value = (
        lax.all_to_all(query_low, "uly", split_axis=0, concat_axis=1, tiled=True),
        lax.all_to_all(key_low, "uly", split_axis=0, concat_axis=1, tiled=True),
        lax.all_to_all(value_low, "uly", split_axis=0, concat_axis=1, tiled=True),
    )
    attn_out = attn_heads.reshape(block_rows, local_width)
    columns = grad_block.astype(jnp.float32)
    grad_weight = lax.psum_scatter(
        lax.dot_general(
            columns, attn_out, (((0,), (0,)), ((), ())), precision=lax.Precision.HIGHEST
        ),
        ("dp", "blk"),
        scatter_dimension=0,
        tiled=True,
    )
    return (grad_query, grad_key, grad_value, grad_weight)


def solution(mesh):
    in_specs = (
        P(("dp", "blk", "uly"), None),
        P(("dp", "blk", "uly"), None),
        P(("dp", "blk", "uly"), None),
        P(("dp", "blk", "uly"), None),
        P(("dp", "blk"), "uly"),
    )
    out_specs = (
        P(("dp", "blk", "uly"), None),
        P(("dp", "blk", "uly"), None),
        P(("dp", "blk", "uly"), None),
        P(("dp", "blk"), "uly"),
    )
    return jax.shard_map(
        per_device, mesh=mesh, in_specs=in_specs, out_specs=out_specs, check_vma=False
    )
```

profile of v0, /device:TPU:0, one launch (start us, length us, event | category | flops | bytes accessed | tf_op | source)
XLA Modules:
  0.0 712.7 jit_solution(4480987929428811050)
XLA Ops:
  15.9 7.2 %all-to-all-done.2 = bf16[64,8,384]{2,0,1:T(8,128)(2,1)S(1)} async-done(((bf16[64,8,384]{2,0,1:T(8,128)(2,1)}), bf16[64,8,384]{2,0,1:T(8,128)(2,1)S(1)}, u32[]{:S(2)}, u32[]{:S(2)}) %all-to-all-start.2) | async-done | bytes 393248 | tf_op jit(solution)/shard_map/all_to_all | solution.py:68
  27.3 8.1 %all-to-all-done = bf16[64,8,384]{2,0,1:T(8,128)(2,1)S(1)} async-done(((bf16[64,8,384]{2,0,1:T(8,128)(2,1)}), bf16[64,8,384]{2,0,1:T(8,128)(2,1)S(1)}, u32[]{:S(2)}, u32[]{:S(2)}) %all-to-all-start) | async-done | bytes 393248 | tf_op jit(solution)/shard_map/all_to_all | solution.py:69
  41.5 6.2 all-to-all-done.1
  50.3 156.9 %while.38 = (s32[]{:T(128)}, f32[3,512]{1,0:T(4,128)S(1)}, f32[3,512]{1,0:T(4,128)}, f32[512,3,128]{2,0,1:T(8,128)}, bf16[512,3,128]{2,0,1:T(8,128)(2,1)}, /*ind...) while((s32[]{:T(128)}, f32[3,512]{1,0:T(4,128)S(1)}, ...), condition=%wide.region_3.0_spmd.clone, body=%wide.region_0.0_spmd.clone.sunk | while | flops 1415390208 | bytes 17006776 | solution.py:99
  61.7 4.7 fusion.112
  66.4 5.9 collective-permute-done
  72.3 8.1 %collective-permute-done.1 = bf16[512,3,128]{2,0,1:T(8,128)(2,1)} collective-permute-done((bf16[512,3,128]{2,0,1:T(8,128)(2,1)}, bf16[512,3,128]{2,0,1:T(8,128)(2,1)}, u32[]{:S(2)}, u32[]{:S(2)}) %collective-permute-start.1) | collective-permute-done | bytes 393248 | tf_op jit(solution)/shard_map/while/body/eval_jaxpr/ppermute | solution.py:12
  89.5 5.0 fusion.112
  96.6 7.2 %collective-permute-done.1 = bf16[512,3,128]{2,0,1:T(8,128)(2,1)} collective-permute-done((bf16[512,3,128]{2,0,1:T(8,128)(2,1)}, bf16[512,3,128]{2,0,1:T(8,128)(2,1)}, u32[]{:S(2)}, u32[]{:S(2)}) %collective-permute-start.1) | collective-permute-done | bytes 393248 | tf_op jit(solution)/shard_map/while/body/eval_jaxpr/ppermute | solution.py:12
  112.7 4.9 fusion.112
  120.1 6.3 collective-permute-done.1
  135.2 4.9 fusion.112
  142.6 5.4 collective-permute-done.1
  156.8 4.9 fusion.112
  164.2 4.4 collective-permute-done.1
  177.5 4.9 fusion.112
  197.2 4.9 fusion.112
  212.9 6.0 convolution_convert_fusion
  221.9 8.7 %convolution_bitcast_fusion = f32[5120,384]{0,1:T(8,128)} fusion(f32[512,384]{0,1:T(8,128)S(1)} %bitcast.170, bf16[512,5120]{1,0:T(8,128)(2,1)S(1)} %copy-done.4), kind=kOutput, calls=%fused_computation.30 | convolution fusion | flops 12079595520 | bytes 13893632 | tf_op jit(solution)/shard_map/dot_general | solution.py:138
  230.7 9.1 %copy.132 = f32[5120,384]{1,0:T(8,128)} copy(f32[5120,384]{0,1:T(8,128)} %convolution_bitcast_fusion) | data formatting | bytes 15728640
  242.9 409.9 %while.39 = (s32[]{:T(128)}, f32[512,3,128]{2,0,1:T(8,128)}, bf16[512,3,128]{2,0,1:T(8,128)(2,1)S(1)}, bf16[512,3,128]{2,0,1:T(8,128)(2,1)}, f32[512,3,128]{2,0,...) while((s32[]{:T(128)}, f32[512,3,128]{2,0,1:T(8,128)}, ...), condition=%wide.region_8.0_spmd.clone, body=%wide.region_7.0_spmd.clone.sunk | while | flops 1014104064 | bytes 32655648 | solution.py:119
  257.4 68.1 %collective-permute-done.2 = bf16[512,3,128]{2,0,1:T(8,128)(2,1)S(1)} collective-permute-done((bf16[512,3,128]{2,0,1:T(8,128)(2,1)S(1)}, bf16[512,3,128]{2,0,1:T(8,128)(2,1)S(1)}, u32[]{:S(2)}, u32[]{:S(2)}) %collective-permute-start.2) | collective-permute-done | bytes 393248 | tf_op jit(solution)/shard_map/while/body/eval_jaxpr/ppermute | solution.py:12
  325.5 9.3 %collective-permute-done.3 = bf16[512,3,128]{2,0,1:T(8,128)(2,1)} collective-permute-done((bf16[512,3,128]{2,0,1:T(8,128)(2,1)S(1)}, bf16[512,3,128]{2,0,1:T(8,128)(2,1)}, u32[]{:S(2)}, u32[]{:S(2)}) %collective-permute-start.3) | collective-permute-done | bytes 393248 | tf_op jit(solution)/shard_map/while/body/eval_jaxpr/ppermute | solution.py:12
  348.3 35.5 %collective-permute-done.2 = bf16[512,3,128]{2,0,1:T(8,128)(2,1)S(1)} collective-permute-done((bf16[512,3,128]{2,0,1:T(8,128)(2,1)S(1)}, bf16[512,3,128]{2,0,1:T(8,128)(2,1)S(1)}, u32[]{:S(2)}, u32[]{:S(2)}) %collective-permute-start.2) | collective-permute-done | bytes 393248 | tf_op jit(solution)/shard_map/while/body/eval_jaxpr/ppermute | solution.py:12
  403.8 32.6 %collective-permute-done.2 = bf16[512,3,128]{2,0,1:T(8,128)(2,1)S(1)} collective-permute-done((bf16[512,3,128]{2,0,1:T(8,128)(2,1)S(1)}, bf16[512,3,128]{2,0,1:T(8,128)(2,1)S(1)}, u32[]{:S(2)}, u32[]{:S(2)}) %collective-permute-start.2) | collective-permute-done | bytes 393248 | tf_op jit(solution)/shard_map/while/body/eval_jaxpr/ppermute | solution.py:12
  458.2 30.2 %collective-permute-done.2 = bf16[512,3,128]{2,0,1:T(8,128)(2,1)S(1)} collective-permute-done((bf16[512,3,128]{2,0,1:T(8,128)(2,1)S(1)}, bf16[512,3,128]{2,0,1:T(8,128)(2,1)S(1)}, u32[]{:S(2)}, u32[]{:S(2)}) %collective-permute-start.2) | collective-permute-done | bytes 393248 | tf_op jit(solution)/shard_map/while/body/eval_jaxpr/ppermute | solution.py:12
  511.6 31.2 %collective-permute-done.2 = bf16[512,3,128]{2,0,1:T(8,128)(2,1)S(1)} collective-permute-done((bf16[512,3,128]{2,0,1:T(8,128)(2,1)S(1)}, bf16[512,3,128]{2,0,1:T(8,128)(2,1)S(1)}, u32[]{:S(2)}, u32[]{:S(2)}) %collective-permute-start.2) | collective-permute-done | bytes 393248 | tf_op jit(solution)/shard_map/while/body/eval_jaxpr/ppermute | solution.py:12
  564.0 32.0 %collective-permute-done.2 = bf16[512,3,128]{2,0,1:T(8,128)(2,1)S(1)} collective-permute-done((bf16[512,3,128]{2,0,1:T(8,128)(2,1)S(1)}, bf16[512,3,128]{2,0,1:T(8,128)(2,1)S(1)}, u32[]{:S(2)}, u32[]{:S(2)}) %collective-permute-start.2) | collective-permute-done | bytes 393248 | tf_op jit(solution)/shard_map/while/body/eval_jaxpr/ppermute | solution.py:12
  615.6 32.9 %collective-permute-done.2 = bf16[512,3,128]{2,0,1:T(8,128)(2,1)S(1)} collective-permute-done((bf16[512,3,128]{2,0,1:T(8,128)(2,1)S(1)}, bf16[512,3,128]{2,0,1:T(8,128)(2,1)S(1)}, u32[]{:S(2)}, u32[]{:S(2)}) %collective-permute-start.2) | collective-permute-done | bytes 393248 | tf_op jit(solution)/shard_map/while/body/eval_jaxpr/ppermute | solution.py:12
  664.7 7.1 %all-to-all-start.3 = ((bf16[8,64,384]{2,1,0:T(8,128)(2,1)}), bf16[8,64,384]{2,1,0:T(8,128)(2,1)S(1)}, u32[]{:S(2)}, u32[]{:S(2)}) async-start(bf16[8,64,384]{2,1,0:T(8,128)(2,1)} %all_to_all.87), calls=%async_computation.3 | async-start | bytes 786432 | tf_op jit(solution)/shard_map/all_to_all | solution.py:131
  676.0 4.7 all-to-all-done.3
  698.1 7.3 %all-to-all-done.4 = bf16[8,64,384]{2,1,0:T(8,128)(2,1)S(1)} async-done(((bf16[8,64,384]{2,1,0:T(8,128)(2,1)}), bf16[8,64,384]{2,1,0:T(8,128)(2,1)S(1)}, u32[]{:S(2)}, u32[]{:S(2)}) %all-to-all-start.4) | async-done | bytes 393248 | tf_op jit(solution)/shard_map/all_to_all | solution.py:132
  (255 shorter events, 290.8 us)
Async XLA Ops:
  7.2 205.7 %all-gather.5.cloned.1.call-start = ((), (), s32[]{:S(2)}) async-start(), calls=%async_computation.8 | async-start | bytes 4177920 | tf_op jit(solution)/shard_map/all_gather | solution.py:79
  38.8 174.1 %all-gather.3.cloned.1.call-start = ((), (), s32[]{:S(2)}) async-start(), calls=%async_computation.7 | async-start | bytes 5898240 | tf_op jit(solution)/shard_map/all_gather | solution.py:75
  39.6 666.7 %reduce-scatter.4.cloned.1.call-start = ((), (), s32[]{:S(2)}) async-start(), calls=%async_computation.9 | async-start | bytes 8355840
  55.5 24.9 %collective-permute-start.1 = (bf16[512,3,128]{2,0,1:T(8,128)(2,1)}, bf16[512,3,128]{2,0,1:T(8,128)(2,1)}, u32[]{:S(2)}, u32[]{:S(2)}) collective-permute-start(bf16[512,3,128]{2,0,1:T(8,128)(2,1)} %copy.157), channel_id=1, source_target_pairs={{56,0},{0,8},{8,16},{16,24},{24,32},{32,40},{40,48},{48,56},{57,1}... | collective-permute-start | bytes 1179656 | tf_op jit(solution)/shard_map/while/body/eval_jaxpr/ppermute | solution.py:12
  248.3 86.5 %collective-permute-start.4 = (f32[512,3,128]{2,0,1:T(8,128)}, f32[512,3,128]{2,0,1:T(8,128)}, u32[]{:S(2)}, u32[]{:S(2)}) collective-permute-start(f32[512,3,128]{2,0,1:T(8,128)} %fusion.125), channel_id=1, source_target_pairs={{56,0},{0,8},{8,16},{16,24},{24,32},{32,40},{40,48},{48,56},{57,1}... | collective-permute-start | bytes 2359304 | tf_op jit(solution)/shard_map/while/body/eval_jaxpr/ppermute | solution.py:12
  251.5 83.2 %collective-permute-start.5 = (f32[512,3,128]{2,0,1:T(8,128)}, f32[512,3,128]{2,0,1:T(8,128)}, u32[]{:S(2)}, u32[]{:S(2)}) collective-permute-start(f32[512,3,128]{2,0,1:T(8,128)} %fusion.126), channel_id=1, source_target_pairs={{56,0},{0,8},{8,16},{16,24},{24,32},{32,40},{40,48},{48,56},{57,1}... | collective-permute-start | bytes 2359304 | tf_op jit(solution)/shard_map/while/body/eval_jaxpr/ppermute | solution.py:12
  251.5 73.9 %collective-permute-start.2 = (bf16[512,3,128]{2,0,1:T(8,128)(2,1)S(1)}, bf16[512,3,128]{2,0,1:T(8,128)(2,1)S(1)}, u32[]{:S(2)}, u32[]{:S(2)}) collective-permute-start(bf16[512,3,128]{2,0,1:T(8,128)(2,1)S(1)} %copy.172), channel_id=1, source_target_pairs={{56,0},{0,8},{8,16},{16,24},{24,32},{32,40},{40,48},{48,56},{57,1}... | collective-permute-start | bytes 1179656 | tf_op jit(solution)/shard_map/while/body/eval_jaxpr/ppermute | solution.py:12
  251.5 83.2 %collective-permute-start.3 = (bf16[512,3,128]{2,0,1:T(8,128)(2,1)S(1)}, bf16[512,3,128]{2,0,1:T(8,128)(2,1)}, u32[]{:S(2)}, u32[]{:S(2)}) collective-permute-start(bf16[512,3,128]{2,0,1:T(8,128)(2,1)S(1)} %copy.173), channel_id=1, source_target_pairs={{56,0},{0,8},{8,16},{16,24},{24,32},{32,40},{40,48},{48,56},{57,1}... | collective-permute-start | bytes 1179656 | tf_op jit(solution)/shard_map/while/body/eval_jaxpr/ppermute | solution.py:12
  340.2 48.0 %collective-permute-start.4 = (f32[512,3,128]{2,0,1:T(8,128)}, f32[512,3,128]{2,0,1:T(8,128)}, u32[]{:S(2)}, u32[]{:S(2)}) collective-permute-start(f32[512,3,128]{2,0,1:T(8,128)} %fusion.125), channel_id=1, source_target_pairs={{56,0},{0,8},{8,16},{16,24},{24,32},{32,40},{40,48},{48,56},{57,1}... | collective-permute-start | bytes 2359304 | tf_op jit(solution)/shard_map/while/body/eval_jaxpr/ppermute | solution.py:12
  343.4 44.8 %collective-permute-start.5 = (f32[512,3,128]{2,0,1:T(8,128)}, f32[512,3,128]{2,0,1:T(8,128)}, u32[]{:S(2)}, u32[]{:S(2)}) collective-permute-start(f32[512,3,128]{2,0,1:T(8,128)} %fusion.126), channel_id=1, source_target_pairs={{56,0},{0,8},{8,16},{16,24},{24,32},{32,40},{40,48},{48,56},{57,1}... | collective-permute-start | bytes 2359304 | tf_op jit(solution)/shard_map/while/body/eval_jaxpr/ppermute | solution.py:12
  343.5 40.4 %collective-permute-start.2 = (bf16[512,3,128]{2,0,1:T(8,128)(2,1)S(1)}, bf16[512,3,128]{2,0,1:T(8,128)(2,1)S(1)}, u32[]{:S(2)}, u32[]{:S(2)}) collective-permute-start(bf16[512,3,128]{2,0,1:T(8,128)(2,1)S(1)} %copy.172), channel_id=1, source_target_pairs={{56,0},{0,8},{8,16},{16,24},{24,32},{32,40},{40,48},{48,56},{57,1}... | collective-permute-start | bytes 1179656 | tf_op jit(solution)/shard_map/while/body/eval_jaxpr/ppermute | solution.py:12
  343.5 44.7 %collective-permute-start.3 = (bf16[512,3,128]{2,0,1:T(8,128)(2,1)S(1)}, bf16[512,3,128]{2,0,1:T(8,128)(2,1)}, u32[]{:S(2)}, u32[]{:S(2)}) collective-permute-start(bf16[512,3,128]{2,0,1:T(8,128)(2,1)S(1)} %copy.173), channel_id=1, source_target_pairs={{56,0},{0,8},{8,16},{16,24},{24,32},{32,40},{40,48},{48,56},{57,1}... | collective-permute-start | bytes 1179656 | tf_op jit(solution)/shard_map/while/body/eval_jaxpr/ppermute | solution.py:12
  393.6 47.1 %collective-permute-start.4 = (f32[512,3,128]{2,0,1:T(8,128)}, f32[512,3,128]{2,0,1:T(8,128)}, u32[]{:S(2)}, u32[]{:S(2)}) collective-permute-start(f32[512,3,128]{2,0,1:T(8,128)} %fusion.125), channel_id=1, source_target_pairs={{56,0},{0,8},{8,16},{16,24},{24,32},{32,40},{40,48},{48,56},{57,1}... | collective-permute-start | bytes 2359304 | tf_op jit(solution)/shard_map/while/body/eval_jaxpr/ppermute | solution.py:12
  396.9 43.8 %collective-permute-start.5 = (f32[512,3,128]{2,0,1:T(8,128)}, f32[512,3,128]{2,0,1:T(8,128)}, u32[]{:S(2)}, u32[]{:S(2)}) collective-permute-start(f32[512,3,128]{2,0,1:T(8,128)} %fusion.126), channel_id=1, source_target_pairs={{56,0},{0,8},{8,16},{16,24},{24,32},{32,40},{40,48},{48,56},{57,1}... | collective-permute-start | bytes 2359304 | tf_op jit(solution)/shard_map/while/body/eval_jaxpr/ppermute | solution.py:12
  396.9 39.5 %collective-permute-start.2 = (bf16[512,3,128]{2,0,1:T(8,128)(2,1)S(1)}, bf16[512,3,128]{2,0,1:T(8,128)(2,1)S(1)}, u32[]{:S(2)}, u32[]{:S(2)}) collective-permute-start(bf16[512,3,128]{2,0,1:T(8,128)(2,1)S(1)} %copy.172), channel_id=1, source_target_pairs={{56,0},{0,8},{8,16},{16,24},{24,32},{32,40},{40,48},{48,56},{57,1}... | collective-permute-start | bytes 1179656 | tf_op jit(solution)/shard_map/while/body/eval_jaxpr/ppermute | solution.py:12
  396.9 43.8 %collective-permute-start.3 = (bf16[512,3,128]{2,0,1:T(8,128)(2,1)S(1)}, bf16[512,3,128]{2,0,1:T(8,128)(2,1)}, u32[]{:S(2)}, u32[]{:S(2)}) collective-permute-start(bf16[512,3,128]{2,0,1:T(8,128)(2,1)S(1)} %copy.173), channel_id=1, source_target_pairs={{56,0},{0,8},{8,16},{16,24},{24,32},{32,40},{40,48},{48,56},{57,1}... | collective-permute-start | bytes 1179656 | tf_op jit(solution)/shard_map/while/body/eval_jaxpr/ppermute | solution.py:12
  446.1 46.6 %collective-permute-start.4 = (f32[512,3,128]{2,0,1:T(8,128)}, f32[512,3,128]{2,0,1:T(8,128)}, u32[]{:S(2)}, u32[]{:S(2)}) collective-permute-start(f32[512,3,128]{2,0,1:T(8,128)} %fusion.125), channel_id=1, source_target_pairs={{56,0},{0,8},{8,16},{16,24},{24,32},{32,40},{40,48},{48,56},{57,1}... | collective-permute-start | bytes 2359304 | tf_op jit(solution)/shard_map/while/body/eval_jaxpr/ppermute | solution.py:12
  449.3 43.4 %collective-permute-start.5 = (f32[512,3,128]{2,0,1:T(8,128)}, f32[512,3,128]{2,0,1:T(8,128)}, u32[]{:S(2)}, u32[]{:S(2)}) collective-permute-start(f32[512,3,128]{2,0,1:T(8,128)} %fusion.126), channel_id=1, source_target_pairs={{56,0},{0,8},{8,16},{16,24},{24,32},{32,40},{40,48},{48,56},{57,1}... | collective-permute-start | bytes 2359304 | tf_op jit(solution)/shard_map/while/body/eval_jaxpr/ppermute | solution.py:12
  450.7 37.7 %collective-permute-start.2 = (bf16[512,3,128]{2,0,1:T(8,128)(2,1)S(1)}, bf16[512,3,128]{2,0,1:T(8,128)(2,1)S(1)}, u32[]{:S(2)}, u32[]{:S(2)}) collective-permute-start(bf16[512,3,128]{2,0,1:T(8,128)(2,1)S(1)} %copy.172), channel_id=1, source_target_pairs={{56,0},{0,8},{8,16},{16,24},{24,32},{32,40},{40,48},{48,56},{57,1}... | collective-permute-start | bytes 1179656 | tf_op jit(solution)/shard_map/while/body/eval_jaxpr/ppermute | solution.py:12
  451.8 41.0 %collective-permute-start.3 = (bf16[512,3,128]{2,0,1:T(8,128)(2,1)S(1)}, bf16[512,3,128]{2,0,1:T(8,128)(2,1)}, u32[]{:S(2)}, u32[]{:S(2)}) collective-permute-start(bf16[512,3,128]{2,0,1:T(8,128)(2,1)S(1)} %copy.173), channel_id=1, source_target_pairs={{56,0},{0,8},{8,16},{16,24},{24,32},{32,40},{40,48},{48,56},{57,1}... | collective-permute-start | bytes 1179656 | tf_op jit(solution)/shard_map/while/body/eval_jaxpr/ppermute | solution.py:12
  498.2 48.9 %collective-permute-start.4 = (f32[512,3,128]{2,0,1:T(8,128)}, f32[512,3,128]{2,0,1:T(8,128)}, u32[]{:S(2)}, u32[]{:S(2)}) collective-permute-start(f32[512,3,128]{2,0,1:T(8,128)} %fusion.125), channel_id=1, source_target_pairs={{56,0},{0,8},{8,16},{16,24},{24,32},{32,40},{40,48},{48,56},{57,1}... | collective-permute-start | bytes 2359304 | tf_op jit(solution)/shard_map/while/body/eval_jaxpr/ppermute | solution.py:12
  501.5 45.6 %collective-permute-start.5 = (f32[512,3,128]{2,0,1:T(8,128)}, f32[512,3,128]{2,0,1:T(8,128)}, u32[]{:S(2)}, u32[]{:S(2)}) collective-permute-start(f32[512,3,128]{2,0,1:T(8,128)} %fusion.126), channel_id=1, source_target_pairs={{56,0},{0,8},{8,16},{16,24},{24,32},{32,40},{40,48},{48,56},{57,1}... | collective-permute-start | bytes 2359304 | tf_op jit(solution)/shard_map/while/body/eval_jaxpr/ppermute | solution.py:12
  504.0 38.8 %collective-permute-start.2 = (bf16[512,3,128]{2,0,1:T(8,128)(2,1)S(1)}, bf16[512,3,128]{2,0,1:T(8,128)(2,1)S(1)}, u32[]{:S(2)}, u32[]{:S(2)}) collective-permute-start(bf16[512,3,128]{2,0,1:T(8,128)(2,1)S(1)} %copy.172), channel_id=1, source_target_pairs={{56,0},{0,8},{8,16},{16,24},{24,32},{32,40},{40,48},{48,56},{57,1}... | collective-permute-start | bytes 1179656 | tf_op jit(solution)/shard_map/while/body/eval_jaxpr/ppermute | solution.py:12
  505.6 41.4 %collective-permute-start.3 = (bf16[512,3,128]{2,0,1:T(8,128)(2,1)S(1)}, bf16[512,3,128]{2,0,1:T(8,128)(2,1)}, u32[]{:S(2)}, u32[]{:S(2)}) collective-permute-start(bf16[512,3,128]{2,0,1:T(8,128)(2,1)S(1)} %copy.173), channel_id=1, source_target_pairs={{56,0},{0,8},{8,16},{16,24},{24,32},{32,40},{40,48},{48,56},{57,1}... | collective-permute-start | bytes 1179656 | tf_op jit(solution)/shard_map/while/body/eval_jaxpr/ppermute | solution.py:12
  552.5 47.9 %collective-permute-start.4 = (f32[512,3,128]{2,0,1:T(8,128)}, f32[512,3,128]{2,0,1:T(8,128)}, u32[]{:S(2)}, u32[]{:S(2)}) collective-permute-start(f32[512,3,128]{2,0,1:T(8,128)} %fusion.125), channel_id=1, source_target_pairs={{56,0},{0,8},{8,16},{16,24},{24,32},{32,40},{40,48},{48,56},{57,1}... | collective-permute-start | bytes 2359304 | tf_op jit(solution)/shard_map/while/body/eval_jaxpr/ppermute | solution.py:12
  555.7 44.6 %collective-permute-start.5 = (f32[512,3,128]{2,0,1:T(8,128)}, f32[512,3,128]{2,0,1:T(8,128)}, u32[]{:S(2)}, u32[]{:S(2)}) collective-permute-start(f32[512,3,128]{2,0,1:T(8,128)} %fusion.126), channel_id=1, source_target_pairs={{56,0},{0,8},{8,16},{16,24},{24,32},{32,40},{40,48},{48,56},{57,1}... | collective-permute-start | bytes 2359304 | tf_op jit(solution)/shard_map/while/body/eval_jaxpr/ppermute | solution.py:12
  556.2 39.9 %collective-permute-start.2 = (bf16[512,3,128]{2,0,1:T(8,128)(2,1)S(1)}, bf16[512,3,128]{2,0,1:T(8,128)(2,1)S(1)}, u32[]{:S(2)}, u32[]{:S(2)}) collective-permute-start(bf16[512,3,128]{2,0,1:T(8,128)(2,1)S(1)} %copy.172), channel_id=1, source_target_pairs={{56,0},{0,8},{8,16},{16,24},{24,32},{32,40},{40,48},{48,56},{57,1}... | collective-permute-start | bytes 1179656 | tf_op jit(solution)/shard_map/while/body/eval_jaxpr/ppermute | solution.py:12
  558.5 41.9 %collective-permute-start.3 = (bf16[512,3,128]{2,0,1:T(8,128)(2,1)S(1)}, bf16[512,3,128]{2,0,1:T(8,128)(2,1)}, u32[]{:S(2)}, u32[]{:S(2)}) collective-permute-start(bf16[512,3,128]{2,0,1:T(8,128)(2,1)S(1)} %copy.173), channel_id=1, source_target_pairs={{56,0},{0,8},{8,16},{16,24},{24,32},{32,40},{40,48},{48,56},{57,1}... | collective-permute-start | bytes 1179656 | tf_op jit(solution)/shard_map/while/body/eval_jaxpr/ppermute | solution.py:12
  605.8 46.9 %collective-permute-start.4 = (f32[512,3,128]{2,0,1:T(8,128)}, f32[512,3,128]{2,0,1:T(8,128)}, u32[]{:S(2)}, u32[]{:S(2)}) collective-permute-start(f32[512,3,128]{2,0,1:T(8,128)} %fusion.125), channel_id=1, source_target_pairs={{56,0},{0,8},{8,16},{16,24},{24,32},{32,40},{40,48},{48,56},{57,1}... | collective-permute-start | bytes 2359304 | tf_op jit(solution)/shard_map/while/body/eval_jaxpr/ppermute | solution.py:12
  609.0 43.7 %collective-permute-start.5 = (f32[512,3,128]{2,0,1:T(8,128)}, f32[512,3,128]{2,0,1:T(8,128)}, u32[]{:S(2)}, u32[]{:S(2)}) collective-permute-start(f32[512,3,128]{2,0,1:T(8,128)} %fusion.126), channel_id=1, source_target_pairs={{56,0},{0,8},{8,16},{16,24},{24,32},{32,40},{40,48},{48,56},{57,1}... | collective-permute-start | bytes 2359304 | tf_op jit(solution)/shard_map/while/body/eval_jaxpr/ppermute | solution.py:12
  609.0 39.4 %collective-permute-start.2 = (bf16[512,3,128]{2,0,1:T(8,128)(2,1)S(1)}, bf16[512,3,128]{2,0,1:T(8,128)(2,1)S(1)}, u32[]{:S(2)}, u32[]{:S(2)}) collective-permute-start(bf16[512,3,128]{2,0,1:T(8,128)(2,1)S(1)} %copy.172), channel_id=1, source_target_pairs={{56,0},{0,8},{8,16},{16,24},{24,32},{32,40},{40,48},{48,56},{57,1}... | collective-permute-start | bytes 1179656 | tf_op jit(solution)/shard_map/while/body/eval_jaxpr/ppermute | solution.py:12
  610.3 42.4 %collective-permute-start.3 = (bf16[512,3,128]{2,0,1:T(8,128)(2,1)S(1)}, bf16[512,3,128]{2,0,1:T(8,128)(2,1)}, u32[]{:S(2)}, u32[]{:S(2)}) collective-permute-start(bf16[512,3,128]{2,0,1:T(8,128)(2,1)S(1)} %copy.173), channel_id=1, source_target_pairs={{56,0},{0,8},{8,16},{16,24},{24,32},{32,40},{40,48},{48,56},{57,1}... | collective-permute-start | bytes 1179656 | tf_op jit(solution)/shard_map/while/body/eval_jaxpr/ppermute | solution.py:12
  (35 other events, 377.2 us)
Sparse Core Ops, SparseCore 0:
  10.1 59.3 all-gather.4
  71.2 36.2 all-gather.2
  239.9 101.2 reduce-scatter.3
where the time goes:
time: 717 us; the launch traced here: 713 us
  waiting for transfers between devices  398 us (56%)
  matrix products  147 us (21%)
  local copies, waits for them, and re-layouts  67.4 us (9%)
  starting transfers between devices  63.5 us (9%)
  other arithmetic  23.1 us (3%)
  between operations  14.1 us (2%)
    ppermute x44, waiting for transfers between devices, shifted(): return lax.ppermute(block, axis, route)  359 us
    ppermute x44, starting transfers between devices, shifted(): return lax.ppermute(block, axis, route)  38 us
    dot_general x8, matrix products, forward_block(): jnp.einsum('hqk,khd->qhd', weights, values_now.astype(jnp.float32), preci...  37.3 us
    while x35, local copies, waits for them, and re-layouts  32 us
    dot_general x8, matrix products, backward_block(): jnp.einsum('hqk,qhd->khd', probs_low, grad_heads, preferred_element_type=...  24 us
    dot_general x8, matrix products, backward_block(): jnp.einsum('hqk,qhd->khd', grad_scores, queries, preferred_element_type=j...  21.1 us
    dot_general x8, matrix products, backward_block(): jnp.einsum('hqk,khd->qhd', grad_scores, keys_now, preferred_element_type=...  18.2 us
    dot_general x8, matrix products, forward_block(): jnp.einsum('qhd,khd->hqk', queries, keys_now, preferred_element_type=jnp....  16.8 us
  transfers between devices with their start and end apart: 53, of which 35 were waited for; matrix products, arithmetic and copies ran while one was open for 29% of the time, Pallas kernels for 0%

commit v1 on v0

v1 whole, which is shorter than its diff:
```python
import functools

import jax
import jax.numpy as jnp
from jax import lax
from jax.experimental import pallas as pl
from jax.experimental.pallas import tpu as pltpu
from jax.sharding import PartitionSpec as P

HD = 128
HEADS = 3
U = 8
T = 64
W = HEADS * HD
ROWS = U * T
SCALE = HD**-0.5
SCALE2 = SCALE * 1.4426950408889634
BF = jnp.bfloat16
F32 = jnp.float32
VMEM = 48 * 1024 * 1024


def nt(a, b):
    return lax.dot_general(a, b, (((1,), (1,)), ((), ())), preferred_element_type=F32)


def nn(a, b):
    return jnp.dot(a, b, preferred_element_type=F32)


def flat(ref):
    return ref[...].reshape(ROWS, HD)


def forward_kernel(qa, qb, kv0, kv1, kv2, k3, v3, ot_ref, st_ref):
    keys = jnp.concatenate(
        [kv0[:, 0].reshape(ROWS, HD), kv1[:, 0].reshape(ROWS, HD), kv2[:, 0].reshape(ROWS, HD), flat(k3)], axis=0
    )
    values = jnp.concatenate(
        [kv0[:, 1].reshape(ROWS, HD), kv1[:, 1].reshape(ROWS, HD), kv2[:, 1].reshape(ROWS, HD), flat(v3)], axis=0
    )
    values_t = values.T
    for part, q in enumerate((qa, qb)):
        queries = flat(q)
        for tile in range(2):
            at = part * ROWS + tile * 256
            scores = nt(keys, queries[tile * 256 : (tile + 1) * 256])
            top = jnp.max(scores, axis=0, keepdims=True) * SCALE2
            weights = jnp.exp2(scores * SCALE2 - top)
            total = jnp.sum(weights, axis=0, keepdims=True)
            ot_ref[:, at : at + 256] = nn(values_t, weights.astype(BF))
            st_ref[0, 0:1, at : at + 256] = top
            st_ref[0, 1:2, at : at + 256] = total


def head_block(lead, *dims):
    n = len(dims)
    return pl.BlockSpec(tuple(dims) + (HD,), lambda h: (0,) * n + (h,))


Q_SPEC = pl.BlockSpec((U, T, HD), lambda h: (0, 0, h))
KV_SPEC = pl.BlockSpec((U, 2, T, HD), lambda h: (0, 0, 0, h))
OT_SPEC = pl.BlockSpec((HD, 2 * ROWS), lambda h: (h, 0))
ST_SPEC = pl.BlockSpec((1, 8, 2 * ROWS), lambda h: (h, 0, 0))
ROW_SPEC = pl.BlockSpec((ROWS, HD), lambda h: (0, h))
PARAMS = pltpu.CompilerParams(vmem_limit_bytes=VMEM, dimension_semantics=("arbitrary",))


def struct(shape, dtype):
    return jax.ShapeDtypeStruct(shape, dtype)


def cost(flops, nbytes):
    return pl.CostEstimate(flops=flops, bytes_accessed=nbytes, transcendentals=0)


def forward(qa, qb, kv0, kv1, kv2, k3, v3):
    return pl.pallas_call(
        forward_kernel,
        grid=(HEADS,),
        in_specs=[Q_SPEC, Q_SPEC, KV_SPEC, KV_SPEC, KV_SPEC, Q_SPEC, Q_SPEC],
        out_specs=[OT_SPEC, ST_SPEC],
        out_shape=[struct((W, 2 * ROWS), F32), struct((HEADS, 8, 2 * ROWS), F32)],
        compiler_params=PARAMS,
        cost_estimate=cost(2 * 2 * 1024 * 2048 * W, 6 << 20),
        name="attn_forward",
    )(qa, qb, kv0, kv1, kv2, k3, v3)


def dot_kernel(ot_ref, st_ref, da, db, out_ref):
    out_ref[0, 0:2] = st_ref[0, 0:2]
    for part, d in enumerate((da, db)):
        at = slice(part * ROWS, (part + 1) * ROWS)
        grad_t = d[...].astype(F32).T
        out_ref[0, 2:3, at] = jnp.sum(grad_t * ot_ref[:, at], axis=0, keepdims=True)


def row_dots(ot, st, da, db):
    return pl.pallas_call(
        dot_kernel,
        grid=(HEADS,),
        in_specs=[OT_SPEC, ST_SPEC, ROW_SPEC, ROW_SPEC],
        out_specs=ST_SPEC,
        out_shape=struct((HEADS, 8, 2 * ROWS), F32),
        compiler_params=PARAMS,
        cost_estimate=cost(1 << 20, 3 << 20),
        name="row_dots",
    )(ot, st, da, db)


def merge_kernel(ot_ref, st_ref, pst_ref, keep_ref, send_ref, fin_ref):
    mine = st_ref[0]
    other = pst_ref[0]
    other = jnp.concatenate([other[:, ROWS:], other[:, :ROWS]], axis=1)
    top = jnp.maximum(mine[0:1], other[0:1])
    a = jnp.exp2(mine[0:1] - top)
    b = jnp.exp2(other[0:1] - top)
    total = a * mine[1:2] + b * other[1:2]
    fin_ref[0, 0:1] = top + jnp.log2(total)
    fin_ref[0, 1:2] = (a * mine[2:3] + b * other[2:3]) / total
    out_t = ot_ref[...] * (a / total)
    keep_ref[...] = out_t[:, :ROWS].T
    send_ref[...] = out_t[:, ROWS:].T.astype(BF)


def merge(ot, st, pst):
    return pl.pallas_call(
        merge_kernel,
        grid=(HEADS,),
        in_specs=[OT_SPEC, ST_SPEC, ST_SPEC],
        out_specs=[ROW_SPEC, ROW_SPEC, ST_SPEC],
        out_shape=[struct((ROWS, W), F32), struct((ROWS, W), BF), struct((HEADS, 8, 2 * ROWS), F32)],
        compiler_params=PARAMS,
        cost_estimate=cost(1 << 20, 3 << 20),
        name="merge_halves",
    )(ot, st, pst)


CHUNK = 256


def backward_block(keys, values, queries, grads, log_total, row_dot):
    scores = nt(keys, queries)
    probs = jnp.exp2(scores * SCALE2 - log_total)
    grad_probs = nt(values, grads)
    grad_scores = (probs * (grad_probs - row_dot)).astype(BF)
    grad_values = nn(probs.astype(BF), grads)
    grad_keys = nn(grad_scores, queries) * SCALE
    grad_queries_t = nn(keys.T, grad_scores)
    return grad_keys, grad_values, grad_queries_t


def backward_common(qa, qb, da, db, fin):
    queries = jnp.concatenate([flat(qa), flat(qb)], axis=0)
    grads = jnp.concatenate([da[...], db[...]], axis=0)
    return queries, grads, fin[0, 0:1], fin[0, 1:2]


def chunks_of(x):
    return [x[i * CHUNK : (i + 1) * CHUNK] for i in range(ROWS // CHUNK)]


def run_block(keys, values, common):
    dks, dvs, dqt = [], [], None
    for k, v in zip(chunks_of(keys), chunks_of(values)):
        dk, dv, q = backward_block(k, v, *common)
        dks.append(dk)
        dvs.append(dv)
        dqt = q if dqt is None else dqt + q
    return jnp.concatenate(dks, axis=0), jnp.concatenate(dvs, axis=0), dqt


def far_kernel(qa, qb, da, db, fin, k3, v3, dk_ref, dv_ref, dqt_ref):
    common = backward_common(qa, qb, da, db, fin)
    dk, dv, dqt = run_block(flat(k3), flat(v3), common)
    dk_ref[...] = dk.astype(BF).reshape(U, T, HD)
    dv_ref[...] = dv.astype(BF).reshape(U, T, HD)
    dqt_ref[...] = dqt


def near_kernel(qa, qb, da, db, fin, kv1, kv2, dqt_in, o1_ref, o2_ref, dqt_ref):
    common = backward_common(qa, qb, da, db, fin)
    total = dqt_in[...]
    for kv, o in ((kv1, o1_ref), (kv2, o2_ref)):
        dk, dv, dqt = run_block(kv[:, 0].reshape(ROWS, HD), kv[:, 1].reshape(ROWS, HD), common)
        o[:, 0] = dk.astype(o.dtype).reshape(U, T, HD)
        o[:, 1] = dv.astype(o.dtype).reshape(U, T, HD)
        total = total + dqt
    dqt_ref[...] = total


def own_kernel(qa, qb, da, db, fin, kv0, dqt_in, o0_ref, qkeep_ref, qsend_ref):
    common = backward_common(qa, qb, da, db, fin)
    dk, dv, dqt = run_block(kv0[:, 0].reshape(ROWS, HD), kv0[:, 1].reshape(ROWS, HD), common)
    o0_ref[:, 0] = dk.reshape(U, T, HD)
    o0_ref[:, 1] = dv.reshape(U, T, HD)
    total = (dqt_in[...] + dqt) * SCALE
    qkeep_ref[...] = total[:, :ROWS].T.reshape(U, T, HD)
    qsend_ref[...] = total[:, ROWS:].T.astype(BF).reshape(U, T, HD)


COMMON_SPECS = [Q_SPEC, Q_SPEC, ROW_SPEC, ROW_SPEC, ST_SPEC]


def backward_far(common, k3, v3):
    return pl.pallas_call(
        far_kernel,
        grid=(HEADS,),
        in_specs=COMMON_SPECS + [Q_SPEC, Q_SPEC],
        out_specs=[Q_SPEC, Q_SPEC, OT_SPEC],
        out_shape=[struct((U, T, W), BF), struct((U, T, W), BF), struct((W, 2 * ROWS), F32)],
        compiler_params=PARAMS,
        cost_estimate=cost(5 * 2 * 1024 * 512 * W, 6 << 20),
        name="backward_far",
    )(*common, k3, v3)


def backward_near(common, kv1, kv2, dqt):
    return pl.pallas_call(
        near_kernel,
        grid=(HEADS,),
        in_specs=COMMON_SPECS + [KV_SPEC, KV_SPEC, OT_SPEC],
        out_specs=[KV_SPEC, KV_SPEC, OT_SPEC],
        out_shape=[struct((U, 2, T, W), F32), struct((U, 2, T, W), F32), struct((W, 2 * ROWS), F32)],
        compiler_params=PARAMS,
        cost_estimate=cost(5 * 2 * 1024 * 1024 * W, 9 << 20),
        name="backward_near",
    )(*common, kv1, kv2, dqt)


def backward_own(common, kv0, dqt):
    return pl.pallas_call(
        own_kernel,
        grid=(HEADS,),
        in_specs=COMMON_SPECS + [KV_SPEC, OT_SPEC],
        out_specs=[KV_SPEC, Q_SPEC, Q_SPEC],
        out_shape=[struct((U, 2, T, W), F32), struct((U, T, W), F32), struct((U, T, W), BF)],
        compiler_params=PARAMS,
        cost_estimate=cost(5 * 2 * 1024 * 512 * W, 8 << 20),
        name="backward_own",
    )(*common, kv0, dqt)


def move(x, axis, to, n):
    return lax.ppermute(x, axis, [(i, to(i)) for i in range(n)])


def y_shift(x, d):
    return move(x, "blk", lambda i: i // 4 * 4 + (i + d) % 4, 8)


def z_swap(x):
    return move(x, "blk", lambda i: (i + 4) % 8, 8)


def to_heads(*rows):
    parts = [r.reshape(T, U, 1, W) for r in rows]
    stacked = jnp.concatenate(parts, axis=2) if len(parts) > 1 else parts[0]
    return lax.all_to_all(jnp.transpose(stacked, (1, 2, 0, 3)), "uly", split_axis=0, concat_axis=0, tiled=True)


def to_tokens(x):
    got = lax.all_to_all(x, "uly", split_axis=0, concat_axis=0, tiled=True)
    return [jnp.transpose(got[:, i], (1, 0, 2)).reshape(T, U * W) for i in range(x.shape[1])]


def per_device(query_rows, key_rows, value_rows, out_grad, out_weight):
    grad_block = lax.all_gather(out_grad, "uly", axis=0, tiled=True)
    weight = lax.all_gather(out_weight, ("dp", "blk"), axis=0, tiled=True)
    kv0 = to_heads(key_rows, value_rows)
    kv_prev = y_shift(kv0, 1)
    kv_next = y_shift(kv0, -1)
    qa = to_heads(query_rows)[:, 0]
    qb = z_swap(qa)
    k_far = y_shift(kv_prev[:, 0], 1)
    v_far = y_shift(kv_next[:, 1], -1)
    ot, st = forward(qa, qb, kv0, kv_prev, kv_next, k_far, v_far)
    da = nn(grad_block, weight).astype(BF)
    db = z_swap(da)
    st = row_dots(ot, st, da, db)
    pst = z_swap(st)
    o_keep, o_send, fin = merge(ot, st, pst)
    attn_out = (o_keep + z_swap(o_send).astype(F32)).astype(BF)

    common = (qa, qb, da, db, fin)
    dk_far, dv_far, dqt = backward_far(common, k_far, v_far)
    k_got = y_shift(dk_far, 1)
    v_got = y_shift(dv_far, -1)
    g_prev, g_next, dqt = backward_near(common, kv_prev, kv_next, dqt)
    add_k = jnp.stack([k_got, jnp.zeros_like(k_got)], axis=1).astype(F32)
    add_v = jnp.stack([jnp.zeros_like(v_got), v_got], axis=1).astype(F32)
    from_prev = y_shift((g_next + add_k).astype(BF), 1)
    from_next = y_shift((g_prev + add_v).astype(BF), -1)
    g_own, q_keep, q_send = backward_own(common, kv0, dqt)
    dq = (q_keep + z_swap(q_send).astype(F32)).astype(BF)
    (grad_query,) = to_tokens(dq[:, None])
    dkv = (g_own + from_prev.astype(F32) + from_next.astype(F32)).astype(BF)
    grad_key, grad_value = to_tokens(dkv)

    partial = lax.dot_general(grad_block, attn_out, (((0,), (0,)), ((), ())), preferred_element_type=F32)
    pieces = lax.all_to_all(partial.astype(BF), ("dp", "blk"), split_axis=0, concat_axis=0, tiled=True)
    grad_weight = jnp.sum(pieces.reshape(16, 320, W).astype(F32), axis=0)
    return (grad_query, grad_key, grad_value, grad_weight)


def solution(mesh):
    rows = P(("dp", "blk", "uly"), None)
    weight = P(("dp", "blk"), "uly")
    return jax.shard_map(
        per_device,
        mesh=mesh,
        in_specs=(rows, rows, rows, rows, weight),
        out_specs=(rows, rows, rows, weight),
        check_vma=False,
    )
```

time: 717 us -> 296 us (0.41)
  waiting for transfers between devices: 398 us -> 140 us
  matrix products: 147 us -> 13.4 us
  local copies, waits for them, and re-layouts: 67.4 us -> 16.3 us
  Pallas kernels: 0 us -> 40.6 us
  starting transfers between devices: 63.5 us -> 31.6 us
  blocking collectives: 0 us -> 28.8 us
  other arithmetic: 23.1 us -> 10.4 us
    ppermute x44 -> x13, waiting for transfers between devices: 359 us -> 23.4 us  [move(): return lax.ppermute(x, axis, [(i, to(i)) for i in range(n)])]
    dot_general x58 -> x2, matrix products: 147 us -> 13.4 us  [the longest x1 6.83 us: per_device(): lax.dot_general(grad_block, attn_out, (((0,), (0,)), ((), ())), preferred...]
    pallas_call x0 -> x6, Pallas kernels: none -> 40.6 us  [the longest x1 16.9 us: forward(): pl.pallas_call(forward_kernel, grid=(HEADS,), in_specs=[Q_SPEC, Q_SPEC, K...]
    all_gather x1, waiting for transfers between devices: 0.01 us -> 37.5 us  [per_device(): grad_block = lax.all_gather(out_grad, 'uly', axis=0, tiled=True)]
    while x38 -> x0, local copies, waits for them, and re-layouts: 36 us -> none
    all_to_all x0 -> x2, blocking collectives: none -> 28.8 us  [to_heads(): lax.all_to_all(jnp.transpose(stacked, (1, 2, 0, 3)), 'uly', split_axis=0,...]
    all_to_all x6 -> x3, waiting for transfers between devices: 37.6 us -> 63.7 us  [the longest x1 57.9 us: per_device(): lax.all_to_all(partial.astype(BF), ('dp', 'blk'), split_axis=0, concat_ax...]
    ppermute x44 -> x13, starting transfers between devices: 38 us -> 17.9 us  [move(): return lax.ppermute(x, axis, [(i, to(i)) for i in range(n)])]
  transfers between devices with their start and end apart: 53 -> 18, of which waited for: 35 -> 7; matrix products, arithmetic and copies ran while one was open for 29% -> 11% of each run, Pallas kernels for 0% -> 11%
where the time goes in v1:
time: 296 us; the launch traced here: 295 us
  waiting for transfers between devices  140 us (47%)
  Pallas kernels  40.6 us (14%)
  starting transfers between devices  31.6 us (11%)
  blocking collectives  28.8 us (10%)
  local copies, waits for them, and re-layouts  16.3 us (6%)
  between operations  14.3 us (5%)
  matrix products  13.4 us (5%)
  other arithmetic  10.4 us (4%)
    all_to_all x1, waiting for transfers between devices, per_device(): lax.all_to_all(partial.astype(BF), ('dp', 'blk'), split_axis=0, concat_ax...  57.9 us
    all_gather x1, waiting for transfers between devices, per_device(): grad_block = lax.all_gather(out_grad, 'uly', axis=0, tiled=True)  37.5 us
    all_to_all x2, blocking collectives, to_heads(): lax.all_to_all(jnp.transpose(stacked, (1, 2, 0, 3)), 'uly', split_axis=0,...  28.8 us
    ppermute x13, waiting for transfers between devices, move(): return lax.ppermute(x, axis, [(i, to(i)) for i in range(n)])  23.4 us
    ppermute x13, starting transfers between devices, move(): return lax.ppermute(x, axis, [(i, to(i)) for i in range(n)])  17.9 us
    pallas_call x1, Pallas kernels, forward(): pl.pallas_call(forward_kernel, grid=(HEADS,), in_specs=[Q_SPEC, Q_SPEC, K...  16.9 us
    all_gather x1, waiting for transfers between devices, per_device(): weight = lax.all_gather(out_weight, ('dp', 'blk'), axis=0, tiled=True)  13.8 us
    pallas_call x1, Pallas kernels, backward_near(): pl.pallas_call(near_kernel, grid=(HEADS,), in_specs=COMMON_SPECS + [KV_SP...  10.7 us
  transfers between devices with their start and end apart: 18, of which 7 were waited for; matrix products, arithmetic and copies ran while one was open for 11% of the time, Pallas kernels for 11%

profile of v1, /device:TPU:0, one launch (start us, length us, event | category | flops | bytes accessed | tf_op | source)
XLA Modules:
  0.0 295.1 jit_solution(12562263219019403687)
XLA Ops:
  8.7 1.0 copy.28
  9.8 1.0 copy.29
  11.0 17.4 %all_to_all.29.kv0 = bf16[8,2,64,384]{3,2,1,0:T(8,128)(2,1)S(1)} all-to-all(bf16[8,2,64,384]{3,2,1,0:T(8,128)(2,1)S(1)} %maximum_bitcast_fusion), channel_id=1, replica_groups=mesh['dp'=2,'blk'=8,'uly'=8] {'uly'}, dimensions={0} | all-to-all | bytes 1572864 | tf_op jit(solution)/shard_map/all_to_all | solution.py:259
  28.4 3.0 %collective-permute-start.3 = (bf16[8,2,64,384]{3,2,1,0:T(8,128)(2,1)S(1)}, bf16[8,2,64,384]{3,2,1,0:T(8,128)(2,1)S(1)}, u32[]{:S(2)}, u32[]{:S(2)}) collective-permute-start(bf16[8,2,64,384]{3,2,1,0:T(8,128)(2,1)S(1)} %all_to_all.29.kv0), channel_id=1, source_target_pairs={{0,24},{8,0},{16,8},{24,16},{32,56},{40,32},{48,40},{56,48},{1,25}... | collective-permute-start | bytes 2359304 | tf_op jit(solution)/shard_map/ppermute | solution.py:245
  31.5 11.3 %all_to_all.30 = bf16[8,1,64,384]{3,2,1,0:T(8,128)(2,1)S(1)} all-to-all(bf16[8,1,64,384]{3,2,1,0:T(8,128)(2,1)S(1)} %copy.16), channel_id=1, replica_groups=mesh['dp'=2,'blk'=8,'uly'=8] {'uly'}, dimensions={0} | all-to-all | bytes 786432 | tf_op jit(solution)/shard_map/all_to_all | solution.py:259
  42.9 1.9 collective-permute-start
  44.8 10.4 %collective-permute-done.3.kv2 = bf16[8,2,64,384]{3,2,1,0:T(8,128)(2,1)S(1)} collective-permute-done((bf16[8,2,64,384]{3,2,1,0:T(8,128)(2,1)S(1)}, bf16[8,2,64,384]{3,2,1,0:T(8,128)(2,1)S(1)}, u32[]{:S(2)}, u32[]{:S(2)}) %collective-permute-start.3) | collective-permute-done | bytes 786464 | tf_op jit(solution)/shard_map/ppermute | solution.py:245
  55.9 3.7 %collective-permute-start.5 = (bf16[8,64,384]{2,1,0:T(8,128)(2,1)}, bf16[8,64,384]{2,1,0:T(8,128)(2,1)S(1)}, u32[]{:S(2)}, u32[]{:S(2)}) collective-permute-start(bf16[8,64,384]{2,1,0:T(8,128)(2,1)} %slice_bitcast_fusion.2), channel_id=1, source_target_pairs={{0,24},{8,0},{16,8},{24,16},{32,56},{40,32},{48,40},{56,48},{1,25}... | collective-permute-start | bytes 1179656 | tf_op jit(solution)/shard_map/ppermute | solution.py:245
  60.4 13.8 %all-gather.5.cloned.1.call-done = bf16[5120,384]{1,0:T(8,128)(2,1)} async-done(((bf16[320,384]{1,0:T(8,128)(2,1)}), bf16[5120,384]{1,0:T(8,128)(2,1)}) %all-gather.5.cloned.1.call-update) | async-done | bytes 3932176 | tf_op jit(solution)/shard_map/all_gather | solution.py:269
  74.3 37.5 %all-gather.3.cloned.1.call-done = bf16[512,5120]{1,0:T(8,128)(2,1)} async-done(((bf16[64,5120]{1,0:T(8,128)(2,1)}), bf16[512,5120]{1,0:T(8,128)(2,1)}) %all-gather.3.cloned.1.call-update) | async-done | bytes 5242896 | tf_op jit(solution)/shard_map/all_gather | solution.py:268
  111.8 6.5 %convolution_convert_fusion.1.da = bf16[512,384]{1,0:T(8,128)(2,1)S(1)} fusion(bf16[512,5120]{1,0:T(8,128)(2,1)} %all-gather.3.cloned.1.call-done, bf16[5120,384]{1,0:T(8,128)(2,1)} %all-gather.5.cloned.1.call-done), kind=kOutput, calls=%fused_computation.6 | convolution fusion | flops 2013462528 | bytes 9568256 | tf_op jit(solution)/shard_map/dot_general | solution.py:28
  118.3 1.6 collective-permute-start.1
  121.7 16.9 %attn_forward.1 = (f32[384,1024]{1,0:T(8,128)S(1)}, f32[3,8,1024]{2,1,0:T(8,128)S(1)}) custom-call(bf16[8,64,384]{2,1,0:T(8,128)(2,1)S(1)} %bitcast.51, bf16[8,64,384]{2,1,0:T(8,128)(2,1)S(1)} %collective-permute-done.qb, bf16[8,2,64,384]{3,2,1,0:T(8,128)(2,1)S(1)} %all_to_all.29.kv0, bf16[8,2,64,384]{3,2,1,0:T(8,128)(2,1)S(1)} %collective-permute-done.2.kv1, ...), custom_call_target="tpu_custom_call" | custom-call | flops 3221225472 | bytes 6291456 | tf_op jit(solution)/shard_map/attn_forward/pallas_call | solution.py:78
  139.9 4.2 %collective-permute-done.6.pst_ref = f32[3,8,1024]{2,1,0:T(8,128)S(1)} collective-permute-done((f32[3,8,1024]{2,1,0:T(8,128)S(1)}, f32[3,8,1024]{2,1,0:T(8,128)S(1)}, u32[]{:S(2)}, u32[]{:S(2)}) %collective-permute-start.6) | collective-permute-done | bytes 98336 | tf_op jit(solution)/shard_map/ppermute | solution.py:245
  145.5 5.5 %backward_far.1 = (bf16[8,64,384]{2,1,0:T(8,128)(2,1)S(1)}, bf16[8,64,384]{2,1,0:T(8,128)(2,1)S(1)}, f32[384,1024]{1,0:T(8,128)S(1)}) custom-call(bf16[8,64,384]{2,1,0:T(8,128)(2,1)S(1)} %bitcast.52, bf16[8,64,384]{2,1,0:T(8,128)(2,1)S(1)} %copy-done.1, bf16[512,384]{1,0:T(8,128)(2,1)S(1)} %convolution_convert_fusion.1.da, ...), custom_call_target="tpu_custom_call" | custom-call | flops 2013265920 | bytes 6291456 | tf_op jit(solution)/shard_map/backward_far/pallas_call | solution.py:206
  151.1 1.2 copy-done.6
  152.2 2.7 collective-permute-start.10
  155.0 10.7 %backward_near.1 = (f32[8,2,64,384]{3,2,1,0:T(8,128)S(1)}, f32[8,2,64,384]{3,2,1,0:T(8,128)}, f32[384,1024]{1,0:T(8,128)}) custom-call(bf16[8,64,384]{2,1,0:T(8,128)(2,1)S(1)} %bitcast.53, bf16[8,64,384]{2,1,0:T(8,128)(2,1)S(1)} %copy-done.1, bf16[512,384]{1,0:T(8,128)(2,1)S(1)} %convolution_convert_fusion.1.da, ...), custom_call_target="tpu_custom_call" | custom-call | flops 4026531840 | bytes 9437184 | tf_op jit(solution)/shard_map/backward_near/pallas_call | solution.py:219
  165.7 1.0 add_convert_fusion.1
  166.7 3.2 %collective-permute-start.11 = (bf16[8,2,64,384]{3,2,1,0:T(8,128)(2,1)}, bf16[8,2,64,384]{3,2,1,0:T(8,128)(2,1)}, u32[]{:S(2)}, u32[]{:S(2)}) collective-permute-start(bf16[8,2,64,384]{3,2,1,0:T(8,128)(2,1)} %add_convert_fusion.1), channel_id=1, source_target_pairs={{0,24},{8,0},{16,8},{24,16},{32,56},{40,32},{48,40},{56,48},{1,25}... | collective-permute-start | bytes 2359304 | tf_op jit(solution)/shard_map/ppermute | solution.py:245
  169.9 2.4 add_convert_fusion.2
  172.4 6.2 %backward_own.1 = (f32[8,2,64,384]{3,2,1,0:T(8,128)S(1)}, f32[8,64,384]{2,1,0:T(8,128)S(1)}, bf16[8,64,384]{2,1,0:T(8,128)(2,1)S(1)}) custom-call(bf16[8,64,384]{2,1,0:T(8,128)(2,1)S(1)} %bitcast.54, bf16[8,64,384]{2,1,0:T(8,128)(2,1)S(1)} %copy-done.1, bf16[512,384]{1,0:T(8,128)(2,1)S(1)} %convolution_convert_fusion.1.da, ...), custom_call_target="tpu_custom_call" | custom-call | flops 2013265920 | bytes 8388608 | tf_op jit(solution)/shard_map/backward_own/pallas_call | solution.py:232
  179.1 8.8 %collective-permute-done.7 = bf16[8,64,384]{2,1,0:T(8,128)(2,1)S(1)} collective-permute-done((bf16[8,64,384]{2,1,0:T(8,128)(2,1)S(1)}, bf16[8,64,384]{2,1,0:T(8,128)(2,1)S(1)}, u32[]{:S(2)}, u32[]{:S(2)}) %collective-permute-start.7) | collective-permute-done | bytes 393248 | tf_op jit(solution)/shard_map/ppermute | solution.py:245
  188.8 3.5 %all-to-all-start.2 = ((bf16[8,1,64,384]{3,2,1,0:T(8,128)(2,1)}), bf16[8,1,64,384]{3,2,1,0:T(8,128)(2,1)S(1)}, u32[]{:S(2)}, u32[]{:S(2)}) async-start(bf16[8,1,64,384]{3,2,1,0:T(8,128)(2,1)} %fusion.1), calls=%async_computation.2 | async-start | bytes 786432 | tf_op jit(solution)/shard_map/all_to_all | solution.py:263
  192.8 2.6 add_convert_fusion
  195.3 5.8 %all-to-all-done.2 = bf16[8,1,64,384]{3,2,1,0:T(8,128)(2,1)S(1)} async-done(((bf16[8,1,64,384]{3,2,1,0:T(8,128)(2,1)}), bf16[8,1,64,384]{3,2,1,0:T(8,128)(2,1)S(1)}, u32[]{:S(2)}, u32[]{:S(2)}) %all-to-all-start.2) | async-done | bytes 393248 | tf_op jit(solution)/shard_map/all_to_all | solution.py:263
  201.1 3.5 %all-to-all-start.3 = ((bf16[8,2,64,384]{3,2,1,0:T(8,128)(2,1)}), bf16[8,2,64,384]{3,2,1,0:T(8,128)(2,1)S(1)}, u32[]{:S(2)}, u32[]{:S(2)}) async-start(bf16[8,2,64,384]{3,2,1,0:T(8,128)(2,1)} %add_convert_fusion), calls=%async_computation.3 | async-start | bytes 1572864 | tf_op jit(solution)/shard_map/all_to_all | solution.py:263
  204.6 6.8 %fusion = bf16[5120,384]{0,1:T(8,128)(2,1)} fusion(bf16[512,5120]{1,0:T(8,128)(2,1)} %all-gather.3.cloned.1.call-done, f32[512,384]{1,0:T(8,128)S(1)} %get-tuple-element.30, bf16[512,384]{1,0:T(8,128)(2,1)} %collective-permute-done.12), kind=kOutput, calls=%fused_computation.2 | convolution fusion | flops 2015821824 | bytes 10354688 | tf_op jit(solution)/shard_map/dot_general | solution.py:300
  211.5 6.3 %copy.23 = bf16[5120,384]{1,0:T(8,128)(2,1)} copy(bf16[5120,384]{0,1:T(8,128)(2,1)} %fusion) | data formatting | bytes 7864320 | tf_op jit(solution)/shard_map/convert_element_type | solution.py:301
  217.7 6.7 %all-to-all-start.4 = ((bf16[16,320,384]{2,1,0:T(8,128)(2,1)}), bf16[16,320,384]{2,1,0:T(8,128)(2,1)}, u32[]{:S(2)}, u32[]{:S(2)}) async-start(bf16[16,320,384]{2,1,0:T(8,128)(2,1)} %bitcast.55), calls=%async_computation.4 | async-start | bytes 7864320 | tf_op jit(solution)/shard_map/all_to_all | solution.py:301
  226.9 57.9 %all-to-all-done.4 = bf16[16,320,384]{2,1,0:T(8,128)(2,1)} async-done(((bf16[16,320,384]{2,1,0:T(8,128)(2,1)}), bf16[16,320,384]{2,1,0:T(8,128)(2,1)}, u32[]{:S(2)}, u32[]{:S(2)}) %all-to-all-start.4) | async-done | bytes 3932192 | tf_op jit(solution)/shard_map/all_to_all | solution.py:301
  284.8 3.5 %convert_reduce_fusion = f32[320,384]{1,0:T(8,128)} fusion(bf16[16,320,384]{2,1,0:T(8,128)(2,1)} %all-to-all-done.4), kind=kLoop, calls=%fused_computation | loop fusion | flops 3809280 | bytes 4423680 | tf_op jit(solution)/shard_map/reduce_sum | solution.py:302
  (51 shorter events, 12.1 us)
Async XLA Ops:
  7.2 24.3 %copy-start.7 = (bf16[64,3072]{1,0:T(8,128)(2,1)S(1)}, bf16[64,3072]{1,0:T(8,128)(2,1)}, u32[]{:S(2)}) copy-start(bf16[64,3072]{1,0:T(8,128)(2,1)} %param.5) | copy-start | bytes 1179652
  7.2 67.1 %all-gather.5.cloned.1.call-start = ((), (), s32[]{:S(2)}) async-start(), calls=%async_computation.6 | async-start | bytes 4177920 | tf_op jit(solution)/shard_map/all_gather | solution.py:269
  7.9 103.8 %all-gather.3.cloned.1.call-start = ((), (), s32[]{:S(2)}) async-start(), calls=%async_computation.5 | async-start | bytes 5898240 | tf_op jit(solution)/shard_map/all_gather | solution.py:268
  28.4 26.7 %collective-permute-start.3 = (bf16[8,2,64,384]{3,2,1,0:T(8,128)(2,1)S(1)}, bf16[8,2,64,384]{3,2,1,0:T(8,128)(2,1)S(1)}, u32[]{:S(2)}, u32[]{:S(2)}) collective-permute-start(bf16[8,2,64,384]{3,2,1,0:T(8,128)(2,1)S(1)} %all_to_all.29.kv0), channel_id=1, source_target_pairs={{0,24},{8,0},{16,8},{24,16},{32,56},{40,32},{48,40},{56,48},{1,25}... | collective-permute-start | bytes 2359304 | tf_op jit(solution)/shard_map/ppermute | solution.py:245
  31.4 28.2 %collective-permute-start.2 = (bf16[8,2,64,384]{3,2,1,0:T(8,128)(2,1)S(1)}, bf16[8,2,64,384]{3,2,1,0:T(8,128)(2,1)S(1)}, u32[]{:S(2)}, u32[]{:S(2)}) collective-permute-start(bf16[8,2,64,384]{3,2,1,0:T(8,128)(2,1)S(1)} %all_to_all.29.kv0), channel_id=1, source_target_pairs={{0,8},{8,16},{16,24},{24,0},{32,40},{40,48},{48,56},{56,32},{1,9},... | collective-permute-start | bytes 2359304 | tf_op jit(solution)/shard_map/ppermute | solution.py:245
  42.9 77.1 %collective-permute-start = (bf16[8,64,384]{2,1,0:T(8,128)(2,1)S(1)}, bf16[8,64,384]{2,1,0:T(8,128)(2,1)S(1)}, u32[]{:S(2)}, u32[]{:S(2)}) collective-permute-start(bf16[8,64,384]{2,1,0:T(8,128)(2,1)S(1)} %bitcast.50), channel_id=1, source_target_pairs={{0,32},{8,40},{16,48},{24,56},{32,0},{40,8},{48,16},{56,24},{1,33}... | collective-permute-start | bytes 1179656 | tf_op jit(solution)/shard_map/ppermute | solution.py:245
  55.9 64.0 %collective-permute-start.5 = (bf16[8,64,384]{2,1,0:T(8,128)(2,1)}, bf16[8,64,384]{2,1,0:T(8,128)(2,1)S(1)}, u32[]{:S(2)}, u32[]{:S(2)}) collective-permute-start(bf16[8,64,384]{2,1,0:T(8,128)(2,1)} %slice_bitcast_fusion.2), channel_id=1, source_target_pairs={{0,24},{8,0},{16,8},{24,16},{32,56},{40,32},{48,40},{56,48},{1,25}... | collective-permute-start | bytes 1179656 | tf_op jit(solution)/shard_map/ppermute | solution.py:245
  60.4 60.3 %collective-permute-start.4 = (bf16[8,64,384]{2,1,0:T(8,128)(2,1)}, bf16[8,64,384]{2,1,0:T(8,128)(2,1)}, u32[]{:S(2)}, u32[]{:S(2)}) collective-permute-start(bf16[8,64,384]{2,1,0:T(8,128)(2,1)} %slice_bitcast_fusion.3), channel_id=1, source_target_pairs={{0,8},{8,16},{16,24},{24,0},{32,40},{40,48},{48,56},{56,32},{1,9},... | collective-permute-start | bytes 1179656 | tf_op jit(solution)/shard_map/ppermute | solution.py:245
  118.3 20.3 %collective-permute-start.1 = (bf16[512,384]{1,0:T(8,128)(2,1)S(1)}, bf16[512,384]{1,0:T(8,128)(2,1)S(1)}, u32[]{:S(2)}, u32[]{:S(2)}) collective-permute-start(bf16[512,384]{1,0:T(8,128)(2,1)S(1)} %convolution_convert_fusion.1.da), channel_id=1, source_target_pairs={{0,32},{8,40},{16,48},{24,56},{32,0},{40,8},{48,16},{56,24},{1,33}... | collective-permute-start | bytes 1179656 | tf_op jit(solution)/shard_map/ppermute | solution.py:245
  119.9 18.7 %copy-start = (bf16[8,64,384]{2,1,0:T(8,128)(2,1)}, bf16[8,64,384]{2,1,0:T(8,128)(2,1)S(1)}, u32[]{:S(2)}) copy-start(bf16[8,64,384]{2,1,0:T(8,128)(2,1)S(1)} %collective-permute-done.qb) | copy-start | bytes 1179652
  119.9 0.8 copy-start.3
  120.7 1.0 copy-start.4
  138.6 6.9 %copy-start.5 = (bf16[8,64,384]{2,1,0:T(8,128)(2,1)S(1)}, bf16[8,64,384]{2,1,0:T(8,128)(2,1)}, u32[]{:S(2)}) copy-start(bf16[8,64,384]{2,1,0:T(8,128)(2,1)} %copy-done.3) | copy-start | bytes 1179652
  138.6 6.9 %copy-start.1 = (bf16[8,64,384]{2,1,0:T(8,128)(2,1)S(1)}, bf16[8,64,384]{2,1,0:T(8,128)(2,1)}, u32[]{:S(2)}) copy-start(bf16[8,64,384]{2,1,0:T(8,128)(2,1)} %copy-done) | copy-start | bytes 1179652
  139.3 4.8 %collective-permute-start.6 = (f32[3,8,1024]{2,1,0:T(8,128)S(1)}, f32[3,8,1024]{2,1,0:T(8,128)S(1)}, u32[]{:S(2)}, u32[]{:S(2)}) collective-permute-start(f32[3,8,1024]{2,1,0:T(8,128)S(1)} %row_dots.1.st_ref), channel_id=1, source_target_pairs={{0,32},{8,40},{16,48},{24,56},{32,0},{40,8},{48,16},{56,24},{1,33}... | collective-permute-start | bytes 294920 | tf_op jit(solution)/shard_map/ppermute | solution.py:245
  144.8 0.7 copy-start.2
  151.1 1.2 copy-start.6
  152.2 13.4 %collective-permute-start.10 = (bf16[8,64,384]{2,1,0:T(8,128)(2,1)S(1)}, bf16[8,64,384]{2,1,0:T(8,128)(2,1)S(1)}, u32[]{:S(2)}, u32[]{:S(2)}) collective-permute-start(bf16[8,64,384]{2,1,0:T(8,128)(2,1)S(1)} %get-tuple-element.29), channel_id=1, source_target_pairs={{0,24},{8,0},{16,8},{24,16},{32,56},{40,32},{48,40},{56,48},{1,25}... | collective-permute-start | bytes 1179656 | tf_op jit(solution)/shard_map/ppermute | solution.py:245
  155.0 14.9 %collective-permute-start.8 = (bf16[8,64,384]{2,1,0:T(8,128)(2,1)S(1)}, bf16[8,64,384]{2,1,0:T(8,128)(2,1)S(1)}, u32[]{:S(2)}, u32[]{:S(2)}) collective-permute-start(bf16[8,64,384]{2,1,0:T(8,128)(2,1)S(1)} %get-tuple-element.27), channel_id=1, source_target_pairs={{0,8},{8,16},{16,24},{24,0},{32,40},{40,48},{48,56},{56,32},{1,9},... | collective-permute-start | bytes 1179656 | tf_op jit(solution)/shard_map/ppermute | solution.py:245
  166.7 26.1 %collective-permute-start.11 = (bf16[8,2,64,384]{3,2,1,0:T(8,128)(2,1)}, bf16[8,2,64,384]{3,2,1,0:T(8,128)(2,1)}, u32[]{:S(2)}, u32[]{:S(2)}) collective-permute-start(bf16[8,2,64,384]{3,2,1,0:T(8,128)(2,1)} %add_convert_fusion.1), channel_id=1, source_target_pairs={{0,24},{8,0},{16,8},{24,16},{32,56},{40,32},{48,40},{56,48},{1,25}... | collective-permute-start | bytes 2359304 | tf_op jit(solution)/shard_map/ppermute | solution.py:245
  172.4 20.4 %collective-permute-start.9 = (bf16[8,2,64,384]{3,2,1,0:T(8,128)(2,1)}, bf16[8,2,64,384]{3,2,1,0:T(8,128)(2,1)}, u32[]{:S(2)}, u32[]{:S(2)}) collective-permute-start(bf16[8,2,64,384]{3,2,1,0:T(8,128)(2,1)} %add_convert_fusion.2), channel_id=1, source_target_pairs={{0,8},{8,16},{16,24},{24,0},{32,40},{40,48},{48,56},{56,32},{1,9},... | collective-permute-start | bytes 2359304 | tf_op jit(solution)/shard_map/ppermute | solution.py:245
  178.6 9.4 %collective-permute-start.7 = (bf16[8,64,384]{2,1,0:T(8,128)(2,1)S(1)}, bf16[8,64,384]{2,1,0:T(8,128)(2,1)S(1)}, u32[]{:S(2)}, u32[]{:S(2)}) collective-permute-start(bf16[8,64,384]{2,1,0:T(8,128)(2,1)S(1)} %get-tuple-element.24), channel_id=1, source_target_pairs={{0,32},{8,40},{16,48},{24,56},{32,0},{40,8},{48,16},{56,24},{1,33}... | collective-permute-start | bytes 1179656 | tf_op jit(solution)/shard_map/ppermute | solution.py:245
  188.8 12.3 %all-to-all-start.2 = ((bf16[8,1,64,384]{3,2,1,0:T(8,128)(2,1)}), bf16[8,1,64,384]{3,2,1,0:T(8,128)(2,1)S(1)}, u32[]{:S(2)}, u32[]{:S(2)}) async-start(bf16[8,1,64,384]{3,2,1,0:T(8,128)(2,1)} %fusion.1), calls=%async_computation.2 | async-start | bytes 786432 | tf_op jit(solution)/shard_map/all_to_all | solution.py:263
  192.2 12.4 %collective-permute-start.12 = (bf16[512,384]{1,0:T(8,128)(2,1)}, bf16[512,384]{1,0:T(8,128)(2,1)}, u32[]{:S(2)}, u32[]{:S(2)}) collective-permute-start(bf16[512,384]{1,0:T(8,128)(2,1)} %copy-done.2), channel_id=1, source_target_pairs={{0,32},{8,40},{16,48},{24,56},{32,0},{40,8},{48,16},{56,24},{1,33}... | collective-permute-start | bytes 1179656 | tf_op jit(solution)/shard_map/ppermute | solution.py:245
  201.1 16.7 %all-to-all-start.3 = ((bf16[8,2,64,384]{3,2,1,0:T(8,128)(2,1)}), bf16[8,2,64,384]{3,2,1,0:T(8,128)(2,1)S(1)}, u32[]{:S(2)}, u32[]{:S(2)}) async-start(bf16[8,2,64,384]{3,2,1,0:T(8,128)(2,1)} %add_convert_fusion), calls=%async_computation.3 | async-start | bytes 1572864 | tf_op jit(solution)/shard_map/all_to_all | solution.py:263
  217.7 67.1 %all-to-all-start.4 = ((bf16[16,320,384]{2,1,0:T(8,128)(2,1)}), bf16[16,320,384]{2,1,0:T(8,128)(2,1)}, u32[]{:S(2)}, u32[]{:S(2)}) async-start(bf16[16,320,384]{2,1,0:T(8,128)(2,1)} %bitcast.55), calls=%async_computation.4 | async-start | bytes 7864320 | tf_op jit(solution)/shard_map/all_to_all | solution.py:301
Sparse Core Ops, SparseCore 0:
  10.1 64.0 all-gather.4
  76.0 35.7 all-gather.2

commit v2 on v1

v2 whole, which is shorter than its diff:
```python
import functools

import jax
import jax.numpy as jnp
from jax import lax
from jax.experimental import pallas as pl
from jax.experimental.pallas import tpu as pltpu
from jax.sharding import PartitionSpec as P

HD = 128
HEADS = 3
U = 8
T = 64
W = HEADS * HD
ROWS = U * T
SCALE = HD**-0.5
SCALE2 = SCALE * 1.4426950408889634
BF = jnp.bfloat16
F32 = jnp.float32
VMEM = 60 * 1024 * 1024


def nt(a, b):
    return lax.dot_general(a, b, (((1,), (1,)), ((), ())), preferred_element_type=F32)


def nn(a, b):
    return jnp.dot(a, b, preferred_element_type=F32)


def flat(ref):
    return ref[...].reshape(ROWS, HD)


def joined(low, high, i):
    return jnp.concatenate([low[:, i].reshape(ROWS // 2, HD), high[:, i].reshape(ROWS // 2, HD)], axis=0)


def forward_kernel(qa, qb, kv0, kv1, kv2, kv3a, kv3b, ot_ref, st_ref):
    queries = jnp.concatenate([flat(qa), flat(qb)], axis=0)
    keys = [r[:, 0].reshape(ROWS, HD) for r in (kv0, kv1, kv2)] + [joined(kv3a, kv3b, 0)]
    values = [r[:, 1].reshape(ROWS, HD) for r in (kv0, kv1, kv2)] + [joined(kv3a, kv3b, 1)]
    later = nt(keys[0], queries)
    top = total = acc = None
    for j in range(4):
        scores = later
        if j < 3:
            later = nt(keys[j + 1], queries)
        peak = jnp.max(scores, axis=0, keepdims=True) * SCALE2
        if j > 0:
            peak = jnp.maximum(peak, top)
        weights = jnp.exp2(scores * SCALE2 - peak)
        sums = jnp.sum(weights, axis=0, keepdims=True)
        out = nn(values[j].T, weights.astype(BF))
        if j > 0:
            fade = jnp.exp2(top - peak)
            sums = sums + total * fade
            out = out + acc * fade
        top, total, acc = peak, sums, out
    st_ref[0, 0:1] = top
    st_ref[0, 1:2] = total
    ot_ref[...] = acc


Q_SPEC = pl.BlockSpec((U, T, HD), lambda h: (0, 0, h))
KV_SPEC = pl.BlockSpec((U, 2, T, HD), lambda h: (0, 0, 0, h))
HALF_SPEC = pl.BlockSpec((U // 2, 2, T, HD), lambda h: (0, 0, 0, h))
OT_SPEC = pl.BlockSpec((HD, 2 * ROWS), lambda h: (h, 0))
ST_SPEC = pl.BlockSpec((1, 8, 2 * ROWS), lambda h: (h, 0, 0))
ROW_SPEC = pl.BlockSpec((ROWS, HD), lambda h: (0, h))
SMALL_VMEM = 24 * 1024 * 1024
PARAMS = pltpu.CompilerParams(vmem_limit_bytes=VMEM, dimension_semantics=("arbitrary",))
SMALL = pltpu.CompilerParams(vmem_limit_bytes=SMALL_VMEM, dimension_semantics=("arbitrary",))


def struct(shape, dtype):
    return jax.ShapeDtypeStruct(shape, dtype)


def cost(flops, nbytes):
    return pl.CostEstimate(flops=flops, bytes_accessed=nbytes, transcendentals=0)


def forward(qa, qb, kv0, kv1, kv2, kv3a, kv3b):
    return pl.pallas_call(
        forward_kernel,
        grid=(HEADS,),
        in_specs=[Q_SPEC, Q_SPEC, KV_SPEC, KV_SPEC, KV_SPEC, HALF_SPEC, HALF_SPEC],
        out_specs=[OT_SPEC, ST_SPEC],
        out_shape=[struct((W, 2 * ROWS), F32), struct((HEADS, 8, 2 * ROWS), F32)],
        compiler_params=PARAMS,
        cost_estimate=cost(2 * 2 * 1024 * 2048 * W, 6 << 20),
        name="attn_forward",
    )(qa, qb, kv0, kv1, kv2, kv3a, kv3b)


def merge_kernel(ot_ref, st_ref, pst_ref, keep_ref, send_ref, fin_ref):
    mine = st_ref[0]
    other = halves_swapped(pst_ref[0])
    top = jnp.maximum(mine[0:1], other[0:1])
    a = jnp.exp2(mine[0:1] - top)
    b = jnp.exp2(other[0:1] - top)
    total = a * mine[1:2] + b * other[1:2]
    factor = a / total
    fin_ref[0, 0:1] = top + jnp.log2(total)
    fin_ref[0, 1:2] = factor
    out_t = ot_ref[...] * factor
    keep_ref[...] = out_t[:, :ROWS].T
    send_ref[...] = out_t[:, ROWS:].T.astype(BF)


def halves_swapped(x):
    return jnp.concatenate([x[:, ROWS:], x[:, :ROWS]], axis=1)


def merge(ot, st, pst):
    return pl.pallas_call(
        merge_kernel,
        grid=(HEADS,),
        in_specs=[OT_SPEC, ST_SPEC, ST_SPEC],
        out_specs=[ROW_SPEC, ROW_SPEC, ST_SPEC],
        out_shape=[struct((ROWS, W), F32), struct((ROWS, W), BF), struct((HEADS, 8, 2 * ROWS), F32)],
        compiler_params=SMALL,
        cost_estimate=cost(1 << 20, 3 << 20),
        name="merge_halves",
    )(ot, st, pst)


def dot_kernel(ot_ref, fin_ref, da, db, out_ref):
    for part, d in enumerate((da, db)):
        at = slice(part * ROWS, (part + 1) * ROWS)
        grad_t = d[...].astype(F32).T
        sums = jnp.sum(grad_t * ot_ref[:, at], axis=0, keepdims=True)
        out_ref[0, 0:1, at] = sums * fin_ref[0, 1:2, at]


def row_dots(ot, fin, da, db):
    return pl.pallas_call(
        dot_kernel,
        grid=(HEADS,),
        in_specs=[OT_SPEC, ST_SPEC, ROW_SPEC, ROW_SPEC],
        out_specs=ST_SPEC,
        out_shape=struct((HEADS, 8, 2 * ROWS), F32),
        compiler_params=SMALL,
        cost_estimate=cost(1 << 20, 3 << 20),
        name="row_dots",
    )(ot, fin, da, db)


FEATURES = 5120
QUARTER = FEATURES // 4
SHARD = FEATURES // 16
ANY_SPEC = pl.BlockSpec(memory_space=pl.ANY)
SMEM_SPEC = pl.BlockSpec(memory_space=pltpu.SMEM)
VMEM_SPEC = pl.BlockSpec(memory_space=pltpu.VMEM)
PLAIN = pltpu.CompilerParams(vmem_limit_bytes=VMEM)
PIECES = 10


def token_rows(place, piece):
    offset = (0, 1, 3, 2, 2)[piece % 5]
    x = lax.rem(place[0] + offset, 4)
    core = place[1] if piece < 5 else 1 - place[1]
    first = (x * 2 + core) * T + (T // 2 if piece % 5 == 4 else 0)
    return pl.multiple_of(first, T // 2), (T if piece % 5 < 3 else T // 2)


def grad_copies(place, pieces, held, sems, columns):
    copies = []
    for i, piece in enumerate(pieces):
        first, rows = token_rows(place, i)
        copies.append(pltpu.make_async_copy(piece.at[:, columns], held.at[pl.ds(first, rows)], sems.at[i]))
    return copies


def stack_kernel(*refs):
    for i, piece in enumerate(refs[:4]):
        refs[4][i * SHARD : (i + 1) * SHARD] = piece[...]


def stacked_rows(*pieces):
    return pl.pallas_call(
        stack_kernel,
        in_specs=[VMEM_SPEC] * 4,
        out_specs=VMEM_SPEC,
        out_shape=struct((QUARTER, W), BF),
        compiler_params=pltpu.CompilerParams(vmem_limit_bytes=SMALL_VMEM),
        cost_estimate=cost(0, 2 << 20),
        name="stack_rows",
    )(*pieces)


def project_kernel(place, *refs):
    pieces, (w0, w1, w2a, w2b, w3), (out_ref, held, weight, sems) = refs[:PIECES], refs[PIECES : PIECES + 5], refs[PIECES + 5 :]
    groups = []
    for oz in range(4):
        quarter = lax.rem(place[2] + oz, 4)
        columns = pl.ds(pl.multiple_of(quarter * QUARTER, 128), QUARTER)
        copies = grad_copies(place, pieces, held.at[oz], sems.at[oz], columns)
        for oy in range(4):
            source, row = ((w0, oy), (w1, oy), (w2a, oy) if oy < 2 else (w2b, oy - 2), (w3, oy))[oz]
            at = pl.multiple_of(lax.rem(place[3] + oy, 4) * SHARD, SHARD)
            target = weight.at[oz, pl.ds(at, SHARD)]
            copies.append(pltpu.make_async_copy(source.at[pl.ds(row * SHARD, SHARD)], target, sems.at[oz, PIECES + oy]))
        for c in copies:
            c.start()
        groups.append(copies)
    total = None
    for oz in range(4):
        for c in groups[oz]:
            c.wait()
        part = nn(held[oz], weight[oz])
        total = part if total is None else total + part
    out_ref[...] = total.astype(BF)


def project(place, pieces, weights):
    return pl.pallas_call(
        project_kernel,
        in_specs=[SMEM_SPEC] + [ANY_SPEC] * (PIECES + 5),
        out_specs=VMEM_SPEC,
        out_shape=struct((ROWS, W), BF),
        scratch_shapes=[
            pltpu.VMEM((4, ROWS, QUARTER), BF),
            pltpu.VMEM((4, QUARTER, W), BF),
            pltpu.SemaphoreType.DMA((4, PIECES + 4)),
        ],
        compiler_params=PLAIN,
        cost_estimate=cost(2 * ROWS * FEATURES * W, 10 << 20),
        name="project",
    )(place, *pieces, *weights)


def tn(a, b):
    return lax.dot_general(a, b, (((0,), (0,)), ((), ())), preferred_element_type=F32)


def weight_part(place, oz, pieces, attn, held, sems):
    at = lax.rem(place[2] + oz, 4) * QUARTER
    copies = grad_copies(place, pieces, held, sems, pl.ds(pl.multiple_of(at, 128), QUARTER))
    for c in copies:
        c.start()
    for c in copies:
        c.wait()
    return tn(held[...], attn[...])


def weight_far_kernel(place, *refs):
    pieces, (attn, a_ref, b_ref, held, sems) = refs[:PIECES], refs[PIECES:]
    part = weight_part(place, 2, pieces, attn, held, sems).astype(BF)
    a_ref[...] = part[: QUARTER // 2]
    b_ref[...] = part[QUARTER // 2 :]


def weight_near_kernel(place, *refs):
    pieces, (attn, a_got, b_got, up_ref, down_ref, held, sems) = refs[:PIECES], refs[PIECES:]
    half = QUARTER // 2
    part = weight_part(place, 1, pieces, attn, held, sems)
    up_ref[:half] = (part[:half] + a_got[...].astype(F32)).astype(BF)
    up_ref[half:] = part[half:].astype(BF)
    part = weight_part(place, 3, pieces, attn, held, sems)
    down_ref[:half] = part[:half].astype(BF)
    down_ref[half:] = (part[half:] + b_got[...].astype(F32)).astype(BF)


def weight_own_kernel(place, *refs):
    pieces, (attn, below, above, o0, o1, o2, o3, held, sems, total) = refs[:PIECES], refs[PIECES:]
    part = weight_part(place, 0, pieces, attn, held, sems)
    total[...] = part + below[...].astype(F32) + above[...].astype(F32)
    for oy, o in enumerate((o0, o1, o2, o3)):
        at = pl.multiple_of(lax.rem(place[3] + oy, 4) * SHARD, SHARD)
        o[...] = total[pl.ds(at, SHARD)].astype(o.dtype)


def weight_call(kernel, name, parts, outs, extra, place, pieces, *more):
    return pl.pallas_call(
        kernel,
        in_specs=[SMEM_SPEC] + [ANY_SPEC] * PIECES + [VMEM_SPEC] * len(more),
        out_specs=[VMEM_SPEC] * len(outs),
        out_shape=outs,
        scratch_shapes=[pltpu.VMEM((ROWS, QUARTER), BF), pltpu.SemaphoreType.DMA((PIECES,))] + extra,
        compiler_params=PLAIN,
        cost_estimate=cost(parts * 2 * ROWS * QUARTER * W, parts * 3 << 20),
        name=name,
    )(place, *pieces, *more)


CHUNK = 256


def backward_block(keys, values, queries, grads, log_total, row_dot):
    scores = nt(keys, queries)
    probs = jnp.exp2(scores * SCALE2 - log_total)
    grad_probs = nt(values, grads)
    grad_scores = (probs * (grad_probs - row_dot)).astype(BF)
    grad_values = nn(probs.astype(BF), grads)
    grad_keys = nn(grad_scores, queries) * SCALE
    grad_queries_t = nn(keys.T, grad_scores)
    return grad_keys, grad_values, grad_queries_t


def backward_common(qa, qb, da, db, fin, dots, pdots):
    queries = jnp.concatenate([flat(qa), flat(qb)], axis=0)
    grads = jnp.concatenate([da[...], db[...]], axis=0)
    row_dot = dots[0, 0:1] + halves_swapped(pdots[0, 0:1])
    return queries, grads, fin[0, 0:1], row_dot


def chunks_of(x):
    return [x[i * CHUNK : (i + 1) * CHUNK] for i in range(ROWS // CHUNK)]


def run_block(keys, values, common):
    dks, dvs, dqt = [], [], None
    for k, v in zip(chunks_of(keys), chunks_of(values)):
        dk, dv, q = backward_block(k, v, *common)
        dks.append(dk)
        dvs.append(dv)
        dqt = q if dqt is None else dqt + q
    return jnp.concatenate(dks, axis=0), jnp.concatenate(dvs, axis=0), dqt


def store_halves(low, high, i, x):
    low[:, i] = x[: ROWS // 2].astype(low.dtype).reshape(U // 2, T, HD)
    high[:, i] = x[ROWS // 2 :].astype(high.dtype).reshape(U // 2, T, HD)


def far_kernel(qa, qb, da, db, fin, dots, pdots, kv3a, kv3b, low_ref, high_ref, dqt_ref):
    common = backward_common(qa, qb, da, db, fin, dots, pdots)
    dk, dv, dqt = run_block(joined(kv3a, kv3b, 0), joined(kv3a, kv3b, 1), common)
    store_halves(low_ref, high_ref, 0, dk)
    store_halves(low_ref, high_ref, 1, dv)
    dqt_ref[...] = dqt


def near_kernel(qa, qb, da, db, fin, dots, pdots, kv1, kv2, dqt_in, l1_ref, h1_ref, l2_ref, h2_ref, dqt_ref):
    common = backward_common(qa, qb, da, db, fin, dots, pdots)
    total = dqt_in[...]
    for kv, low, high in ((kv1, l1_ref, h1_ref), (kv2, l2_ref, h2_ref)):
        dk, dv, dqt = run_block(kv[:, 0].reshape(ROWS, HD), kv[:, 1].reshape(ROWS, HD), common)
        store_halves(low, high, 0, dk)
        store_halves(low, high, 1, dv)
        total = total + dqt
    dqt_ref[...] = total


def own_kernel(qa, qb, da, db, fin, dots, pdots, kv0, dqt_in, o0_ref, qkeep_ref, qsend_ref):
    common = backward_common(qa, qb, da, db, fin, dots, pdots)
    dk, dv, dqt = run_block(kv0[:, 0].reshape(ROWS, HD), kv0[:, 1].reshape(ROWS, HD), common)
    o0_ref[:, 0] = dk.reshape(U, T, HD)
    o0_ref[:, 1] = dv.reshape(U, T, HD)
    total = (dqt_in[...] + dqt) * SCALE
    qkeep_ref[...] = total[:, :ROWS].T.reshape(U, T, HD)
    qsend_ref[...] = total[:, ROWS:].T.astype(BF).reshape(U, T, HD)


COMMON_SPECS = [Q_SPEC, Q_SPEC, ROW_SPEC, ROW_SPEC, ST_SPEC, ST_SPEC, ST_SPEC]


def backward_far(common, kv3a, kv3b):
    return pl.pallas_call(
        far_kernel,
        grid=(HEADS,),
        in_specs=COMMON_SPECS + [HALF_SPEC, HALF_SPEC],
        out_specs=[HALF_SPEC, HALF_SPEC, OT_SPEC],
        out_shape=[struct((U // 2, 2, T, W), BF)] * 2 + [struct((W, 2 * ROWS), F32)],
        compiler_params=PARAMS,
        cost_estimate=cost(5 * 2 * 1024 * 512 * W, 6 << 20),
        name="backward_far",
    )(*common, kv3a, kv3b)


def backward_near(common, kv1, kv2, dqt):
    return pl.pallas_call(
        near_kernel,
        grid=(HEADS,),
        in_specs=COMMON_SPECS + [KV_SPEC, KV_SPEC, OT_SPEC],
        out_specs=[HALF_SPEC] * 4 + [OT_SPEC],
        out_shape=[struct((U // 2, 2, T, W), t) for t in (BF, F32, F32, BF)] + [struct((W, 2 * ROWS), F32)],
        compiler_params=PARAMS,
        cost_estimate=cost(5 * 2 * 1024 * 1024 * W, 9 << 20),
        name="backward_near",
    )(*common, kv1, kv2, dqt)


def backward_own(common, kv0, dqt):
    return pl.pallas_call(
        own_kernel,
        grid=(HEADS,),
        in_specs=COMMON_SPECS + [KV_SPEC, OT_SPEC],
        out_specs=[KV_SPEC, Q_SPEC, Q_SPEC],
        out_shape=[struct((U, 2, T, W), F32), struct((U, T, W), F32), struct((U, T, W), BF)],
        compiler_params=PARAMS,
        cost_estimate=cost(5 * 2 * 1024 * 512 * W, 8 << 20),
        name="backward_own",
    )(*common, kv0, dqt)


def move(x, axis, to, n):
    return lax.ppermute(x, axis, [(i, to(i)) for i in range(n)])


def y_shift(x, d):
    return move(x, "blk", lambda i: i // 4 * 4 + (i + d) % 4, 8)


def z_shift(x, d):
    return move(x, ("dp", "blk"), lambda i: (i // 4 + d) % 4 * 4 + i % 4, 16)


def x_shift(x, d):
    return move(x, "uly", lambda i: (i // 2 + d) % 4 * 2 + i % 2, 8)


def core_swap(x):
    return move(x, "uly", lambda i: i ^ 1, 8)


def z_swap(x):
    return move(x, "blk", lambda i: (i + 4) % 8, 8)


def by_head(*rows):
    stacked = jnp.concatenate([r.reshape(T, U, 1, W) for r in rows], axis=2)
    return jnp.transpose(stacked, (1, 2, 0, 3))


def exchange(x):
    return lax.all_to_all(x, "uly", split_axis=0, concat_axis=0, tiled=True)


def to_tokens(x):
    got = exchange(x)
    return [jnp.transpose(got[:, i], (1, 0, 2)).reshape(T, U * W) for i in range(x.shape[1])]


def after(x, *others):
    return lax.optimization_barrier((x, *others))[0]


def per_device(query_rows, key_rows, value_rows, out_grad, out_weight):
    uly, blk = lax.axis_index("uly"), lax.axis_index("blk")
    place = jnp.stack([uly // 2, uly % 2, lax.axis_index("dp") * 2 + blk // 4, blk % 4]).astype(jnp.int32)
    leaving = by_head(key_rows, value_rows, query_rows)
    shards = (out_weight, y_shift(out_weight, -1), y_shift(out_weight, 2), y_shift(out_weight, 1))
    grad_below, grad_above = x_shift(out_grad, 1), x_shift(out_grad, -1)
    heads = exchange(leaving)
    weight_own = stacked_rows(*after(shards, heads))
    kv0, qa = heads[:, :2], heads[:, 2]
    kv_prev, kv_next = y_shift(kv0, 1), y_shift(kv0, -1)
    qb = z_swap(qa)
    weight_below, weight_above = z_shift(weight_own, 1), z_shift(weight_own, -1)
    near_parts = (kv_prev[: U // 2], kv_next[U // 2 :])
    grad_parts = (grad_above[: T // 2], grad_below[T // 2 :])
    cut = QUARTER // 2
    weight_parts = (weight_above[:cut], weight_below[cut:])
    far_low, far_high = y_shift(near_parts[0], 1), y_shift(near_parts[1], -1)
    grad_far = [x_shift(grad_parts[0], -1), x_shift(grad_parts[1], 1)]
    weight_far = [z_shift(weight_parts[0], -1), z_shift(weight_parts[1], 1)]
    weights = (weight_own, weight_above, *weight_far, weight_below)
    mine = [out_grad, grad_above, grad_below] + grad_far
    pieces = mine + [core_swap(p) for p in mine]
    da = project(place, pieces, weights)
    db = z_swap(da)
    ot, st = forward(after(qa, da), qb, kv0, kv_prev, kv_next, far_low, far_high)
    pst = z_swap(st)
    o_keep, o_send, fin = merge(ot, st, pst)
    dots = row_dots(ot, fin, da, db)
    attn_out = (o_keep + z_swap(o_send).astype(F32)).astype(BF)
    common = (qa, qb, da, db, fin, dots, z_swap(dots))

    low, high, dqt = backward_far(common, far_low, far_high)
    low_got, high_got = y_shift(low, 1), y_shift(high, -1)
    half = struct((QUARTER // 2, W), BF)
    a, b = weight_call(weight_far_kernel, "weight_far", 1, [half, half], [], place, pieces, after(attn_out, dqt))
    a_got, b_got = z_shift(a, 1), z_shift(b, -1)
    prev_low, prev_high, next_low, next_high, dqt = backward_near(common, kv_prev, kv_next, after(dqt, a, b))
    high_below = y_shift(next_high, 1)
    low_above = y_shift(prev_low, -1)
    low_below = y_shift((next_low + low_got.astype(F32)).astype(BF), 1)
    high_above = y_shift((prev_high + high_got.astype(F32)).astype(BF), -1)
    g_own, q_keep, q_send = backward_own(common, kv0, dqt)
    whole = struct((QUARTER, W), BF)
    up, down = weight_call(
        weight_near_kernel, "weight_near", 2, [whole, whole], [], place, pieces, after(attn_out, q_send), a_got, b_got
    )
    below, above = z_shift(up, 1), z_shift(down, -1)
    dq = (q_keep + z_swap(q_send).astype(F32)).astype(BF)
    g_low = g_own[: U // 2] + low_below.astype(F32) + low_above.astype(F32)
    g_high = g_own[U // 2 :] + high_below.astype(F32) + high_above.astype(F32)
    dkv = jnp.concatenate([g_low.astype(BF), g_high.astype(BF)], axis=0)
    grads = jnp.concatenate([dkv, dq[:, None]], axis=1)
    grad_key, grad_value, grad_query = to_tokens(grads)
    o0, o1, o2, o3 = weight_call(
        weight_own_kernel,
        "weight_own",
        1,
        [struct((SHARD, W), F32)] + [struct((SHARD, W), BF)] * 3,
        [pltpu.VMEM((QUARTER, W), F32)],
        place,
        pieces,
        after(attn_out, grads),
        below,
        above,
    )
    grad_weight = o0 + y_shift(o1, 1).astype(F32) + y_shift(o2, 2).astype(F32) + y_shift(o3, -1).astype(F32)
    return (grad_query, grad_key, grad_value, grad_weight)


def solution(mesh):
    rows = P(("dp", "blk", "uly"), None)
    weight = P(("dp", "blk"), "uly")
    return jax.shard_map(
        per_device,
        mesh=mesh,
        in_specs=(rows, rows, rows, rows, weight),
        out_specs=(rows, rows, rows, weight),
        check_vma=False,
    )
```

time: 296 us -> 220 us (0.74)
  waiting for transfers between devices: 140 us -> 70.7 us
  starting transfers between devices: 31.6 us -> 60.8 us
  blocking collectives: 28.8 us -> 0 us
  Pallas kernels: 40.6 us -> 59.6 us
  matrix products: 13.4 us -> 0 us
  between operations: 14.3 us -> 1.15 us
    all_to_all x3 -> x2, waiting for transfers between devices: 63.7 us -> 1.08 us  [exchange(): return lax.all_to_all(x, 'uly', split_axis=0, concat_axis=0, tiled=True)]
    all_gather x2 -> x0, waiting for transfers between devices: 51.3 us -> none  [the longest x1 37.5 us: per_device(): grad_block = lax.all_gather(out_grad, 'uly', axis=0, tiled=True)]
    ppermute x13 -> x39, waiting for transfers between devices: 23.4 us -> 69.6 us  [move(): return lax.ppermute(x, axis, [(i, to(i)) for i in range(n)])]
    ppermute x13 -> x39, starting transfers between devices: 17.9 us -> 52.7 us  [move(): return lax.ppermute(x, axis, [(i, to(i)) for i in range(n)])]
    all_to_all x2 -> x0, blocking collectives: 28.8 us -> none  [to_heads(): lax.all_to_all(jnp.transpose(stacked, (1, 2, 0, 3)), 'uly', split_axis=0,...]
    pallas_call x1 -> x6, Pallas kernels: 5.55 us -> 29.8 us  [the longest x3 15.9 us: weight_call(): pl.pallas_call(kernel, in_specs=[SMEM_SPEC] + [ANY_SPEC] * PIECES + [VMEM...]
    dot_general x2 -> x0, matrix products: 13.4 us -> none  [the longest x1 6.83 us: per_device(): lax.dot_general(grad_block, attn_out, (((0,), (0,)), ((), ())), preferred...]
    convert_element_type x1 -> x0, local copies, waits for them, and re-layouts: 6.27 us -> none  [per_device(): partial.astype(BF)]
  transfers between devices with their start and end apart: 18 -> 41, of which waited for: 7 -> 16; matrix products, arithmetic and copies ran while one was open for 11% -> 6% of each run, Pallas kernels for 11% -> 25%
where the time goes in v2:
time: 220 us; the launch traced here: 219 us
  waiting for transfers between devices  70.7 us (32%)
  starting transfers between devices  60.8 us (28%)
  Pallas kernels  59.6 us (27%)
  local copies, waits for them, and re-layouts  17.5 us (8%)
  other arithmetic  9.18 us (4%)
    ppermute x39, waiting for transfers between devices, move(): return lax.ppermute(x, axis, [(i, to(i)) for i in range(n)])  69.6 us
    ppermute x39, starting transfers between devices, move(): return lax.ppermute(x, axis, [(i, to(i)) for i in range(n)])  52.7 us
    pallas_call x3, Pallas kernels, weight_call(): pl.pallas_call(kernel, in_specs=[SMEM_SPEC] + [ANY_SPEC] * PIECES + [VMEM...  15.9 us
    pallas_call x1, Pallas kernels, forward(): pl.pallas_call(forward_kernel, grid=(HEADS,), in_specs=[Q_SPEC, Q_SPEC, K...  11.1 us
    pallas_call x1, Pallas kernels, backward_near(): pl.pallas_call(near_kernel, grid=(HEADS,), in_specs=COMMON_SPECS + [KV_SP...  10.5 us
    unnamed x82, local copies, waits for them, and re-layouts  8.63 us
    all_to_all x2, starting transfers between devices, exchange(): return lax.all_to_all(x, 'uly', split_axis=0, concat_axis=0, tiled=True)  8.08 us
    pallas_call x1, Pallas kernels, project(): pl.pallas_call(project_kernel, in_specs=[SMEM_SPEC] + [ANY_SPEC] * (PIECE...  7.31 us
  transfers between devices with their start and end apart: 41, of which 16 were waited for; matrix products, arithmetic and copies ran while one was open for 6% of the time, Pallas kernels for 25%

profile of v2, /device:TPU:0, one launch (start us, length us, event | category | flops | bytes accessed | tf_op | source)
XLA Modules:
  0.0 218.9 jit_solution(6106537040480683371)
XLA Ops:
  4.1 4.5 %all-to-all-start = ((bf16[8,3,64,384]{3,2,1,0:T(8,128)(2,1)}), bf16[8,3,64,384]{3,2,1,0:T(8,128)(2,1)}, u32[]{:S(2)}, u32[]{:S(2)}) async-start(bf16[8,3,64,384]{3,2,1,0:T(8,128)(2,1)} %maximum_bitcast_fusion), calls=%async_computation | async-start | bytes 2359296 | tf_op jit(solution)/shard_map/all_to_all | solution.py:429
  8.6 2.0 collective-permute-start.2
  10.6 3.2 %collective-permute-start.11 = (bf16[320,384]{1,0:T(8,128)(2,1)S(1)}, bf16[320,384]{1,0:T(8,128)(2,1)S(1)}, u32[]{:S(2)}, u32[]{:S(2)}) collective-permute-start(bf16[320,384]{1,0:T(8,128)(2,1)S(1)} %copy-done.5), channel_id=1, source_target_pairs={{0,16},{8,24},{16,0},{24,8},{32,48},{40,56},{48,32},{56,40},{1,17}... | collective-permute-start | bytes 737288 | tf_op jit(solution)/shard_map/ppermute | solution.py:400
  17.1 3.8 %collective-permute-done.11.refs_2_ = bf16[320,384]{1,0:T(8,128)(2,1)S(1)} collective-permute-done((bf16[320,384]{1,0:T(8,128)(2,1)S(1)}, bf16[320,384]{1,0:T(8,128)(2,1)S(1)}, u32[]{:S(2)}, u32[]{:S(2)}) %collective-permute-start.11) | collective-permute-done | bytes 245792 | tf_op jit(solution)/shard_map/ppermute | solution.py:400
  20.9 4.5 %collective-permute-done.10.refs_1_ = bf16[320,384]{1,0:T(8,128)(2,1)S(1)} collective-permute-done((bf16[320,384]{1,0:T(8,128)(2,1)S(1)}, bf16[320,384]{1,0:T(8,128)(2,1)S(1)}, u32[]{:S(2)}, u32[]{:S(2)}) %collective-permute-start.10) | collective-permute-done | bytes 245792 | tf_op jit(solution)/shard_map/ppermute | solution.py:400
  26.7 2.0 collective-permute-start.15
  28.6 11.0 %collective-permute-done.2.refs_2_ = bf16[64,5120]{1,0:T(8,128)(2,1)S(1)} collective-permute-done((bf16[64,5120]{1,0:T(8,128)(2,1)S(1)}, bf16[64,5120]{1,0:T(8,128)(2,1)S(1)}, u32[]{:S(2)}, u32[]{:S(2)}) %collective-permute-start.2) | collective-permute-done | bytes 655392 | tf_op jit(solution)/shard_map/ppermute | solution.py:400
  39.9 3.3 %collective-permute-start.3 = (bf16[32,5120]{1,0:T(8,128)(2,1)S(1)}, bf16[32,5120]{1,0:T(8,128)(2,1)S(1)}, u32[]{:S(2)}, u32[]{:S(2)}) collective-permute-start(bf16[32,5120]{1,0:T(8,128)(2,1)S(1)} %slice.53), channel_id=1, source_target_pairs={{0,6},{1,7},{2,0},{3,1},{4,2},{5,3},{6,4},{7,5},{8,14},{9,15},{10,... | collective-permute-start | bytes 983048 | tf_op jit(solution)/shard_map/ppermute | solution.py:400
  43.1 4.0 %collective-permute-start.13 = (bf16[1280,384]{1,0:T(8,128)(2,1)S(1)}, bf16[1280,384]{1,0:T(8,128)(2,1)S(1)}, u32[]{:S(2)}, u32[]{:S(2)}) collective-permute-start(bf16[1280,384]{1,0:T(8,128)(2,1)S(1)} %stack_rows.1.refs_10_), channel_id=1, source_target_pairs={{0,96},{8,104},{16,112},{24,120},{32,0},{40,8},{48,16},{56,24},{64... | collective-permute-start | bytes 2949128 | tf_op jit(solution)/shard_map/ppermute | solution.py:400
  48.4 3.1 %collective-permute-start.19 = (bf16[8,2,64,384]{3,2,1,0:T(8,128)(2,1)S(1)}, bf16[8,2,64,384]{3,2,1,0:T(8,128)(2,1)S(1)}, u32[]{:S(2)}, u32[]{:S(2)}) collective-permute-start(bf16[8,2,64,384]{3,2,1,0:T(8,128)(2,1)S(1)} %slice.57.kv0), channel_id=1, source_target_pairs={{0,24},{8,0},{16,8},{24,16},{32,56},{40,32},{48,40},{56,48},{1,25}... | collective-permute-start | bytes 2359304 | tf_op jit(solution)/shard_map/ppermute | solution.py:400
  54.1 13.4 %collective-permute-done.13.refs_11_ = bf16[1280,384]{1,0:T(8,128)(2,1)S(1)} collective-permute-done((bf16[1280,384]{1,0:T(8,128)(2,1)S(1)}, bf16[1280,384]{1,0:T(8,128)(2,1)S(1)}, u32[]{:S(2)}, u32[]{:S(2)}) %collective-permute-start.13) | collective-permute-done | bytes 983072 | tf_op jit(solution)/shard_map/ppermute | solution.py:400
  70.8 3.2 %collective-permute-start.14 = (bf16[640,384]{1,0:T(8,128)(2,1)}, bf16[640,384]{1,0:T(8,128)(2,1)}, u32[]{:S(2)}, u32[]{:S(2)}) collective-permute-start(bf16[640,384]{1,0:T(8,128)(2,1)} %slice.55), channel_id=1, source_target_pairs={{0,96},{8,104},{16,112},{24,120},{32,0},{40,8},{48,16},{56,24},{64... | collective-permute-start | bytes 1474568 | tf_op jit(solution)/shard_map/ppermute | solution.py:400
  77.6 2.1 collective-permute-start.21
  80.5 4.7 %collective-permute-done.16.refs_13_ = bf16[640,384]{1,0:T(8,128)(2,1)} collective-permute-done((bf16[640,384]{1,0:T(8,128)(2,1)}, bf16[640,384]{1,0:T(8,128)(2,1)}, u32[]{:S(2)}, u32[]{:S(2)}) %collective-permute-start.16) | collective-permute-done | bytes 491552 | tf_op jit(solution)/shard_map/ppermute | solution.py:400
  85.3 7.3 %project.1.da = bf16[512,384]{1,0:T(8,128)(2,1)} custom-call(s32[4]{0:T(128)} %pad_add_fusion.place, bf16[64,5120]{1,0:T(8,128)(2,1)} %refs_0_.8, bf16[64,5120]{1,0:T(8,128)(2,1)} %copy-done.10, bf16[64,5120]{1,0:T(8,128)(2,1)} %copy-done.9, bf16[32,5120]{1,0:T(8,128)(2,1)} %copy-done.15, bf16[32,5120]{1,0:T(8,128)(2,1)} %copy-done.14, ...), custom_call_target="tpu_custom_call" | custom-call | flops 2013265920 | bytes 10485760 | tf_op jit(solution)/shard_map/project/pallas_call | solution.py:218
  95.6 11.1 %attn_forward.1 = (f32[384,1024]{1,0:T(8,128)}, f32[3,8,1024]{2,1,0:T(8,128)}) custom-call(bf16[8,64,384]{2,1,0:T(8,128)(2,1)} %slice_bitcast_fusion.3.qa, bf16[8,64,384]{2,1,0:T(8,128)(2,1)} %copy-done.33, bf16[8,2,64,384]{3,2,1,0:T(8,128)(2,1)} %copy-done.23, bf16[8,2,64,384]{3,2,1,0:T(8,128)(2,1)} %copy-done.32, bf16[8,2,64,384]{3,2,1,0:T(8,128)(2,1)} %copy-done.31, ...), custom_call_target="tpu_custom_call" | custom-call | flops 3221225472 | bytes 6291456 | tf_op jit(solution)/shard_map/attn_forward/pallas_call | solution.py:85
  107.6 3.9 %collective-permute-done.22.pst_ref = f32[3,8,1024]{2,1,0:T(8,128)S(1)} collective-permute-done((f32[3,8,1024]{2,1,0:T(8,128)}, f32[3,8,1024]{2,1,0:T(8,128)S(1)}, u32[]{:S(2)}, u32[]{:S(2)}) %collective-permute-start.22) | collective-permute-done | bytes 98336 | tf_op jit(solution)/shard_map/ppermute | solution.py:400
  117.4 8.5 %collective-permute-done.23.pdots = f32[3,8,1024]{2,1,0:T(8,128)S(1)} collective-permute-done((f32[3,8,1024]{2,1,0:T(8,128)S(1)}, f32[3,8,1024]{2,1,0:T(8,128)S(1)}, u32[]{:S(2)}, u32[]{:S(2)}) %collective-permute-start.23) | collective-permute-done | bytes 98336 | tf_op jit(solution)/shard_map/ppermute | solution.py:400
  126.5 6.4 %backward_far.1 = (bf16[4,2,64,384]{3,2,1,0:T(8,128)(2,1)}, bf16[4,2,64,384]{3,2,1,0:T(8,128)(2,1)}, f32[384,1024]{1,0:T(8,128)}) custom-call(bf16[8,64,384]{2,1,0:T(8,128)(2,1)} %slice_bitcast_fusion.3.qa, bf16[8,64,384]{2,1,0:T(8,128)(2,1)} %copy-done.33, bf16[512,384]{1,0:T(8,128)(2,1)} %project.1.da, bf16[512,384]{1,0:T(8,128)(2,1)} %copy-done.4, ...), custom_call_target="tpu_custom_call" | custom-call | flops 2013265920 | bytes 6291456 | tf_op jit(solution)/shard_map/backward_far/pallas_call | solution.py:361
  133.8 4.2 %weight_far.1 = (bf16[640,384]{1,0:T(8,128)(2,1)}, bf16[640,384]{1,0:T(8,128)(2,1)}) custom-call(s32[4]{0:T(128)} %pad_add_fusion.place, bf16[64,5120]{1,0:T(8,128)(2,1)} %refs_0_.8, bf16[64,5120]{1,0:T(8,128)(2,1)} %copy-done.10, bf16[64,5120]{1,0:T(8,128)(2,1)} %copy-done.9, bf16[32,5120]{1,0:T(8,128)(2,1)} %copy-done.15, bf16[32,5120]{1,0:T(8,128)(2,1)} %copy-done.14, ...), custom_call_target="tpu_custom_call" | custom-call | flops 503316480 | bytes 3145728 | tf_op jit(solution)/shard_map/weight_far/pallas_call | solution.py:276
  139.2 2.1 collective-permute-start.33
  144.6 10.5 %backward_near.1 = (bf16[4,2,64,384]{3,2,1,0:T(8,128)(2,1)}, f32[4,2,64,384]{3,2,1,0:T(8,128)}, f32[4,2,64,384]{3,2,1,0:T(8,128)}, bf16[4,2,64,384]{3,2,1,0:T(8,128)(2,1)}, f32[384,1024]{1,0:T(8,128)}) custom-call(bf16[8,64,384]{2,1,0:T(8,128)(2,1)} %slice_bitcast_fusion.3.qa, bf16[8,64,384]{2,1,0:T(8,128)(2,1)} %copy-done.33, bf16[512,384]{1,0:T(8,128)(2,1)} %project.1.da, ...), custom_call_target="tpu_custom_call" | custom-call | flops 4026531840 | bytes 9437184 | tf_op jit(solution)/shard_map/backward_near/pallas_call | solution.py:374
  155.1 6.9 %backward_own.1 = (f32[8,2,64,384]{3,2,1,0:T(8,128)}, f32[8,64,384]{2,1,0:T(8,128)}, bf16[8,64,384]{2,1,0:T(8,128)(2,1)}) custom-call(bf16[8,64,384]{2,1,0:T(8,128)(2,1)} %slice_bitcast_fusion.3.qa, bf16[8,64,384]{2,1,0:T(8,128)(2,1)} %copy-done.33, bf16[512,384]{1,0:T(8,128)(2,1)} %project.1.da, bf16[512,384]{1,0:T(8,128)(2,1)} %copy-done.4, ...), custom_call_target="tpu_custom_call" | custom-call | flops 2013265920 | bytes 8388608 | tf_op jit(solution)/shard_map/backward_own/pallas_call | solution.py:387
  166.5 2.8 %collective-permute-start.30 = (bf16[4,2,64,384]{3,2,1,0:T(8,128)(2,1)}, bf16[4,2,64,384]{3,2,1,0:T(8,128)(2,1)}, u32[]{:S(2)}, u32[]{:S(2)}) collective-permute-start(bf16[4,2,64,384]{3,2,1,0:T(8,128)(2,1)} %add_convert_fusion.2), channel_id=1, source_target_pairs={{0,24},{8,0},{16,8},{24,16},{32,56},{40,32},{48,40},{56,48},{1,25}... | collective-permute-start | bytes 1179656 | tf_op jit(solution)/shard_map/ppermute | solution.py:400
  169.4 6.6 %weight_near.1 = (bf16[1280,384]{1,0:T(8,128)(2,1)}, bf16[1280,384]{1,0:T(8,128)(2,1)}) custom-call(s32[4]{0:T(128)} %pad_add_fusion.place, bf16[64,5120]{1,0:T(8,128)(2,1)} %refs_0_.8, bf16[64,5120]{1,0:T(8,128)(2,1)} %copy-done.10, bf16[64,5120]{1,0:T(8,128)(2,1)} %copy-done.9, bf16[32,5120]{1,0:T(8,128)(2,1)} %copy-done.15, bf16[32,5120]{1,0:T(8,128)(2,1)} %copy-done.14, ...), custom_call_target="tpu_custom_call" | custom-call | flops 1006632960 | bytes 6291456 | tf_op jit(solution)/shard_map/weight_near/pallas_call | solution.py:276
  176.0 2.0 collective-permute-start.34
  179.4 2.5 %collective-permute-done.26 = bf16[4,2,64,384]{3,2,1,0:T(8,128)(2,1)} collective-permute-done((bf16[4,2,64,384]{3,2,1,0:T(8,128)(2,1)}, bf16[4,2,64,384]{3,2,1,0:T(8,128)(2,1)}, u32[]{:S(2)}, u32[]{:S(2)}) %collective-permute-start.26) | collective-permute-done | bytes 393248 | tf_op jit(solution)/shard_map/ppermute | solution.py:400
  184.8 3.6 %all-to-all-start.1 = ((bf16[8,3,64,384]{3,2,1,0:T(8,128)(2,1)}), bf16[8,3,64,384]{3,2,1,0:T(8,128)(2,1)S(1)}, u32[]{:S(2)}, u32[]{:S(2)}) async-start(bf16[8,3,64,384]{3,2,1,0:T(8,128)(2,1)} %pad_maximum_fusion), calls=%async_computation.1 | async-start | bytes 2359296 | tf_op jit(solution)/shard_map/all_to_all | solution.py:429
  188.3 7.9 %collective-permute-done.34.refs_11_ = bf16[1280,384]{1,0:T(8,128)(2,1)S(1)} collective-permute-done((bf16[1280,384]{1,0:T(8,128)(2,1)}, bf16[1280,384]{1,0:T(8,128)(2,1)S(1)}, u32[]{:S(2)}, u32[]{:S(2)}) %collective-permute-start.34) | collective-permute-done | bytes 983072 | tf_op jit(solution)/shard_map/ppermute | solution.py:400
  198.2 5.2 %weight_own.1 = (f32[320,384]{1,0:T(8,128)}, bf16[320,384]{1,0:T(8,128)(2,1)}, bf16[320,384]{1,0:T(8,128)(2,1)}, bf16[320,384]{1,0:T(8,128)(2,1)}) custom-call(s32[4]{0:T(128)} %pad_add_fusion.place, bf16[64,5120]{1,0:T(8,128)(2,1)} %refs_0_.8, bf16[64,5120]{1,0:T(8,128)(2,1)} %copy-done.10, bf16[64,5120]{1,0:T(8,128)(2,1)} %copy-done.9, ...), custom_call_target="tpu_custom_call" | custom-call | flops 503316480 | bytes 3145728 | tf_op jit(solution)/shard_map/weight_own/pallas_call | solution.py:276
  203.4 3.1 %collective-permute-start.37 = (bf16[320,384]{1,0:T(8,128)(2,1)}, bf16[320,384]{1,0:T(8,128)(2,1)S(1)}, u32[]{:S(2)}, u32[]{:S(2)}) collective-permute-start(bf16[320,384]{1,0:T(8,128)(2,1)} %get-tuple-element.68), channel_id=1, source_target_pairs={{0,16},{8,24},{16,0},{24,8},{32,48},{40,56},{48,32},{56,40},{1,17}... | collective-permute-start | bytes 737288 | tf_op jit(solution)/shard_map/ppermute | solution.py:400
  208.2 5.5 %collective-permute-done.36 = bf16[320,384]{1,0:T(8,128)(2,1)S(1)} collective-permute-done((bf16[320,384]{1,0:T(8,128)(2,1)}, bf16[320,384]{1,0:T(8,128)(2,1)S(1)}, u32[]{:S(2)}, u32[]{:S(2)}) %collective-permute-start.36) | collective-permute-done | bytes 245792 | tf_op jit(solution)/shard_map/ppermute | solution.py:400
  (166 shorter events, 52.7 us)
Async XLA Ops:
  4.1 22.5 %all-to-all-start = ((bf16[8,3,64,384]{3,2,1,0:T(8,128)(2,1)}), bf16[8,3,64,384]{3,2,1,0:T(8,128)(2,1)}, u32[]{:S(2)}, u32[]{:S(2)}) async-start(bf16[8,3,64,384]{3,2,1,0:T(8,128)(2,1)} %maximum_bitcast_fusion), calls=%async_computation | async-start | bytes 2359296 | tf_op jit(solution)/shard_map/all_to_all | solution.py:429
  8.6 31.1 %collective-permute-start.2 = (bf16[64,5120]{1,0:T(8,128)(2,1)S(1)}, bf16[64,5120]{1,0:T(8,128)(2,1)S(1)}, u32[]{:S(2)}, u32[]{:S(2)}) collective-permute-start(bf16[64,5120]{1,0:T(8,128)(2,1)S(1)} %copy-done.11), channel_id=1, source_target_pairs={{0,2},{1,3},{2,4},{3,5},{4,6},{5,7},{6,0},{7,1},{8,10},{9,11},{10,... | collective-permute-start | bytes 1966088 | tf_op jit(solution)/shard_map/ppermute | solution.py:400
  13.8 26.0 %collective-permute-start.1 = (bf16[64,5120]{1,0:T(8,128)(2,1)S(1)}, bf16[64,5120]{1,0:T(8,128)(2,1)S(1)}, u32[]{:S(2)}, u32[]{:S(2)}) collective-permute-start(bf16[64,5120]{1,0:T(8,128)(2,1)S(1)} %copy-done.11), channel_id=1, source_target_pairs={{0,6},{1,7},{2,0},{3,1},{4,2},{5,3},{6,4},{7,5},{8,14},{9,15},{10,... | collective-permute-start | bytes 1966088 | tf_op jit(solution)/shard_map/ppermute | solution.py:400
  15.1 10.4 %collective-permute-start.10 = (bf16[320,384]{1,0:T(8,128)(2,1)S(1)}, bf16[320,384]{1,0:T(8,128)(2,1)S(1)}, u32[]{:S(2)}, u32[]{:S(2)}) collective-permute-start(bf16[320,384]{1,0:T(8,128)(2,1)S(1)} %copy-done.5), channel_id=1, source_target_pairs={{0,24},{8,0},{16,8},{24,16},{32,56},{40,32},{48,40},{56,48},{1,25}... | collective-permute-start | bytes 737288 | tf_op jit(solution)/shard_map/ppermute | solution.py:400
  20.9 27.5 %collective-permute-start.5 = (bf16[64,5120]{1,0:T(8,128)(2,1)S(1)}, bf16[64,5120]{1,0:T(8,128)(2,1)}, u32[]{:S(2)}, u32[]{:S(2)}) collective-permute-start(bf16[64,5120]{1,0:T(8,128)(2,1)S(1)} %copy-done.11), channel_id=1, source_target_pairs={{0,1},{1,0},{2,3},{3,2},{4,5},{5,4},{6,7},{7,6},{8,9},{9,8},{10,11... | collective-permute-start | bytes 1966088 | tf_op jit(solution)/shard_map/ppermute | solution.py:400
  26.7 27.1 %collective-permute-start.15 = (bf16[1280,384]{1,0:T(8,128)(2,1)S(1)}, bf16[1280,384]{1,0:T(8,128)(2,1)S(1)}, u32[]{:S(2)}, u32[]{:S(2)}) collective-permute-start(bf16[1280,384]{1,0:T(8,128)(2,1)S(1)} %stack_rows.1.refs_10_), channel_id=1, source_target_pairs={{0,32},{8,40},{16,48},{24,56},{32,64},{40,72},{48,80},{56,88},{64,... | collective-permute-start | bytes 2949128 | tf_op jit(solution)/shard_map/ppermute | solution.py:400
  39.7 11.8 %collective-permute-start.4 = (bf16[32,5120]{1,0:T(8,128)(2,1)S(1)}, bf16[32,5120]{1,0:T(8,128)(2,1)S(1)}, u32[]{:S(2)}, u32[]{:S(2)}) collective-permute-start(bf16[32,5120]{1,0:T(8,128)(2,1)S(1)} %slice.54), channel_id=1, source_target_pairs={{0,2},{1,3},{2,4},{3,5},{4,6},{5,7},{6,0},{7,1},{8,10},{9,11},{10,... | collective-permute-start | bytes 983048 | tf_op jit(solution)/shard_map/ppermute | solution.py:400
  39.9 12.1 %collective-permute-start.3 = (bf16[32,5120]{1,0:T(8,128)(2,1)S(1)}, bf16[32,5120]{1,0:T(8,128)(2,1)S(1)}, u32[]{:S(2)}, u32[]{:S(2)}) collective-permute-start(bf16[32,5120]{1,0:T(8,128)(2,1)S(1)} %slice.53), channel_id=1, source_target_pairs={{0,6},{1,7},{2,0},{3,1},{4,2},{5,3},{6,4},{7,5},{8,14},{9,15},{10,... | collective-permute-start | bytes 983048 | tf_op jit(solution)/shard_map/ppermute | solution.py:400
  43.1 24.4 %collective-permute-start.13 = (bf16[1280,384]{1,0:T(8,128)(2,1)S(1)}, bf16[1280,384]{1,0:T(8,128)(2,1)S(1)}, u32[]{:S(2)}, u32[]{:S(2)}) collective-permute-start(bf16[1280,384]{1,0:T(8,128)(2,1)S(1)} %stack_rows.1.refs_10_), channel_id=1, source_target_pairs={{0,96},{8,104},{16,112},{24,120},{32,0},{40,8},{48,16},{56,24},{64... | collective-permute-start | bytes 2949128 | tf_op jit(solution)/shard_map/ppermute | solution.py:400
  48.4 20.9 %collective-permute-start.19 = (bf16[8,2,64,384]{3,2,1,0:T(8,128)(2,1)S(1)}, bf16[8,2,64,384]{3,2,1,0:T(8,128)(2,1)S(1)}, u32[]{:S(2)}, u32[]{:S(2)}) collective-permute-start(bf16[8,2,64,384]{3,2,1,0:T(8,128)(2,1)S(1)} %slice.57.kv0), channel_id=1, source_target_pairs={{0,24},{8,0},{16,8},{24,16},{32,56},{40,32},{48,40},{56,48},{1,25}... | collective-permute-start | bytes 2359304 | tf_op jit(solution)/shard_map/ppermute | solution.py:400
  51.5 19.3 %collective-permute-start.18 = (bf16[8,2,64,384]{3,2,1,0:T(8,128)(2,1)S(1)}, bf16[8,2,64,384]{3,2,1,0:T(8,128)(2,1)S(1)}, u32[]{:S(2)}, u32[]{:S(2)}) collective-permute-start(bf16[8,2,64,384]{3,2,1,0:T(8,128)(2,1)S(1)} %slice.57.kv0), channel_id=1, source_target_pairs={{0,8},{8,16},{16,24},{24,0},{32,40},{40,48},{48,56},{56,32},{1,9},... | collective-permute-start | bytes 2359304 | tf_op jit(solution)/shard_map/ppermute | solution.py:400
  53.6 23.8 %collective-permute-start.7 = (bf16[64,5120]{1,0:T(8,128)(2,1)S(1)}, bf16[64,5120]{1,0:T(8,128)(2,1)S(1)}, u32[]{:S(2)}, u32[]{:S(2)}) collective-permute-start(bf16[64,5120]{1,0:T(8,128)(2,1)S(1)} %collective-permute-done.2.refs_2_), channel_id=1, source_target_pairs={{0,1},{1,0},{2,3},{3,2},{4,5},{5,4},{6,7},{7,6},{8,9},{9,8},{10,11... | collective-permute-start | bytes 1966088 | tf_op jit(solution)/shard_map/ppermute | solution.py:400
  53.8 26.0 %collective-permute-start.6 = (bf16[64,5120]{1,0:T(8,128)(2,1)S(1)}, bf16[64,5120]{1,0:T(8,128)(2,1)S(1)}, u32[]{:S(2)}, u32[]{:S(2)}) collective-permute-start(bf16[64,5120]{1,0:T(8,128)(2,1)S(1)} %collective-permute-done.1.refs_1_), channel_id=1, source_target_pairs={{0,1},{1,0},{2,3},{3,2},{4,5},{5,4},{6,7},{7,6},{8,9},{9,8},{10,11... | collective-permute-start | bytes 1966088 | tf_op jit(solution)/shard_map/ppermute | solution.py:400
  69.3 15.8 %collective-permute-start.16 = (bf16[640,384]{1,0:T(8,128)(2,1)}, bf16[640,384]{1,0:T(8,128)(2,1)}, u32[]{:S(2)}, u32[]{:S(2)}) collective-permute-start(bf16[640,384]{1,0:T(8,128)(2,1)} %slice.56), channel_id=1, source_target_pairs={{0,32},{8,40},{16,48},{24,56},{32,64},{40,72},{48,80},{56,88},{64,... | collective-permute-start | bytes 1474568 | tf_op jit(solution)/shard_map/ppermute | solution.py:400
  70.8 14.5 %collective-permute-start.14 = (bf16[640,384]{1,0:T(8,128)(2,1)}, bf16[640,384]{1,0:T(8,128)(2,1)}, u32[]{:S(2)}, u32[]{:S(2)}) collective-permute-start(bf16[640,384]{1,0:T(8,128)(2,1)} %slice.55), channel_id=1, source_target_pairs={{0,96},{8,104},{16,112},{24,120},{32,0},{40,8},{48,16},{56,24},{64... | collective-permute-start | bytes 1474568 | tf_op jit(solution)/shard_map/ppermute | solution.py:400
  77.5 16.4 %collective-permute-start = (bf16[8,64,384]{2,1,0:T(8,128)(2,1)}, bf16[8,64,384]{2,1,0:T(8,128)(2,1)S(1)}, u32[]{:S(2)}, u32[]{:S(2)}) collective-permute-start(bf16[8,64,384]{2,1,0:T(8,128)(2,1)} %slice_bitcast_fusion.3.qa), channel_id=1, source_target_pairs={{0,32},{8,40},{16,48},{24,56},{32,0},{40,8},{48,16},{56,24},{1,33}... | collective-permute-start | bytes 1179656 | tf_op jit(solution)/shard_map/ppermute | solution.py:400
  77.6 16.3 %collective-permute-start.21 = (bf16[4,2,64,384]{3,2,1,0:T(8,128)(2,1)}, bf16[4,2,64,384]{3,2,1,0:T(8,128)(2,1)S(1)}, u32[]{:S(2)}, u32[]{:S(2)}) collective-permute-start(bf16[4,2,64,384]{3,2,1,0:T(8,128)(2,1)} %slice.59), channel_id=1, source_target_pairs={{0,24},{8,0},{16,8},{24,16},{32,56},{40,32},{48,40},{56,48},{1,25}... | collective-permute-start | bytes 1179656 | tf_op jit(solution)/shard_map/ppermute | solution.py:400
  79.7 14.2 %collective-permute-start.20 = (bf16[4,2,64,384]{3,2,1,0:T(8,128)(2,1)}, bf16[4,2,64,384]{3,2,1,0:T(8,128)(2,1)S(1)}, u32[]{:S(2)}, u32[]{:S(2)}) collective-permute-start(bf16[4,2,64,384]{3,2,1,0:T(8,128)(2,1)} %slice.58), channel_id=1, source_target_pairs={{0,8},{8,16},{16,24},{24,0},{32,40},{40,48},{48,56},{56,32},{1,9},... | collective-permute-start | bytes 1179656 | tf_op jit(solution)/shard_map/ppermute | solution.py:400
  92.6 22.9 %collective-permute-start.17 = (bf16[512,384]{1,0:T(8,128)(2,1)}, bf16[512,384]{1,0:T(8,128)(2,1)S(1)}, u32[]{:S(2)}, u32[]{:S(2)}) collective-permute-start(bf16[512,384]{1,0:T(8,128)(2,1)} %project.1.da), channel_id=1, source_target_pairs={{0,32},{8,40},{16,48},{24,56},{32,0},{40,8},{48,16},{56,24},{1,33}... | collective-permute-start | bytes 1179656 | tf_op jit(solution)/shard_map/ppermute | solution.py:400
  114.5 18.4 %collective-permute-start.24 = (bf16[512,384]{1,0:T(8,128)(2,1)S(1)}, bf16[512,384]{1,0:T(8,128)(2,1)S(1)}, u32[]{:S(2)}, u32[]{:S(2)}) collective-permute-start(bf16[512,384]{1,0:T(8,128)(2,1)S(1)} %get-tuple-element.47), channel_id=1, source_target_pairs={{0,32},{8,40},{16,48},{24,56},{32,0},{40,8},{48,16},{56,24},{1,33}... | collective-permute-start | bytes 1179656 | tf_op jit(solution)/shard_map/ppermute | solution.py:400
  138.0 28.1 %collective-permute-start.32 = (bf16[640,384]{1,0:T(8,128)(2,1)}, bf16[640,384]{1,0:T(8,128)(2,1)S(1)}, u32[]{:S(2)}, u32[]{:S(2)}) collective-permute-start(bf16[640,384]{1,0:T(8,128)(2,1)} %get-tuple-element.49), channel_id=1, source_target_pairs={{0,32},{8,40},{16,48},{24,56},{32,64},{40,72},{48,80},{56,88},{64,... | collective-permute-start | bytes 1474568 | tf_op jit(solution)/shard_map/ppermute | solution.py:400
  139.2 27.4 %collective-permute-start.33 = (bf16[640,384]{1,0:T(8,128)(2,1)}, bf16[640,384]{1,0:T(8,128)(2,1)S(1)}, u32[]{:S(2)}, u32[]{:S(2)}) collective-permute-start(bf16[640,384]{1,0:T(8,128)(2,1)} %get-tuple-element.50), channel_id=1, source_target_pairs={{0,96},{8,104},{16,112},{24,120},{32,0},{40,8},{48,16},{56,24},{64... | collective-permute-start | bytes 1474568 | tf_op jit(solution)/shard_map/ppermute | solution.py:400
  141.3 23.7 %collective-permute-start.25 = (bf16[4,2,64,384]{3,2,1,0:T(8,128)(2,1)S(1)}, bf16[4,2,64,384]{3,2,1,0:T(8,128)(2,1)S(1)}, u32[]{:S(2)}, u32[]{:S(2)}) collective-permute-start(bf16[4,2,64,384]{3,2,1,0:T(8,128)(2,1)S(1)} %copy-done.37), channel_id=1, source_target_pairs={{0,8},{8,16},{16,24},{24,0},{32,40},{40,48},{48,56},{56,32},{1,9},... | collective-permute-start | bytes 1179656 | tf_op jit(solution)/shard_map/ppermute | solution.py:400
  143.0 19.3 %collective-permute-start.29 = (bf16[4,2,64,384]{3,2,1,0:T(8,128)(2,1)}, bf16[4,2,64,384]{3,2,1,0:T(8,128)(2,1)S(1)}, u32[]{:S(2)}, u32[]{:S(2)}) collective-permute-start(bf16[4,2,64,384]{3,2,1,0:T(8,128)(2,1)} %get-tuple-element.59), channel_id=1, source_target_pairs={{0,24},{8,0},{16,8},{24,16},{32,56},{40,32},{48,40},{56,48},{1,25}... | collective-permute-start | bytes 1179656 | tf_op jit(solution)/shard_map/ppermute | solution.py:400
  162.0 13.9 %collective-permute-start.31 = (bf16[8,64,384]{2,1,0:T(8,128)(2,1)}, bf16[8,64,384]{2,1,0:T(8,128)(2,1)S(1)}, u32[]{:S(2)}, u32[]{:S(2)}) collective-permute-start(bf16[8,64,384]{2,1,0:T(8,128)(2,1)} %get-tuple-element.61), channel_id=1, source_target_pairs={{0,32},{8,40},{16,48},{24,56},{32,0},{40,8},{48,16},{56,24},{1,33}... | collective-permute-start | bytes 1179656 | tf_op jit(solution)/shard_map/ppermute | solution.py:400
  162.3 15.6 %collective-permute-start.27 = (bf16[4,2,64,384]{3,2,1,0:T(8,128)(2,1)S(1)}, bf16[4,2,64,384]{3,2,1,0:T(8,128)(2,1)}, u32[]{:S(2)}, u32[]{:S(2)}) collective-permute-start(bf16[4,2,64,384]{3,2,1,0:T(8,128)(2,1)S(1)} %copy-done.36), channel_id=1, source_target_pairs={{0,24},{8,0},{16,8},{24,16},{32,56},{40,32},{48,40},{56,48},{1,25}... | collective-permute-start | bytes 1179656 | tf_op jit(solution)/shard_map/ppermute | solution.py:400
  165.0 14.3 %collective-permute-start.28 = (bf16[4,2,64,384]{3,2,1,0:T(8,128)(2,1)}, bf16[4,2,64,384]{3,2,1,0:T(8,128)(2,1)}, u32[]{:S(2)}, u32[]{:S(2)}) collective-permute-start(bf16[4,2,64,384]{3,2,1,0:T(8,128)(2,1)} %get-tuple-element.57), channel_id=1, source_target_pairs={{0,8},{8,16},{16,24},{24,0},{32,40},{40,48},{48,56},{56,32},{1,9},... | collective-permute-start | bytes 1179656 | tf_op jit(solution)/shard_map/ppermute | solution.py:400
  166.1 15.8 %collective-permute-start.26 = (bf16[4,2,64,384]{3,2,1,0:T(8,128)(2,1)}, bf16[4,2,64,384]{3,2,1,0:T(8,128)(2,1)}, u32[]{:S(2)}, u32[]{:S(2)}) collective-permute-start(bf16[4,2,64,384]{3,2,1,0:T(8,128)(2,1)} %add_convert_fusion.4), channel_id=1, source_target_pairs={{0,8},{8,16},{16,24},{24,0},{32,40},{40,48},{48,56},{56,32},{1,9},... | collective-permute-start | bytes 1179656 | tf_op jit(solution)/shard_map/ppermute | solution.py:400
  166.5 15.3 %collective-permute-start.30 = (bf16[4,2,64,384]{3,2,1,0:T(8,128)(2,1)}, bf16[4,2,64,384]{3,2,1,0:T(8,128)(2,1)}, u32[]{:S(2)}, u32[]{:S(2)}) collective-permute-start(bf16[4,2,64,384]{3,2,1,0:T(8,128)(2,1)} %add_convert_fusion.2), channel_id=1, source_target_pairs={{0,24},{8,0},{16,8},{24,16},{32,56},{40,32},{48,40},{56,48},{1,25}... | collective-permute-start | bytes 1179656 | tf_op jit(solution)/shard_map/ppermute | solution.py:400
  176.0 20.3 %collective-permute-start.34 = (bf16[1280,384]{1,0:T(8,128)(2,1)}, bf16[1280,384]{1,0:T(8,128)(2,1)S(1)}, u32[]{:S(2)}, u32[]{:S(2)}) collective-permute-start(bf16[1280,384]{1,0:T(8,128)(2,1)} %get-tuple-element.64), channel_id=1, source_target_pairs={{0,32},{8,40},{16,48},{24,56},{32,64},{40,72},{48,80},{56,88},{64,... | collective-permute-start | bytes 2949128 | tf_op jit(solution)/shard_map/ppermute | solution.py:400
  178.0 18.5 %collective-permute-start.35 = (bf16[1280,384]{1,0:T(8,128)(2,1)}, bf16[1280,384]{1,0:T(8,128)(2,1)S(1)}, u32[]{:S(2)}, u32[]{:S(2)}) collective-permute-start(bf16[1280,384]{1,0:T(8,128)(2,1)} %get-tuple-element.65), channel_id=1, source_target_pairs={{0,96},{8,104},{16,112},{24,120},{32,0},{40,8},{48,16},{56,24},{64... | collective-permute-start | bytes 2949128 | tf_op jit(solution)/shard_map/ppermute | solution.py:400
  184.8 31.7 %all-to-all-start.1 = ((bf16[8,3,64,384]{3,2,1,0:T(8,128)(2,1)}), bf16[8,3,64,384]{3,2,1,0:T(8,128)(2,1)S(1)}, u32[]{:S(2)}, u32[]{:S(2)}) async-start(bf16[8,3,64,384]{3,2,1,0:T(8,128)(2,1)} %pad_maximum_fusion), calls=%async_computation.1 | async-start | bytes 2359296 | tf_op jit(solution)/shard_map/all_to_all | solution.py:429
  (48 other events, 399.5 us)

commit v3 on v2

v3 whole, which is shorter than its diff:
```python
import functools

import jax
import jax.numpy as jnp
from jax import lax
from jax.experimental import pallas as pl
from jax.experimental.pallas import tpu as pltpu
from jax.sharding import PartitionSpec as P

HD = 128
HEADS = 3
U = 8
T = 64
W = HEADS * HD
ROWS = U * T
SCALE = HD**-0.5
SCALE2 = SCALE * 1.4426950408889634
BF = jnp.bfloat16
F32 = jnp.float32
VMEM = 60 * 1024 * 1024


def nt(a, b):
    return lax.dot_general(a, b, (((1,), (1,)), ((), ())), preferred_element_type=F32)


def nn(a, b):
    return jnp.dot(a, b, preferred_element_type=F32)


def flat(ref):
    return ref[...].reshape(ROWS, HD)


def joined(low, high, i):
    return jnp.concatenate([low[:, i].reshape(ROWS // 2, HD), high[:, i].reshape(ROWS // 2, HD)], axis=0)


def forward_blocks(queries, blocks, state):
    top, total, acc = state
    later = nt(blocks[0][0], queries)
    for j, (_, values) in enumerate(blocks):
        scores = later
        if j + 1 < len(blocks):
            later = nt(blocks[j + 1][0], queries)
        peak = jnp.max(scores, axis=0, keepdims=True) * SCALE2
        if top is not None:
            peak = jnp.maximum(peak, top)
        weights = jnp.exp2(scores * SCALE2 - peak)
        sums = jnp.sum(weights, axis=0, keepdims=True)
        out = nn(values.T, weights.astype(BF))
        if top is not None:
            fade = jnp.exp2(top - peak)
            sums = sums + total * fade
            out = out + acc * fade
        top, total, acc = peak, sums, out
    return top, total, acc


def forward_near_kernel(qa, qb, kv0, kv1, kv2, ot_ref, st_ref):
    queries = jnp.concatenate([flat(qa), flat(qb)], axis=0)
    blocks = [(r[:, 0].reshape(ROWS, HD), r[:, 1].reshape(ROWS, HD)) for r in (kv0, kv1, kv2)]
    st_ref[0, 0:1], st_ref[0, 1:2], ot_ref[...] = forward_blocks(queries, blocks, (None, None, None))


def forward_far_kernel(qa, qb, kv3a, kv3b, ot_in, st_in, ot_ref, st_ref):
    queries = jnp.concatenate([flat(qa), flat(qb)], axis=0)
    blocks = [(joined(kv3a, kv3b, 0), joined(kv3a, kv3b, 1))]
    state = (st_in[0, 0:1], st_in[0, 1:2], ot_in[...])
    st_ref[0, 0:1], st_ref[0, 1:2], ot_ref[...] = forward_blocks(queries, blocks, state)


Q_SPEC = pl.BlockSpec((U, T, HD), lambda h: (0, 0, h))
KV_SPEC = pl.BlockSpec((U, 2, T, HD), lambda h: (0, 0, 0, h))
HALF_SPEC = pl.BlockSpec((U // 2, 2, T, HD), lambda h: (0, 0, 0, h))
OT_SPEC = pl.BlockSpec((HD, 2 * ROWS), lambda h: (h, 0))
ST_SPEC = pl.BlockSpec((1, 8, 2 * ROWS), lambda h: (h, 0, 0))
ROW_SPEC = pl.BlockSpec((ROWS, HD), lambda h: (0, h))
SMALL_VMEM = 24 * 1024 * 1024
PARAMS = pltpu.CompilerParams(vmem_limit_bytes=VMEM, dimension_semantics=("arbitrary",))
SMALL = pltpu.CompilerParams(vmem_limit_bytes=SMALL_VMEM, dimension_semantics=("arbitrary",))


def struct(shape, dtype):
    return jax.ShapeDtypeStruct(shape, dtype)


def cost(flops, nbytes):
    return pl.CostEstimate(flops=flops, bytes_accessed=nbytes, transcendentals=0)


def forward_call(kernel, name, blocks, in_specs, operands):
    return pl.pallas_call(
        kernel,
        grid=(HEADS,),
        in_specs=in_specs,
        out_specs=[OT_SPEC, ST_SPEC],
        out_shape=[struct((W, 2 * ROWS), F32), struct((HEADS, 8, 2 * ROWS), F32)],
        compiler_params=PARAMS,
        cost_estimate=cost(blocks * 4 * 1024 * ROWS * W, (blocks + 2) << 20),
        name=name,
    )(*operands)


def forward_near(*operands):
    return forward_call(forward_near_kernel, "forward_near", 3, [Q_SPEC] * 2 + [KV_SPEC] * 3, operands)


def forward_far(*operands):
    specs = [Q_SPEC] * 2 + [HALF_SPEC] * 2 + [OT_SPEC, ST_SPEC]
    return forward_call(forward_far_kernel, "forward_far", 1, specs, operands)


def dot_kernel(ot_ref, st_ref, da, db, out_ref):
    out_ref[0, 0:2] = st_ref[0, 0:2]
    for part, d in enumerate((da, db)):
        at = slice(part * ROWS, (part + 1) * ROWS)
        grad_t = d[...].astype(F32).T
        out_ref[0, 2:3, at] = jnp.sum(grad_t * ot_ref[:, at], axis=0, keepdims=True)


def row_dots(ot, st, da, db):
    return pl.pallas_call(
        dot_kernel,
        grid=(HEADS,),
        in_specs=[OT_SPEC, ST_SPEC, ROW_SPEC, ROW_SPEC],
        out_specs=ST_SPEC,
        out_shape=struct((HEADS, 8, 2 * ROWS), F32),
        compiler_params=SMALL,
        cost_estimate=cost(1 << 20, 3 << 20),
        name="row_dots",
    )(ot, st, da, db)


def merge_kernel(ot_ref, st_ref, pst_ref, keep_ref, send_ref, fin_ref):
    mine = st_ref[0]
    other = pst_ref[0]
    other = jnp.concatenate([other[:, ROWS:], other[:, :ROWS]], axis=1)
    top = jnp.maximum(mine[0:1], other[0:1])
    a = jnp.exp2(mine[0:1] - top)
    b = jnp.exp2(other[0:1] - top)
    total = a * mine[1:2] + b * other[1:2]
    fin_ref[0, 0:1] = top + jnp.log2(total)
    fin_ref[0, 1:2] = (a * mine[2:3] + b * other[2:3]) / total
    out_t = ot_ref[...] * (a / total)
    keep_ref[...] = out_t[:, :ROWS].T
    send_ref[...] = out_t[:, ROWS:].T.astype(BF)


def merge(ot, st, pst):
    return pl.pallas_call(
        merge_kernel,
        grid=(HEADS,),
        in_specs=[OT_SPEC, ST_SPEC, ST_SPEC],
        out_specs=[ROW_SPEC, ROW_SPEC, ST_SPEC],
        out_shape=[struct((ROWS, W), F32), struct((ROWS, W), BF), struct((HEADS, 8, 2 * ROWS), F32)],
        compiler_params=SMALL,
        cost_estimate=cost(1 << 20, 3 << 20),
        name="merge_halves",
    )(ot, st, pst)


FEATURES = 5120
QUARTER = FEATURES // 4
SHARD = FEATURES // 16
ANY_SPEC = pl.BlockSpec(memory_space=pl.ANY)
SMEM_SPEC = pl.BlockSpec(memory_space=pltpu.SMEM)
VMEM_SPEC = pl.BlockSpec(memory_space=pltpu.VMEM)
PLAIN = pltpu.CompilerParams(vmem_limit_bytes=VMEM)


def stack_kernel(*refs):
    for i, piece in enumerate(refs[:4]):
        refs[4][i * SHARD : (i + 1) * SHARD] = piece[...]


def stacked_rows(*pieces):
    return pl.pallas_call(
        stack_kernel,
        in_specs=[VMEM_SPEC] * 4,
        out_specs=VMEM_SPEC,
        out_shape=struct((QUARTER, W), BF),
        compiler_params=pltpu.CompilerParams(vmem_limit_bytes=SMALL_VMEM),
        cost_estimate=cost(0, 2 << 20),
        name="stack_rows",
    )(*pieces)


def project_kernel(place, grad, w0, w1, w2a, w2b, w3, out_ref, held, weight, sems):
    groups = []
    for oz in range(4):
        quarter = lax.rem(place[2] + oz, 4)
        columns = pl.ds(pl.multiple_of(quarter * QUARTER, 128), QUARTER)
        copies = [pltpu.make_async_copy(grad.at[:, columns], held.at[oz], sems.at[oz, 4])]
        for oy in range(4):
            source, row = ((w0, oy), (w1, oy), (w2a, oy) if oy < 2 else (w2b, oy - 2), (w3, oy))[oz]
            at = pl.multiple_of(lax.rem(place[3] + oy, 4) * SHARD, SHARD)
            target = weight.at[oz, pl.ds(at, SHARD)]
            copies.append(pltpu.make_async_copy(source.at[pl.ds(row * SHARD, SHARD)], target, sems.at[oz, oy]))
        for c in copies:
            c.start()
        groups.append(copies)
    total = None
    for oz in range(4):
        for c in groups[oz]:
            c.wait()
        part = nn(held[oz], weight[oz])
        total = part if total is None else total + part
    out_ref[...] = total.astype(BF)


def project(place, grad, weights):
    return pl.pallas_call(
        project_kernel,
        in_specs=[SMEM_SPEC] + [ANY_SPEC] * 6,
        out_specs=VMEM_SPEC,
        out_shape=struct((ROWS, W), BF),
        scratch_shapes=[
            pltpu.VMEM((4, ROWS, QUARTER), BF),
            pltpu.VMEM((4, QUARTER, W), BF),
            pltpu.SemaphoreType.DMA((4, 5)),
        ],
        compiler_params=PLAIN,
        cost_estimate=cost(2 * ROWS * FEATURES * W, 10 << 20),
        name="project",
    )(place, grad, *weights)


def tn(a, b):
    return lax.dot_general(a, b, (((0,), (0,)), ((), ())), preferred_element_type=F32)


def weight_part(place, oz, grad, attn, held, sem):
    at = lax.rem(place[2] + oz, 4) * QUARTER
    copy = pltpu.make_async_copy(grad.at[:, pl.ds(pl.multiple_of(at, 128), QUARTER)], held, sem)
    copy.start()
    copy.wait()
    return tn(held[...], attn[...])


def weight_far_kernel(place, grad, attn, a_ref, b_ref, held, sem):
    part = weight_part(place, 2, grad, attn, held, sem).astype(BF)
    a_ref[...] = part[: QUARTER // 2]
    b_ref[...] = part[QUARTER // 2 :]


def weight_near_kernel(place, grad, attn, a_got, b_got, up_ref, down_ref, held, sem):
    half = QUARTER // 2
    part = weight_part(place, 1, grad, attn, held, sem)
    up_ref[:half] = (part[:half] + a_got[...].astype(F32)).astype(BF)
    up_ref[half:] = part[half:].astype(BF)
    part = weight_part(place, 3, grad, attn, held, sem)
    down_ref[:half] = part[:half].astype(BF)
    down_ref[half:] = (part[half:] + b_got[...].astype(F32)).astype(BF)


def weight_own_kernel(place, grad, attn, below, above, o0, o1, o2, o3, held, sem, total):
    part = weight_part(place, 0, grad, attn, held, sem)
    total[...] = part + below[...].astype(F32) + above[...].astype(F32)
    for oy, o in enumerate((o0, o1, o2, o3)):
        at = pl.multiple_of(lax.rem(place[3] + oy, 4) * SHARD, SHARD)
        o[...] = total[pl.ds(at, SHARD)].astype(o.dtype)


def weight_call(kernel, name, parts, outs, extra, place, grad, *more):
    return pl.pallas_call(
        kernel,
        in_specs=[SMEM_SPEC, ANY_SPEC] + [VMEM_SPEC] * len(more),
        out_specs=[VMEM_SPEC] * len(outs),
        out_shape=outs,
        scratch_shapes=[pltpu.VMEM((ROWS, QUARTER), BF), pltpu.SemaphoreType.DMA] + extra,
        compiler_params=PLAIN,
        cost_estimate=cost(parts * 2 * ROWS * QUARTER * W, parts * 3 << 20),
        name=name,
    )(place, grad, *more)


CHUNK = 256


def backward_block(keys, values, queries, grads, log_total, row_dot):
    scores = nt(keys, queries)
    probs = jnp.exp2(scores * SCALE2 - log_total)
    grad_probs = nt(values, grads)
    grad_scores = (probs * (grad_probs - row_dot)).astype(BF)
    grad_values = nn(probs.astype(BF), grads)
    grad_keys = nn(grad_scores, queries) * SCALE
    grad_queries_t = nn(keys.T, grad_scores)
    return grad_keys, grad_values, grad_queries_t


def backward_common(qa, qb, da, db, fin):
    queries = jnp.concatenate([flat(qa), flat(qb)], axis=0)
    grads = jnp.concatenate([da[...], db[...]], axis=0)
    return queries, grads, fin[0, 0:1], fin[0, 1:2]


def chunks_of(x):
    return [x[i * CHUNK : (i + 1) * CHUNK] for i in range(ROWS // CHUNK)]


def run_block(keys, values, common):
    dks, dvs, dqt = [], [], None
    for k, v in zip(chunks_of(keys), chunks_of(values)):
        dk, dv, q = backward_block(k, v, *common)
        dks.append(dk)
        dvs.append(dv)
        dqt = q if dqt is None else dqt + q
    return jnp.concatenate(dks, axis=0), jnp.concatenate(dvs, axis=0), dqt


def store_halves(low, high, i, x):
    low[:, i] = x[: ROWS // 2].astype(low.dtype).reshape(U // 2, T, HD)
    high[:, i] = x[ROWS // 2 :].astype(high.dtype).reshape(U // 2, T, HD)


def far_kernel(qa, qb, da, db, fin, kv3a, kv3b, low_ref, high_ref, dqt_ref):
    common = backward_common(qa, qb, da, db, fin)
    dk, dv, dqt = run_block(joined(kv3a, kv3b, 0), joined(kv3a, kv3b, 1), common)
    store_halves(low_ref, high_ref, 0, dk)
    store_halves(low_ref, high_ref, 1, dv)
    dqt_ref[...] = dqt


def near_kernel(qa, qb, da, db, fin, kv1, kv2, dqt_in, o1_ref, o2_ref, dqt_ref):
    common = backward_common(qa, qb, da, db, fin)
    total = dqt_in[...]
    for kv, o in ((kv1, o1_ref), (kv2, o2_ref)):
        dk, dv, dqt = run_block(kv[:, 0].reshape(ROWS, HD), kv[:, 1].reshape(ROWS, HD), common)
        o[:, 0] = dk.reshape(U, T, HD)
        o[:, 1] = dv.reshape(U, T, HD)
        total = total + dqt
    dqt_ref[...] = total


def own_kernel(qa, qb, da, db, fin, kv0, dqt_in, o0_ref, qkeep_ref, qsend_ref):
    common = backward_common(qa, qb, da, db, fin)
    dk, dv, dqt = run_block(kv0[:, 0].reshape(ROWS, HD), kv0[:, 1].reshape(ROWS, HD), common)
    o0_ref[:, 0] = dk.reshape(U, T, HD)
    o0_ref[:, 1] = dv.reshape(U, T, HD)
    total = (dqt_in[...] + dqt) * SCALE
    qkeep_ref[...] = total[:, :ROWS].T.reshape(U, T, HD)
    qsend_ref[...] = total[:, ROWS:].T.astype(BF).reshape(U, T, HD)


COMMON_SPECS = [Q_SPEC, Q_SPEC, ROW_SPEC, ROW_SPEC, ST_SPEC]


def backward_far(common, kv3a, kv3b):
    return pl.pallas_call(
        far_kernel,
        grid=(HEADS,),
        in_specs=COMMON_SPECS + [HALF_SPEC, HALF_SPEC],
        out_specs=[HALF_SPEC, HALF_SPEC, OT_SPEC],
        out_shape=[struct((U // 2, 2, T, W), BF)] * 2 + [struct((W, 2 * ROWS), F32)],
        compiler_params=PARAMS,
        cost_estimate=cost(5 * 2 * 1024 * 512 * W, 6 << 20),
        name="backward_far",
    )(*common, kv3a, kv3b)


def backward_near(common, kv1, kv2, dqt):
    return pl.pallas_call(
        near_kernel,
        grid=(HEADS,),
        in_specs=COMMON_SPECS + [KV_SPEC, KV_SPEC, OT_SPEC],
        out_specs=[KV_SPEC, KV_SPEC, OT_SPEC],
        out_shape=[struct((U, 2, T, W), F32)] * 2 + [struct((W, 2 * ROWS), F32)],
        compiler_params=PARAMS,
        cost_estimate=cost(5 * 2 * 1024 * 1024 * W, 9 << 20),
        name="backward_near",
    )(*common, kv1, kv2, dqt)


def backward_own(common, kv0, dqt):
    return pl.pallas_call(
        own_kernel,
        grid=(HEADS,),
        in_specs=COMMON_SPECS + [KV_SPEC, OT_SPEC],
        out_specs=[KV_SPEC, Q_SPEC, Q_SPEC],
        out_shape=[struct((U, 2, T, W), F32), struct((U, T, W), F32), struct((U, T, W), BF)],
        compiler_params=PARAMS,
        cost_estimate=cost(5 * 2 * 1024 * 512 * W, 8 << 20),
        name="backward_own",
    )(*common, kv0, dqt)


def move(x, axis, to, n):
    return lax.ppermute(x, axis, [(i, to(i)) for i in range(n)])


def y_shift(x, d):
    return move(x, "blk", lambda i: i // 4 * 4 + (i + d) % 4, 8)


def z_shift(x, d):
    return move(x, ("dp", "blk"), lambda i: (i // 4 + d) % 4 * 4 + i % 4, 16)


def z_swap(x):
    return move(x, "blk", lambda i: (i + 4) % 8, 8)


def by_head(*rows):
    stacked = jnp.concatenate([r.reshape(T, U, 1, W) for r in rows], axis=2)
    return jnp.transpose(stacked, (1, 2, 0, 3))


def exchange(x):
    return lax.all_to_all(x, "uly", split_axis=0, concat_axis=0, tiled=True)


def to_tokens(x):
    got = exchange(x)
    return [jnp.transpose(got[:, i], (1, 0, 2)).reshape(T, U * W) for i in range(x.shape[1])]


def after(x, *others):
    return lax.optimization_barrier((x, *others))[0]


def per_device(query_rows, key_rows, value_rows, out_grad, out_weight):
    uly, blk = lax.axis_index("uly"), lax.axis_index("blk")
    place = jnp.stack([uly // 2, uly % 2, lax.axis_index("dp") * 2 + blk // 4, blk % 4]).astype(jnp.int32)
    leaving = by_head(key_rows, value_rows, query_rows)
    grad_block = lax.all_gather(out_grad, "uly", axis=0, tiled=True)
    shards = (out_weight, y_shift(out_weight, -1), y_shift(out_weight, 2), y_shift(out_weight, 1))
    heads = exchange(leaving)
    weight_own = stacked_rows(*after(shards, leaving))
    heads = after(heads, weight_own)
    kv0, qa = heads[:, :2], heads[:, 2]
    kv_prev, kv_next = y_shift(kv0, 1), y_shift(kv0, -1)
    qb = z_swap(qa)
    weight_below, weight_above = z_shift(weight_own, 1), z_shift(weight_own, -1)
    cut = QUARTER // 2
    weights = (weight_own, weight_above, z_shift(weight_above[:cut], -1), z_shift(weight_below[cut:], 1), weight_below)
    far_low, far_high = y_shift(kv_prev[: U // 2], 1), y_shift(kv_next[U // 2 :], -1)
    ot, st = forward_near(qa, qb, kv0, kv_prev, kv_next)
    da = project(after(place, ot), grad_block, weights)
    db = z_swap(da)
    ot, st = forward_far(after(qa, da), qb, far_low, far_high, ot, st)
    st = row_dots(ot, st, da, db)
    o_keep, o_send, fin = merge(ot, st, z_swap(st))
    attn_out = (o_keep + z_swap(o_send).astype(F32)).astype(BF)
    common = (qa, qb, da, db, fin)

    low, high, dqt = backward_far(common, far_low, far_high)
    low_got, high_got = y_shift(low, 1), y_shift(high, -1)
    half = struct((QUARTER // 2, W), BF)
    a, b = weight_call(weight_far_kernel, "weight_far", 1, [half, half], [], place, grad_block, after(attn_out, dqt))
    a_got, b_got = z_shift(a, 1), z_shift(b, -1)
    g_prev, g_next, dqt = backward_near(common, kv_prev, kv_next, after(dqt, a, b))
    low_half, high_half = slice(0, U // 2), slice(U // 2, U)
    to_next = jnp.concatenate([g_next[low_half] + low_got.astype(F32), g_next[high_half]], axis=0)
    to_prev = jnp.concatenate([g_prev[low_half], g_prev[high_half] + high_got.astype(F32)], axis=0)
    from_below, from_above = y_shift(to_next.astype(BF), 1), y_shift(to_prev.astype(BF), -1)
    g_own, q_keep, q_send = backward_own(common, kv0, dqt)
    whole = struct((QUARTER, W), BF)
    up, down = weight_call(
        weight_near_kernel, "weight_near", 2, [whole, whole], [], place, grad_block, after(attn_out, q_send), a_got, b_got
    )
    below, above = z_shift(up, 1), z_shift(down, -1)
    dq = (q_keep + z_swap(q_send).astype(F32)).astype(BF)
    dkv = (g_own + from_below.astype(F32) + from_above.astype(F32)).astype(BF)
    grads = jnp.concatenate([dkv, dq[:, None]], axis=1)
    grad_key, grad_value, grad_query = to_tokens(grads)
    o0, o1, o2, o3 = weight_call(
        weight_own_kernel,
        "weight_own",
        1,
        [struct((SHARD, W), F32)] + [struct((SHARD, W), BF)] * 3,
        [pltpu.VMEM((QUARTER, W), F32)],
        place,
        grad_block,
        after(attn_out, grads),
        below,
        above,
    )
    grad_weight = o0 + y_shift(o1, 1).astype(F32) + y_shift(o2, 2).astype(F32) + y_shift(o3, -1).astype(F32)
    return (grad_query, grad_key, grad_value, grad_weight)


def solution(mesh):
    rows = P(("dp", "blk", "uly"), None)
    weight = P(("dp", "blk"), "uly")
    return jax.shard_map(
        per_device,
        mesh=mesh,
        in_specs=(rows, rows, rows, rows, weight),
        out_specs=(rows, rows, rows, weight),
        check_vma=False,
    )
```

time: 220 us -> 205 us (0.932)
  waiting for transfers between devices: 70.7 us -> 49 us
  between operations: 1.15 us -> 14.5 us
  starting transfers between devices: 60.8 us -> 48.4 us
  local copies, waits for them, and re-layouts: 17.5 us -> 20.5 us
  Pallas kernels: 59.6 us -> 62.1 us
    ppermute x39 -> x27, waiting for transfers between devices: 69.6 us -> 44.2 us  [move(): return lax.ppermute(x, axis, [(i, to(i)) for i in range(n)])]
    ppermute x39 -> x27, starting transfers between devices: 52.7 us -> 39.7 us  [move(): return lax.ppermute(x, axis, [(i, to(i)) for i in range(n)])]
    slice x6, local copies, waits for them, and re-layouts: 3.39 us -> 8.01 us  [the longest x1 1.78 us: per_device(): kv_prev[:U // 2]]
    all_to_all x2, waiting for transfers between devices: 1.08 us -> 4.1 us  [exchange(): return lax.all_to_all(x, 'uly', split_axis=0, concat_axis=0, tiled=True)]
    pallas_call x5 -> x6, Pallas kernels: 34.4 us -> 37 us  [the longest x3 15.4 us: weight_call(): pl.pallas_call(kernel, in_specs=[SMEM_SPEC, ANY_SPEC] + [VMEM_SPEC] * len...]
    unnamed x82 -> x48, local copies, waits for them, and re-layouts: 8.63 us -> 8.9 us
  transfers between devices with their start and end apart: 41 -> 30, of which waited for: 16 -> 10; matrix products, arithmetic and copies ran while one was open for 6% -> 10% of each run, Pallas kernels for 25% -> 30%
where the time goes in v3:
time: 205 us; the launch traced here: 204 us
  Pallas kernels  62.1 us (30%)
  waiting for transfers between devices  49 us (24%)
  starting transfers between devices  48.4 us (24%)
  local copies, waits for them, and re-layouts  20.5 us (10%)
  between operations  14.5 us (7%)
  other arithmetic  9.02 us (4%)
    ppermute x27, waiting for transfers between devices, move(): return lax.ppermute(x, axis, [(i, to(i)) for i in range(n)])  44.2 us
    ppermute x27, starting transfers between devices, move(): return lax.ppermute(x, axis, [(i, to(i)) for i in range(n)])  39.7 us
    pallas_call x3, Pallas kernels, weight_call(): pl.pallas_call(kernel, in_specs=[SMEM_SPEC, ANY_SPEC] + [VMEM_SPEC] * len...  15.4 us
    pallas_call x2, Pallas kernels, forward_call(): pl.pallas_call(kernel, grid=(HEADS,), in_specs=in_specs, out_specs=[OT_SP...  14.7 us
    pallas_call x1, Pallas kernels, backward_near(): pl.pallas_call(near_kernel, grid=(HEADS,), in_specs=COMMON_SPECS + [KV_SP...  10.5 us
    unnamed x48, local copies, waits for them, and re-layouts  8.9 us
    all_to_all x2, starting transfers between devices, exchange(): return lax.all_to_all(x, 'uly', split_axis=0, concat_axis=0, tiled=True)  8.68 us
    pallas_call x1, Pallas kernels, project(): pl.pallas_call(project_kernel, in_specs=[SMEM_SPEC] + [ANY_SPEC] * 6, out...  6.83 us
  transfers between devices with their start and end apart: 30, of which 10 were waited for; matrix products, arithmetic and copies ran while one was open for 10% of the time, Pallas kernels for 30%

profile of v3, /device:TPU:0, one launch (start us, length us, event | category | flops | bytes accessed | tf_op | source)
XLA Modules:
  0.0 203.5 jit_solution(8867832991343552259)
XLA Ops:
  10.5 4.5 %all-to-all-start = ((bf16[8,3,64,384]{3,2,1,0:T(8,128)(2,1)}), bf16[8,3,64,384]{3,2,1,0:T(8,128)(2,1)S(1)}, u32[]{:S(2)}, u32[]{:S(2)}) async-start(bf16[8,3,64,384]{3,2,1,0:T(8,128)(2,1)} %maximum_bitcast_fusion), calls=%async_computation | async-start | bytes 2359296 | tf_op jit(solution)/shard_map/all_to_all | solution.py:410
  15.0 3.3 %collective-permute-start.1 = (bf16[320,384]{1,0:T(8,128)(2,1)S(1)}, bf16[320,384]{1,0:T(8,128)(2,1)S(1)}, u32[]{:S(2)}, u32[]{:S(2)}) collective-permute-start(bf16[320,384]{1,0:T(8,128)(2,1)S(1)} %copy-done.5), channel_id=1, source_target_pairs={{0,16},{8,24},{16,0},{24,8},{32,48},{40,56},{48,32},{56,40},{1,17}... | collective-permute-start | bytes 737288 | tf_op jit(solution)/shard_map/ppermute | solution.py:389
  20.3 5.0 %collective-permute-done.1.refs_2_ = bf16[320,384]{1,0:T(8,128)(2,1)S(1)} collective-permute-done((bf16[320,384]{1,0:T(8,128)(2,1)S(1)}, bf16[320,384]{1,0:T(8,128)(2,1)S(1)}, u32[]{:S(2)}, u32[]{:S(2)}) %collective-permute-start.1) | collective-permute-done | bytes 245792 | tf_op jit(solution)/shard_map/ppermute | solution.py:389
  25.4 5.2 %collective-permute-done.refs_1_ = bf16[320,384]{1,0:T(8,128)(2,1)S(1)} collective-permute-done((bf16[320,384]{1,0:T(8,128)(2,1)S(1)}, bf16[320,384]{1,0:T(8,128)(2,1)S(1)}, u32[]{:S(2)}, u32[]{:S(2)}) %collective-permute-start) | collective-permute-done | bytes 245792 | tf_op jit(solution)/shard_map/ppermute | solution.py:389
  30.7 2.0 collective-permute-start.8
  32.7 2.2 %collective-permute-start.6 = (bf16[1280,384]{1,0:T(8,128)(2,1)S(1)}, bf16[1280,384]{1,0:T(8,128)(2,1)}, u32[]{:S(2)}, u32[]{:S(2)}) collective-permute-start(bf16[1280,384]{1,0:T(8,128)(2,1)S(1)} %stack_rows.1.w0), channel_id=1, source_target_pairs={{0,96},{8,104},{16,112},{24,120},{32,0},{40,8},{48,16},{56,24},{64... | collective-permute-start | bytes 2949128 | tf_op jit(solution)/shard_map/ppermute | solution.py:389
  34.9 4.1 %all-to-all-done = bf16[8,3,64,384]{3,2,1,0:T(8,128)(2,1)S(1)} async-done(((bf16[8,3,64,384]{3,2,1,0:T(8,128)(2,1)}), bf16[8,3,64,384]{3,2,1,0:T(8,128)(2,1)S(1)}, u32[]{:S(2)}, u32[]{:S(2)}) %all-to-all-start) | async-done | bytes 1179680 | tf_op jit(solution)/shard_map/all_to_all | solution.py:410
  40.0 3.3 %collective-permute-start.5 = (bf16[8,2,64,384]{3,2,1,0:T(8,128)(2,1)}, bf16[8,2,64,384]{3,2,1,0:T(8,128)(2,1)}, u32[]{:S(2)}, u32[]{:S(2)}) collective-permute-start(bf16[8,2,64,384]{3,2,1,0:T(8,128)(2,1)} %slice.42.kv0), channel_id=1, source_target_pairs={{0,24},{8,0},{16,8},{24,16},{32,56},{40,32},{48,40},{56,48},{1,25}... | collective-permute-start | bytes 2359304 | tf_op jit(solution)/shard_map/ppermute | solution.py:389
  43.3 2.4 %collective-permute-start.3 = (bf16[8,64,384]{2,1,0:T(8,128)(2,1)S(1)}, bf16[8,64,384]{2,1,0:T(8,128)(2,1)}, u32[]{:S(2)}, u32[]{:S(2)}) collective-permute-start(bf16[8,64,384]{2,1,0:T(8,128)(2,1)S(1)} %slice_bitcast_fusion.3.qa), channel_id=1, source_target_pairs={{0,32},{8,40},{16,48},{24,56},{32,0},{40,8},{48,16},{56,24},{1,33}... | collective-permute-start | bytes 1179656 | tf_op jit(solution)/shard_map/ppermute | solution.py:389
  45.7 10.8 %collective-permute-done.8.w3 = bf16[1280,384]{1,0:T(8,128)(2,1)S(1)} collective-permute-done((bf16[1280,384]{1,0:T(8,128)(2,1)S(1)}, bf16[1280,384]{1,0:T(8,128)(2,1)S(1)}, u32[]{:S(2)}, u32[]{:S(2)}) %collective-permute-start.8) | collective-permute-done | bytes 983072 | tf_op jit(solution)/shard_map/ppermute | solution.py:389
  59.3 2.4 %collective-permute-start.7 = (bf16[640,384]{1,0:T(8,128)(2,1)S(1)}, bf16[640,384]{1,0:T(8,128)(2,1)S(1)}, u32[]{:S(2)}, u32[]{:S(2)}) collective-permute-start(bf16[640,384]{1,0:T(8,128)(2,1)S(1)} %slice.54), channel_id=1, source_target_pairs={{0,96},{8,104},{16,112},{24,120},{32,0},{40,8},{48,16},{56,24},{64... | collective-permute-start | bytes 1474568 | tf_op jit(solution)/shard_map/ppermute | solution.py:389
  64.2 3.0 %collective-permute-start.12 = (bf16[4,2,64,384]{3,2,1,0:T(8,128)(2,1)}, bf16[4,2,64,384]{3,2,1,0:T(8,128)(2,1)S(1)}, u32[]{:S(2)}, u32[]{:S(2)}) collective-permute-start(bf16[4,2,64,384]{3,2,1,0:T(8,128)(2,1)} %slice.57), channel_id=1, source_target_pairs={{0,24},{8,0},{16,8},{24,16},{32,56},{40,32},{48,40},{56,48},{1,25}... | collective-permute-start | bytes 1179656 | tf_op jit(solution)/shard_map/ppermute | solution.py:389
  69.0 9.0 %forward_near.1 = (f32[384,1024]{1,0:T(8,128)}, f32[3,8,1024]{2,1,0:T(8,128)}) custom-call(bf16[8,64,384]{2,1,0:T(8,128)(2,1)} %copy-done.9, bf16[8,64,384]{2,1,0:T(8,128)(2,1)} %collective-permute-done.3.qb, bf16[8,2,64,384]{3,2,1,0:T(8,128)(2,1)} %slice.42.kv0, bf16[8,2,64,384]{3,2,1,0:T(8,128)(2,1)} %collective-permute-done.4.kv1, ...), custom_call_target="tpu_custom_call" | custom-call | flops 2415919104 | bytes 5242880 | tf_op jit(solution)/shard_map/forward_near/pallas_call | solution.py:93
  79.0 6.8 %project.1.da = bf16[512,384]{1,0:T(8,128)(2,1)} custom-call(s32[4]{0:T(128)} %pad_add_fusion.place, bf16[512,5120]{1,0:T(8,128)(2,1)} %all-gather.2.cloned.1.call-done.grad, bf16[1280,384]{1,0:T(8,128)(2,1)} %copy-done.2, bf16[1280,384]{1,0:T(8,128)(2,1)} %collective-permute-done.6.w1, bf16[640,384]{1,0:T(8,128)(2,1)} %copy-done.16, ...), custom_call_target="tpu_custom_call" | custom-call | flops 2013265920 | bytes 10485760 | tf_op jit(solution)/shard_map/project/pallas_call | solution.py:213
  86.7 5.7 %forward_far.1 = (f32[384,1024]{1,0:T(8,128)}, f32[3,8,1024]{2,1,0:T(8,128)}) custom-call(bf16[8,64,384]{2,1,0:T(8,128)(2,1)} %copy-done.9, bf16[8,64,384]{2,1,0:T(8,128)(2,1)} %collective-permute-done.3.qb, bf16[4,2,64,384]{3,2,1,0:T(8,128)(2,1)} %collective-permute-done.11.kv3a, bf16[4,2,64,384]{3,2,1,0:T(8,128)(2,1)} %copy-done.19, ...), custom_call_target="tpu_custom_call" | custom-call | flops 805306368 | bytes 3145728 | tf_op jit(solution)/shard_map/forward_far/pallas_call | solution.py:93
  92.4 3.7 %collective-permute-done.10.db = bf16[512,384]{1,0:T(8,128)(2,1)S(1)} collective-permute-done((bf16[512,384]{1,0:T(8,128)(2,1)}, bf16[512,384]{1,0:T(8,128)(2,1)S(1)}, u32[]{:S(2)}, u32[]{:S(2)}) %collective-permute-start.10) | collective-permute-done | bytes 393248 | tf_op jit(solution)/shard_map/ppermute | solution.py:389
  99.5 4.3 %collective-permute-done.13.pst_ref = f32[3,8,1024]{2,1,0:T(8,128)S(1)} collective-permute-done((f32[3,8,1024]{2,1,0:T(8,128)S(1)}, f32[3,8,1024]{2,1,0:T(8,128)S(1)}, u32[]{:S(2)}, u32[]{:S(2)}) %collective-permute-start.13) | collective-permute-done | bytes 98336 | tf_op jit(solution)/shard_map/ppermute | solution.py:389
  105.5 6.4 %backward_far.1 = (bf16[4,2,64,384]{3,2,1,0:T(8,128)(2,1)}, bf16[4,2,64,384]{3,2,1,0:T(8,128)(2,1)}, f32[384,1024]{1,0:T(8,128)}) custom-call(bf16[8,64,384]{2,1,0:T(8,128)(2,1)} %copy-done.9, bf16[8,64,384]{2,1,0:T(8,128)(2,1)} %collective-permute-done.3.qb, bf16[512,384]{1,0:T(8,128)(2,1)} %project.1.da, bf16[512,384]{1,0:T(8,128)(2,1)} %copy-done.4, ...), custom_call_target="tpu_custom_call" | custom-call | flops 2013265920 | bytes 6291456 | tf_op jit(solution)/shard_map/backward_far/pallas_call | solution.py:350
  111.9 3.2 %collective-permute-start.17 = (bf16[4,2,64,384]{3,2,1,0:T(8,128)(2,1)}, bf16[4,2,64,384]{3,2,1,0:T(8,128)(2,1)S(1)}, u32[]{:S(2)}, u32[]{:S(2)}) collective-permute-start(bf16[4,2,64,384]{3,2,1,0:T(8,128)(2,1)} %get-tuple-element.63), channel_id=1, source_target_pairs={{0,24},{8,0},{16,8},{24,16},{32,56},{40,32},{48,40},{56,48},{1,25}... | collective-permute-start | bytes 1179656 | tf_op jit(solution)/shard_map/ppermute | solution.py:389
  115.9 4.0 %weight_far.1 = (bf16[640,384]{1,0:T(8,128)(2,1)}, bf16[640,384]{1,0:T(8,128)(2,1)}) custom-call(s32[4]{0:T(128)} %pad_add_fusion.place, bf16[512,5120]{1,0:T(8,128)(2,1)} %all-gather.2.cloned.1.call-done.grad, bf16[512,384]{1,0:T(8,128)(2,1)} %add_convert_fusion.4.attn), custom_call_target="tpu_custom_call" | custom-call | flops 503316480 | bytes 3145728 | tf_op jit(solution)/shard_map/weight_far/pallas_call | solution.py:266
  119.9 1.8 collective-permute-start.20
  123.2 10.5 %backward_near.1 = (f32[8,2,64,384]{3,2,1,0:T(8,128)}, f32[8,2,64,384]{3,2,1,0:T(8,128)}, f32[384,1024]{1,0:T(8,128)}) custom-call(bf16[8,64,384]{2,1,0:T(8,128)(2,1)} %copy-done.9, bf16[8,64,384]{2,1,0:T(8,128)(2,1)} %collective-permute-done.3.qb, bf16[512,384]{1,0:T(8,128)(2,1)} %project.1.da, bf16[512,384]{1,0:T(8,128)(2,1)} %copy-done.4, ...), custom_call_target="tpu_custom_call" | custom-call | flops 4026531840 | bytes 9437184 | tf_op jit(solution)/shard_map/backward_near/pallas_call | solution.py:363
  136.5 1.8 collective-permute-start.18
  138.8 6.8 %backward_own.1 = (f32[8,2,64,384]{3,2,1,0:T(8,128)}, f32[8,64,384]{2,1,0:T(8,128)}, bf16[8,64,384]{2,1,0:T(8,128)(2,1)}) custom-call(bf16[8,64,384]{2,1,0:T(8,128)(2,1)} %copy-done.9, bf16[8,64,384]{2,1,0:T(8,128)(2,1)} %collective-permute-done.3.qb, bf16[512,384]{1,0:T(8,128)(2,1)} %project.1.da, bf16[512,384]{1,0:T(8,128)(2,1)} %copy-done.4, ...), custom_call_target="tpu_custom_call" | custom-call | flops 2013265920 | bytes 8388608 | tf_op jit(solution)/shard_map/backward_own/pallas_call | solution.py:376
  147.7 6.4 %weight_near.1 = (bf16[1280,384]{1,0:T(8,128)(2,1)}, bf16[1280,384]{1,0:T(8,128)(2,1)}) custom-call(s32[4]{0:T(128)} %pad_add_fusion.place, bf16[512,5120]{1,0:T(8,128)(2,1)} %all-gather.2.cloned.1.call-done.grad, bf16[512,384]{1,0:T(8,128)(2,1)} %add_convert_fusion.4.attn, bf16[640,384]{1,0:T(8,128)(2,1)} %copy-done.17, bf16[640,384]{1,0:T(8,128)(2,1)} %copy-done.18), custom_call_target="tpu_custom_call" | custom-call | flops 1006632960 | bytes 6291456 | tf_op jit(solution)/shard_map/weight_near/pallas_call | solution.py:266
  161.6 4.2 %all-to-all-start.1 = ((bf16[8,3,64,384]{3,2,1,0:T(8,128)(2,1)}), bf16[8,3,64,384]{3,2,1,0:T(8,128)(2,1)S(1)}, u32[]{:S(2)}, u32[]{:S(2)}) async-start(bf16[8,3,64,384]{3,2,1,0:T(8,128)(2,1)} %pad_maximum_fusion), calls=%async_computation.1 | async-start | bytes 2359296 | tf_op jit(solution)/shard_map/all_to_all | solution.py:410
  165.8 8.2 %collective-permute-done.22.below = bf16[1280,384]{1,0:T(8,128)(2,1)S(1)} collective-permute-done((bf16[1280,384]{1,0:T(8,128)(2,1)}, bf16[1280,384]{1,0:T(8,128)(2,1)S(1)}, u32[]{:S(2)}, u32[]{:S(2)}) %collective-permute-start.22) | collective-permute-done | bytes 983072 | tf_op jit(solution)/shard_map/ppermute | solution.py:389
  176.0 5.0 %weight_own.1 = (f32[320,384]{1,0:T(8,128)}, bf16[320,384]{1,0:T(8,128)(2,1)}, bf16[320,384]{1,0:T(8,128)(2,1)}, bf16[320,384]{1,0:T(8,128)(2,1)}) custom-call(s32[4]{0:T(128)} %pad_add_fusion.place, bf16[512,5120]{1,0:T(8,128)(2,1)} %all-gather.2.cloned.1.call-done.grad, bf16[512,384]{1,0:T(8,128)(2,1)} %add_convert_fusion.4.attn, ...), custom_call_target="tpu_custom_call" | custom-call | flops 503316480 | bytes 3145728 | tf_op jit(solution)/shard_map/weight_own/pallas_call | solution.py:266
  181.6 3.7 %collective-permute-start.25 = (bf16[320,384]{1,0:T(8,128)(2,1)}, bf16[320,384]{1,0:T(8,128)(2,1)S(1)}, u32[]{:S(2)}, u32[]{:S(2)}) collective-permute-start(bf16[320,384]{1,0:T(8,128)(2,1)} %get-tuple-element.72), channel_id=1, source_target_pairs={{0,16},{8,24},{16,0},{24,8},{32,48},{40,56},{48,32},{56,40},{1,17}... | collective-permute-start | bytes 737288 | tf_op jit(solution)/shard_map/ppermute | solution.py:389
  186.0 2.7 %collective-permute-done.24 = bf16[320,384]{1,0:T(8,128)(2,1)S(1)} collective-permute-done((bf16[320,384]{1,0:T(8,128)(2,1)}, bf16[320,384]{1,0:T(8,128)(2,1)S(1)}, u32[]{:S(2)}, u32[]{:S(2)}) %collective-permute-start.24) | collective-permute-done | bytes 245792 | tf_op jit(solution)/shard_map/ppermute | solution.py:389
  188.7 3.6 %collective-permute-done.25 = bf16[320,384]{1,0:T(8,128)(2,1)S(1)} collective-permute-done((bf16[320,384]{1,0:T(8,128)(2,1)}, bf16[320,384]{1,0:T(8,128)(2,1)S(1)}, u32[]{:S(2)}, u32[]{:S(2)}) %collective-permute-start.25) | collective-permute-done | bytes 245792 | tf_op jit(solution)/shard_map/ppermute | solution.py:389
  192.3 1.9 convert_add_fusion
  (114 shorter events, 41.1 us)
Async XLA Ops:
  7.2 70.9 %all-gather.2.cloned.1.call-start = ((), (), s32[]{:S(2)}) async-start(), calls=%async_computation.2 | async-start | bytes 5898240 | tf_op jit(solution)/shard_map/all_gather | solution.py:426
  10.5 28.4 %all-to-all-start = ((bf16[8,3,64,384]{3,2,1,0:T(8,128)(2,1)}), bf16[8,3,64,384]{3,2,1,0:T(8,128)(2,1)S(1)}, u32[]{:S(2)}, u32[]{:S(2)}) async-start(bf16[8,3,64,384]{3,2,1,0:T(8,128)(2,1)} %maximum_bitcast_fusion), calls=%async_computation | async-start | bytes 2359296 | tf_op jit(solution)/shard_map/all_to_all | solution.py:410
  15.0 10.3 %collective-permute-start.1 = (bf16[320,384]{1,0:T(8,128)(2,1)S(1)}, bf16[320,384]{1,0:T(8,128)(2,1)S(1)}, u32[]{:S(2)}, u32[]{:S(2)}) collective-permute-start(bf16[320,384]{1,0:T(8,128)(2,1)S(1)} %copy-done.5), channel_id=1, source_target_pairs={{0,16},{8,24},{16,0},{24,8},{32,48},{40,56},{48,32},{56,40},{1,17}... | collective-permute-start | bytes 737288 | tf_op jit(solution)/shard_map/ppermute | solution.py:389
  18.3 12.3 %collective-permute-start = (bf16[320,384]{1,0:T(8,128)(2,1)S(1)}, bf16[320,384]{1,0:T(8,128)(2,1)S(1)}, u32[]{:S(2)}, u32[]{:S(2)}) collective-permute-start(bf16[320,384]{1,0:T(8,128)(2,1)S(1)} %copy-done.5), channel_id=1, source_target_pairs={{0,24},{8,0},{16,8},{24,16},{32,56},{40,32},{48,40},{56,48},{1,25}... | collective-permute-start | bytes 737288 | tf_op jit(solution)/shard_map/ppermute | solution.py:389
  19.4 11.2 %collective-permute-start.2 = (bf16[320,384]{1,0:T(8,128)(2,1)S(1)}, bf16[320,384]{1,0:T(8,128)(2,1)S(1)}, u32[]{:S(2)}, u32[]{:S(2)}) collective-permute-start(bf16[320,384]{1,0:T(8,128)(2,1)S(1)} %copy-done.5), channel_id=1, source_target_pairs={{0,8},{8,16},{16,24},{24,0},{32,40},{40,48},{48,56},{56,32},{1,9},... | collective-permute-start | bytes 737288 | tf_op jit(solution)/shard_map/ppermute | solution.py:389
  30.7 26.7 %copy-start.2 = (bf16[1280,384]{1,0:T(8,128)(2,1)}, bf16[1280,384]{1,0:T(8,128)(2,1)S(1)}, u32[]{:S(2)}) copy-start(bf16[1280,384]{1,0:T(8,128)(2,1)S(1)} %stack_rows.1.w0) | copy-start | bytes 2949124
  30.7 25.8 %collective-permute-start.8 = (bf16[1280,384]{1,0:T(8,128)(2,1)S(1)}, bf16[1280,384]{1,0:T(8,128)(2,1)S(1)}, u32[]{:S(2)}, u32[]{:S(2)}) collective-permute-start(bf16[1280,384]{1,0:T(8,128)(2,1)S(1)} %stack_rows.1.w0), channel_id=1, source_target_pairs={{0,32},{8,40},{16,48},{24,56},{32,64},{40,72},{48,80},{56,88},{64,... | collective-permute-start | bytes 2949128 | tf_op jit(solution)/shard_map/ppermute | solution.py:389
  32.7 25.6 %collective-permute-start.6 = (bf16[1280,384]{1,0:T(8,128)(2,1)S(1)}, bf16[1280,384]{1,0:T(8,128)(2,1)}, u32[]{:S(2)}, u32[]{:S(2)}) collective-permute-start(bf16[1280,384]{1,0:T(8,128)(2,1)S(1)} %stack_rows.1.w0), channel_id=1, source_target_pairs={{0,96},{8,104},{16,112},{24,120},{32,0},{40,8},{48,16},{56,24},{64... | collective-permute-start | bytes 2949128 | tf_op jit(solution)/shard_map/ppermute | solution.py:389
  40.0 22.4 %collective-permute-start.5 = (bf16[8,2,64,384]{3,2,1,0:T(8,128)(2,1)}, bf16[8,2,64,384]{3,2,1,0:T(8,128)(2,1)}, u32[]{:S(2)}, u32[]{:S(2)}) collective-permute-start(bf16[8,2,64,384]{3,2,1,0:T(8,128)(2,1)} %slice.42.kv0), channel_id=1, source_target_pairs={{0,24},{8,0},{16,8},{24,16},{32,56},{40,32},{48,40},{56,48},{1,25}... | collective-permute-start | bytes 2359304 | tf_op jit(solution)/shard_map/ppermute | solution.py:389
  43.2 23.9 %collective-permute-start.4 = (bf16[8,2,64,384]{3,2,1,0:T(8,128)(2,1)}, bf16[8,2,64,384]{3,2,1,0:T(8,128)(2,1)}, u32[]{:S(2)}, u32[]{:S(2)}) collective-permute-start(bf16[8,2,64,384]{3,2,1,0:T(8,128)(2,1)} %slice.42.kv0), channel_id=1, source_target_pairs={{0,8},{8,16},{16,24},{24,0},{32,40},{40,48},{48,56},{56,32},{1,9},... | collective-permute-start | bytes 2359304 | tf_op jit(solution)/shard_map/ppermute | solution.py:389
  43.3 25.7 %copy-start.9 = (bf16[8,64,384]{2,1,0:T(8,128)(2,1)}, bf16[8,64,384]{2,1,0:T(8,128)(2,1)S(1)}, u32[]{:S(2)}) copy-start(bf16[8,64,384]{2,1,0:T(8,128)(2,1)S(1)} %slice_bitcast_fusion.3.qa) | copy-start | bytes 1179652
  43.3 25.7 %collective-permute-start.3 = (bf16[8,64,384]{2,1,0:T(8,128)(2,1)S(1)}, bf16[8,64,384]{2,1,0:T(8,128)(2,1)}, u32[]{:S(2)}, u32[]{:S(2)}) collective-permute-start(bf16[8,64,384]{2,1,0:T(8,128)(2,1)S(1)} %slice_bitcast_fusion.3.qa), channel_id=1, source_target_pairs={{0,32},{8,40},{16,48},{24,56},{32,0},{40,8},{48,16},{56,24},{1,33}... | collective-permute-start | bytes 1179656 | tf_op jit(solution)/shard_map/ppermute | solution.py:389
  57.3 20.7 %collective-permute-start.9 = (bf16[640,384]{1,0:T(8,128)(2,1)}, bf16[640,384]{1,0:T(8,128)(2,1)S(1)}, u32[]{:S(2)}, u32[]{:S(2)}) collective-permute-start(bf16[640,384]{1,0:T(8,128)(2,1)} %slice.55), channel_id=1, source_target_pairs={{0,32},{8,40},{16,48},{24,56},{32,64},{40,72},{48,80},{56,88},{64,... | collective-permute-start | bytes 1474568 | tf_op jit(solution)/shard_map/ppermute | solution.py:389
  59.3 18.7 %collective-permute-start.7 = (bf16[640,384]{1,0:T(8,128)(2,1)S(1)}, bf16[640,384]{1,0:T(8,128)(2,1)S(1)}, u32[]{:S(2)}, u32[]{:S(2)}) collective-permute-start(bf16[640,384]{1,0:T(8,128)(2,1)S(1)} %slice.54), channel_id=1, source_target_pairs={{0,96},{8,104},{16,112},{24,120},{32,0},{40,8},{48,16},{56,24},{64... | collective-permute-start | bytes 1474568 | tf_op jit(solution)/shard_map/ppermute | solution.py:389
  64.2 21.7 %collective-permute-start.12 = (bf16[4,2,64,384]{3,2,1,0:T(8,128)(2,1)}, bf16[4,2,64,384]{3,2,1,0:T(8,128)(2,1)S(1)}, u32[]{:S(2)}, u32[]{:S(2)}) collective-permute-start(bf16[4,2,64,384]{3,2,1,0:T(8,128)(2,1)} %slice.57), channel_id=1, source_target_pairs={{0,24},{8,0},{16,8},{24,16},{32,56},{40,32},{48,40},{56,48},{1,25}... | collective-permute-start | bytes 1179656 | tf_op jit(solution)/shard_map/ppermute | solution.py:389
  69.0 17.0 %collective-permute-start.11 = (bf16[4,2,64,384]{3,2,1,0:T(8,128)(2,1)}, bf16[4,2,64,384]{3,2,1,0:T(8,128)(2,1)}, u32[]{:S(2)}, u32[]{:S(2)}) collective-permute-start(bf16[4,2,64,384]{3,2,1,0:T(8,128)(2,1)} %slice.56), channel_id=1, source_target_pairs={{0,8},{8,16},{16,24},{24,0},{32,40},{40,48},{48,56},{56,32},{1,9},... | collective-permute-start | bytes 1179656 | tf_op jit(solution)/shard_map/ppermute | solution.py:389
  85.8 10.2 %collective-permute-start.10 = (bf16[512,384]{1,0:T(8,128)(2,1)}, bf16[512,384]{1,0:T(8,128)(2,1)S(1)}, u32[]{:S(2)}, u32[]{:S(2)}) collective-permute-start(bf16[512,384]{1,0:T(8,128)(2,1)} %project.1.da), channel_id=1, source_target_pairs={{0,32},{8,40},{16,48},{24,56},{32,0},{40,8},{48,16},{56,24},{1,33}... | collective-permute-start | bytes 1179656 | tf_op jit(solution)/shard_map/ppermute | solution.py:389
  99.1 4.7 %collective-permute-start.13 = (f32[3,8,1024]{2,1,0:T(8,128)S(1)}, f32[3,8,1024]{2,1,0:T(8,128)S(1)}, u32[]{:S(2)}, u32[]{:S(2)}) collective-permute-start(f32[3,8,1024]{2,1,0:T(8,128)S(1)} %row_dots.1.st_ref), channel_id=1, source_target_pairs={{0,32},{8,40},{16,48},{24,56},{32,0},{40,8},{48,16},{56,24},{1,33}... | collective-permute-start | bytes 294920 | tf_op jit(solution)/shard_map/ppermute | solution.py:389
  105.2 10.0 %collective-permute-start.14 = (bf16[512,384]{1,0:T(8,128)(2,1)S(1)}, bf16[512,384]{1,0:T(8,128)(2,1)S(1)}, u32[]{:S(2)}, u32[]{:S(2)}) collective-permute-start(bf16[512,384]{1,0:T(8,128)(2,1)S(1)} %get-tuple-element.53), channel_id=1, source_target_pairs={{0,32},{8,40},{16,48},{24,56},{32,0},{40,8},{48,16},{56,24},{1,33}... | collective-permute-start | bytes 1179656 | tf_op jit(solution)/shard_map/ppermute | solution.py:389
  111.9 26.4 %collective-permute-start.15 = (bf16[4,2,64,384]{3,2,1,0:T(8,128)(2,1)}, bf16[4,2,64,384]{3,2,1,0:T(8,128)(2,1)S(1)}, u32[]{:S(2)}, u32[]{:S(2)}) collective-permute-start(bf16[4,2,64,384]{3,2,1,0:T(8,128)(2,1)} %get-tuple-element.61), channel_id=1, source_target_pairs={{0,8},{8,16},{16,24},{24,0},{32,40},{40,48},{48,56},{56,32},{1,9},... | collective-permute-start | bytes 1179656 | tf_op jit(solution)/shard_map/ppermute | solution.py:389
  111.9 24.4 %collective-permute-start.17 = (bf16[4,2,64,384]{3,2,1,0:T(8,128)(2,1)}, bf16[4,2,64,384]{3,2,1,0:T(8,128)(2,1)S(1)}, u32[]{:S(2)}, u32[]{:S(2)}) collective-permute-start(bf16[4,2,64,384]{3,2,1,0:T(8,128)(2,1)} %get-tuple-element.63), channel_id=1, source_target_pairs={{0,24},{8,0},{16,8},{24,16},{32,56},{40,32},{48,40},{56,48},{1,25}... | collective-permute-start | bytes 1179656 | tf_op jit(solution)/shard_map/ppermute | solution.py:389
  119.9 26.2 %collective-permute-start.20 = (bf16[640,384]{1,0:T(8,128)(2,1)}, bf16[640,384]{1,0:T(8,128)(2,1)S(1)}, u32[]{:S(2)}, u32[]{:S(2)}) collective-permute-start(bf16[640,384]{1,0:T(8,128)(2,1)} %get-tuple-element.55), channel_id=1, source_target_pairs={{0,32},{8,40},{16,48},{24,56},{32,64},{40,72},{48,80},{56,88},{64,... | collective-permute-start | bytes 1474568 | tf_op jit(solution)/shard_map/ppermute | solution.py:389
  121.8 24.4 %collective-permute-start.21 = (bf16[640,384]{1,0:T(8,128)(2,1)}, bf16[640,384]{1,0:T(8,128)(2,1)S(1)}, u32[]{:S(2)}, u32[]{:S(2)}) collective-permute-start(bf16[640,384]{1,0:T(8,128)(2,1)} %get-tuple-element.56), channel_id=1, source_target_pairs={{0,96},{8,104},{16,112},{24,120},{32,0},{40,8},{48,16},{56,24},{64... | collective-permute-start | bytes 1474568 | tf_op jit(solution)/shard_map/ppermute | solution.py:389
  136.5 22.2 %collective-permute-start.18 = (bf16[8,2,64,384]{3,2,1,0:T(8,128)(2,1)S(1)}, bf16[8,2,64,384]{3,2,1,0:T(8,128)(2,1)}, u32[]{:S(2)}, u32[]{:S(2)}) collective-permute-start(bf16[8,2,64,384]{3,2,1,0:T(8,128)(2,1)S(1)} %pad_maximum_fusion.2), channel_id=1, source_target_pairs={{0,24},{8,0},{16,8},{24,16},{32,56},{40,32},{48,40},{56,48},{1,25}... | collective-permute-start | bytes 2359304 | tf_op jit(solution)/shard_map/ppermute | solution.py:389
  138.4 20.2 %collective-permute-start.16 = (bf16[8,2,64,384]{3,2,1,0:T(8,128)(2,1)S(1)}, bf16[8,2,64,384]{3,2,1,0:T(8,128)(2,1)}, u32[]{:S(2)}, u32[]{:S(2)}) collective-permute-start(bf16[8,2,64,384]{3,2,1,0:T(8,128)(2,1)S(1)} %pad_maximum_fusion.1), channel_id=1, source_target_pairs={{0,8},{8,16},{16,24},{24,0},{32,40},{40,48},{48,56},{56,32},{1,9},... | collective-permute-start | bytes 2359304 | tf_op jit(solution)/shard_map/ppermute | solution.py:389
  145.6 11.8 %collective-permute-start.19 = (bf16[8,64,384]{2,1,0:T(8,128)(2,1)}, bf16[8,64,384]{2,1,0:T(8,128)(2,1)S(1)}, u32[]{:S(2)}, u32[]{:S(2)}) collective-permute-start(bf16[8,64,384]{2,1,0:T(8,128)(2,1)} %get-tuple-element.65), channel_id=1, source_target_pairs={{0,32},{8,40},{16,48},{24,56},{32,0},{40,8},{48,16},{56,24},{1,33}... | collective-permute-start | bytes 1179656 | tf_op jit(solution)/shard_map/ppermute | solution.py:389
  154.2 19.8 %collective-permute-start.22 = (bf16[1280,384]{1,0:T(8,128)(2,1)}, bf16[1280,384]{1,0:T(8,128)(2,1)S(1)}, u32[]{:S(2)}, u32[]{:S(2)}) collective-permute-start(bf16[1280,384]{1,0:T(8,128)(2,1)} %get-tuple-element.68), channel_id=1, source_target_pairs={{0,32},{8,40},{16,48},{24,56},{32,64},{40,72},{48,80},{56,88},{64,... | collective-permute-start | bytes 2949128 | tf_op jit(solution)/shard_map/ppermute | solution.py:389
  155.7 19.0 %collective-permute-start.23 = (bf16[1280,384]{1,0:T(8,128)(2,1)}, bf16[1280,384]{1,0:T(8,128)(2,1)S(1)}, u32[]{:S(2)}, u32[]{:S(2)}) collective-permute-start(bf16[1280,384]{1,0:T(8,128)(2,1)} %get-tuple-element.69), channel_id=1, source_target_pairs={{0,96},{8,104},{16,112},{24,120},{32,0},{40,8},{48,16},{56,24},{64... | collective-permute-start | bytes 2949128 | tf_op jit(solution)/shard_map/ppermute | solution.py:389
  161.6 32.5 %all-to-all-start.1 = ((bf16[8,3,64,384]{3,2,1,0:T(8,128)(2,1)}), bf16[8,3,64,384]{3,2,1,0:T(8,128)(2,1)S(1)}, u32[]{:S(2)}, u32[]{:S(2)}) async-start(bf16[8,3,64,384]{3,2,1,0:T(8,128)(2,1)} %pad_maximum_fusion), calls=%async_computation.1 | async-start | bytes 2359296 | tf_op jit(solution)/shard_map/all_to_all | solution.py:410
  181.0 7.7 %collective-permute-start.24 = (bf16[320,384]{1,0:T(8,128)(2,1)}, bf16[320,384]{1,0:T(8,128)(2,1)S(1)}, u32[]{:S(2)}, u32[]{:S(2)}) collective-permute-start(bf16[320,384]{1,0:T(8,128)(2,1)} %get-tuple-element.71), channel_id=1, source_target_pairs={{0,8},{8,16},{16,24},{24,0},{32,40},{40,48},{48,56},{56,32},{1,9},... | collective-permute-start | bytes 737288 | tf_op jit(solution)/shard_map/ppermute | solution.py:389
  181.6 10.7 %collective-permute-start.25 = (bf16[320,384]{1,0:T(8,128)(2,1)}, bf16[320,384]{1,0:T(8,128)(2,1)S(1)}, u32[]{:S(2)}, u32[]{:S(2)}) collective-permute-start(bf16[320,384]{1,0:T(8,128)(2,1)} %get-tuple-element.72), channel_id=1, source_target_pairs={{0,16},{8,24},{16,0},{24,8},{32,48},{40,56},{48,32},{56,40},{1,17}... | collective-permute-start | bytes 737288 | tf_op jit(solution)/shard_map/ppermute | solution.py:389
  185.2 7.0 %collective-permute-start.26 = (bf16[320,384]{1,0:T(8,128)(2,1)}, bf16[320,384]{1,0:T(8,128)(2,1)S(1)}, u32[]{:S(2)}, u32[]{:S(2)}) collective-permute-start(bf16[320,384]{1,0:T(8,128)(2,1)} %get-tuple-element.73), channel_id=1, source_target_pairs={{0,24},{8,0},{16,8},{24,16},{32,56},{40,32},{48,40},{56,48},{1,25}... | collective-permute-start | bytes 737288 | tf_op jit(solution)/shard_map/ppermute | solution.py:389
  (20 other events, 61.7 us)
Sparse Core Ops, SparseCore 0:
  9.7 45.1 all-gather.1

commit v4 on v3

--- a/solution.py
+++ b/solution.py
@@ -30,10 +30,6 @@
 
 def flat(ref):
     return ref[...].reshape(ROWS, HD)
-
-
-def joined(low, high, i):
-    return jnp.concatenate([low[:, i].reshape(ROWS // 2, HD), high[:, i].reshape(ROWS // 2, HD)], axis=0)
 
 
 def forward_blocks(queries, blocks, state):
@@ -63,9 +59,9 @@
     st_ref[0, 0:1], st_ref[0, 1:2], ot_ref[...] = forward_blocks(queries, blocks, (None, None, None))
 
 
-def forward_far_kernel(qa, qb, kv3a, kv3b, ot_in, st_in, ot_ref, st_ref):
+def forward_far_kernel(qa, qb, kv3, ot_in, st_in, ot_ref, st_ref):
     queries = jnp.concatenate([flat(qa), flat(qb)], axis=0)
-    blocks = [(joined(kv3a, kv3b, 0), joined(kv3a, kv3b, 1))]
+    blocks = [(kv3[:, 0].reshape(ROWS, HD), kv3[:, 1].reshape(ROWS, HD))]
     state = (st_in[0, 0:1], st_in[0, 1:2], ot_in[...])
     st_ref[0, 0:1], st_ref[0, 1:2], ot_ref[...] = forward_blocks(queries, blocks, state)
 
@@ -107,7 +103,7 @@
 
 
 def forward_far(*operands):
-    specs = [Q_SPEC] * 2 + [HALF_SPEC] * 2 + [OT_SPEC, ST_SPEC]
+    specs = [Q_SPEC] * 2 + [KV_SPEC, OT_SPEC, ST_SPEC]
     return forward_call(forward_far_kernel, "forward_far", 1, specs, operands)
 
 
@@ -238,8 +234,9 @@
     return tn(held[...], attn[...])
 
 
-def weight_far_kernel(place, grad, attn, a_ref, b_ref, held, sem):
-    part = weight_part(place, 2, grad, attn, held, sem).astype(BF)
+def weight_far_kernel(place, grad, keep, got, a_ref, b_ref, attn_ref, held, sem):
+    attn_ref[...] = (keep[...] + got[...].astype(F32)).astype(BF)
+    part = weight_part(place, 2, grad, attn_ref, held, sem).astype(BF)
     a_ref[...] = part[: QUARTER // 2]
     b_ref[...] = part[QUARTER // 2 :]
 
@@ -254,12 +251,26 @@
     down_ref[half:] = (part[half:] + b_got[...].astype(F32)).astype(BF)
 
 
-def weight_own_kernel(place, grad, attn, below, above, o0, o1, o2, o3, held, sem, total):
-    part = weight_part(place, 0, grad, attn, held, sem)
-    total[...] = part + below[...].astype(F32) + above[...].astype(F32)
+def weight_own_kernel(place, grad, attn, out_ref, held, sem):
+    out_ref[...] = weight_part(place, 0, grad, attn, held, sem)
+
+
+def weight_sum_kernel(place, mine, below, above, o0, o1, o2, o3):
     for oy, o in enumerate((o0, o1, o2, o3)):
-        at = pl.multiple_of(lax.rem(place[3] + oy, 4) * SHARD, SHARD)
-        o[...] = total[pl.ds(at, SHARD)].astype(o.dtype)
+        rows = pl.ds(pl.multiple_of(lax.rem(place[3] + oy, 4) * SHARD, SHARD), SHARD)
+        o[...] = (mine[rows] + below[rows].astype(F32) + above[rows].astype(F32)).astype(o.dtype)
+
+
+def weight_sum(place, mine, below, above):
+    return pl.pallas_call(
+        weight_sum_kernel,
+        in_specs=[SMEM_SPEC] + [VMEM_SPEC] * 3,
+        out_specs=[VMEM_SPEC] * 4,
+        out_shape=[struct((SHARD, W), F32)] + [struct((SHARD, W), BF)] * 3,
+        compiler_params=PLAIN,
+        cost_estimate=cost(1 << 20, 5 << 20),
+        name="weight_sum",
+    )(place, mine, below, above)
 
 
 def weight_call(kernel, name, parts, outs, extra, place, grad, *more):
@@ -314,21 +325,30 @@
     high[:, i] = x[ROWS // 2 :].astype(high.dtype).reshape(U // 2, T, HD)
 
 
-def far_kernel(qa, qb, da, db, fin, kv3a, kv3b, low_ref, high_ref, dqt_ref):
+def far_kernel(qa, qb, da, db, fin, kv3, low_ref, high_ref, dqt_ref):
     common = backward_common(qa, qb, da, db, fin)
-    dk, dv, dqt = run_block(joined(kv3a, kv3b, 0), joined(kv3a, kv3b, 1), common)
+    dk, dv, dqt = run_block(kv3[:, 0].reshape(ROWS, HD), kv3[:, 1].reshape(ROWS, HD), common)
     store_halves(low_ref, high_ref, 0, dk)
     store_halves(low_ref, high_ref, 1, dv)
     dqt_ref[...] = dqt
 
 
-def near_kernel(qa, qb, da, db, fin, kv1, kv2, dqt_in, o1_ref, o2_ref, dqt_ref):
+def store_sum(o, i, x, got, first):
+    half = ROWS // 2
+    at = slice(first, first + half)
+    rest = slice(half - first, ROWS - first)
+    u, r = slice(first // T, (first + half) // T), slice((half - first) // T, (ROWS - first) // T)
+    o[u, i] = (x[at] + got[:, i].reshape(half, HD).astype(F32)).astype(BF).reshape(U // 2, T, HD)
+    o[r, i] = x[rest].astype(BF).reshape(U // 2, T, HD)
+
+
+def near_kernel(qa, qb, da, db, fin, kv1, kv2, dqt_in, low, high, o1_ref, o2_ref, dqt_ref):
     common = backward_common(qa, qb, da, db, fin)
     total = dqt_in[...]
-    for kv, o in ((kv1, o1_ref), (kv2, o2_ref)):
+    for kv, o, got, first in ((kv1, o1_ref, high, ROWS // 2), (kv2, o2_ref, low, 0)):
         dk, dv, dqt = run_block(kv[:, 0].reshape(ROWS, HD), kv[:, 1].reshape(ROWS, HD), common)
-        o[:, 0] = dk.reshape(U, T, HD)
-        o[:, 1] = dv.reshape(U, T, HD)
+        store_sum(o, 0, dk, got, first)
+        store_sum(o, 1, dv, got, first)
         total = total + dqt
     dqt_ref[...] = total
 
@@ -346,30 +366,30 @@
 COMMON_SPECS = [Q_SPEC, Q_SPEC, ROW_SPEC, ROW_SPEC, ST_SPEC]
 
 
-def backward_far(common, kv3a, kv3b):
+def backward_far(common, kv3):
     return pl.pallas_call(
         far_kernel,
         grid=(HEADS,),
-        in_specs=COMMON_SPECS + [HALF_SPEC, HALF_SPEC],
+        in_specs=COMMON_SPECS + [KV_SPEC],
         out_specs=[HALF_SPEC, HALF_SPEC, OT_SPEC],
         out_shape=[struct((U // 2, 2, T, W), BF)] * 2 + [struct((W, 2 * ROWS), F32)],
         compiler_params=PARAMS,
         cost_estimate=cost(5 * 2 * 1024 * 512 * W, 6 << 20),
         name="backward_far",
-    )(*common, kv3a, kv3b)
-
-
-def backward_near(common, kv1, kv2, dqt):
+    )(*common, kv3)
+
+
+def backward_near(common, kv1, kv2, dqt, low, high):
     return pl.pallas_call(
         near_kernel,
         grid=(HEADS,),
-        in_specs=COMMON_SPECS + [KV_SPEC, KV_SPEC, OT_SPEC],
+        in_specs=COMMON_SPECS + [KV_SPEC, KV_SPEC, OT_SPEC, HALF_SPEC, HALF_SPEC],
         out_specs=[KV_SPEC, KV_SPEC, OT_SPEC],
-        out_shape=[struct((U, 2, T, W), F32)] * 2 + [struct((W, 2 * ROWS), F32)],
+        out_shape=[struct((U, 2, T, W), BF)] * 2 + [struct((W, 2 * ROWS), F32)],
         compiler_params=PARAMS,
         cost_estimate=cost(5 * 2 * 1024 * 1024 * W, 9 << 20),
         name="backward_near",
-    )(*common, kv1, kv2, dqt)
+    )(*common, kv1, kv2, dqt, low, high)
 
 
 def backward_own(common, kv0, dqt):
@@ -426,7 +446,8 @@
     grad_block = lax.all_gather(out_grad, "uly", axis=0, tiled=True)
     shards = (out_weight, y_shift(out_weight, -1), y_shift(out_weight, 2), y_shift(out_weight, 1))
     heads = exchange(leaving)
-    weight_own = stacked_rows(*after(shards, leaving))
+    shards, place = after((shards, place), leaving)
+    weight_own = stacked_rows(*shards)
     heads = after(heads, weight_own)
     kv0, qa = heads[:, :2], heads[:, 2]
     kv_prev, kv_next = y_shift(kv0, 1), y_shift(kv0, -1)
@@ -434,48 +455,37 @@
     weight_below, weight_above = z_shift(weight_own, 1), z_shift(weight_own, -1)
     cut = QUARTER // 2
     weights = (weight_own, weight_above, z_shift(weight_above[:cut], -1), z_shift(weight_below[cut:], 1), weight_below)
-    far_low, far_high = y_shift(kv_prev[: U // 2], 1), y_shift(kv_next[U // 2 :], -1)
+    kv_far = y_shift(kv_prev, 1)
     ot, st = forward_near(qa, qb, kv0, kv_prev, kv_next)
     da = project(after(place, ot), grad_block, weights)
     db = z_swap(da)
-    ot, st = forward_far(after(qa, da), qb, far_low, far_high, ot, st)
+    ot, st = forward_far(after(qa, da), qb, kv_far, ot, st)
     st = row_dots(ot, st, da, db)
     o_keep, o_send, fin = merge(ot, st, z_swap(st))
-    attn_out = (o_keep + z_swap(o_send).astype(F32)).astype(BF)
+    o_got = z_swap(o_send)
     common = (qa, qb, da, db, fin)
 
-    low, high, dqt = backward_far(common, far_low, far_high)
+    low, high, dqt = backward_far(common, kv_far)
     low_got, high_got = y_shift(low, 1), y_shift(high, -1)
     half = struct((QUARTER // 2, W), BF)
-    a, b = weight_call(weight_far_kernel, "weight_far", 1, [half, half], [], place, grad_block, after(attn_out, dqt))
+    outs = [half, half, struct((ROWS, W), BF)]
+    a, b, attn_out = weight_call(weight_far_kernel, "weight_far", 1, outs, [], place, grad_block, after(o_keep, dqt), o_got)
     a_got, b_got = z_shift(a, 1), z_shift(b, -1)
-    g_prev, g_next, dqt = backward_near(common, kv_prev, kv_next, after(dqt, a, b))
-    low_half, high_half = slice(0, U // 2), slice(U // 2, U)
-    to_next = jnp.concatenate([g_next[low_half] + low_got.astype(F32), g_next[high_half]], axis=0)
-    to_prev = jnp.concatenate([g_prev[low_half], g_prev[high_half] + high_got.astype(F32)], axis=0)
-    from_below, from_above = y_shift(to_next.astype(BF), 1), y_shift(to_prev.astype(BF), -1)
+    to_prev, to_next, dqt = backward_near(common, kv_prev, kv_next, after(dqt, a, b), low_got, high_got)
+    from_below, from_above = y_shift(to_next, 1), y_shift(to_prev, -1)
     g_own, q_keep, q_send = backward_own(common, kv0, dqt)
     whole = struct((QUARTER, W), BF)
     up, down = weight_call(
         weight_near_kernel, "weight_near", 2, [whole, whole], [], place, grad_block, after(attn_out, q_send), a_got, b_got
     )
     below, above = z_shift(up, 1), z_shift(down, -1)
-    dq = (q_keep + z_swap(q_send).astype(F32)).astype(BF)
+    dq = (after(q_keep, up) + z_swap(q_send).astype(F32)).astype(BF)
     dkv = (g_own + from_below.astype(F32) + from_above.astype(F32)).astype(BF)
     grads = jnp.concatenate([dkv, dq[:, None]], axis=1)
     grad_key, grad_value, grad_query = to_tokens(grads)
-    o0, o1, o2, o3 = weight_call(
-        weight_own_kernel,
-        "weight_own",
-        1,
-        [struct((SHARD, W), F32)] + [struct((SHARD, W), BF)] * 3,
-        [pltpu.VMEM((QUARTER, W), F32)],
-        place,
-        grad_block,
-        after(attn_out, grads),
-        below,
-        above,
-    )
+    outs = [struct((QUARTER, W), F32)]
+    (mine,) = weight_call(weight_own_kernel, "weight_own", 1, outs, [], place, grad_block, after(attn_out, grads))
+    o0, o1, o2, o3 = weight_sum(place, mine, below, above)
     grad_weight = o0 + y_shift(o1, 1).astype(F32) + y_shift(o2, 2).astype(F32) + y_shift(o3, -1).astype(F32)
     return (grad_query, grad_key, grad_value, grad_weight)
 

time: 205 us -> 202 us (0.985)
  Pallas kernels: 62.1 us -> 65.1 us
  other arithmetic: 9.02 us -> 6.48 us
  local copies, waits for them, and re-layouts: 20.5 us -> 18.1 us
    slice x4 -> x0, local copies, waits for them, and re-layouts: 6.03 us -> none  [the longest x1 1.78 us: per_device(): kv_prev[:U // 2]]
    unnamed x48 -> x56, local copies, waits for them, and re-layouts: 8.9 us -> 14.4 us
    pallas_call x1 -> x2, Pallas kernels: 6.43 us -> 9.7 us  [the longest x1 6.36 us: backward_far(): pl.pallas_call(far_kernel, grid=(HEADS,), in_specs=COMMON_SPECS + [KV_SPE...]
    ppermute x27 -> x26, starting transfers between devices: 39.7 us -> 38.5 us  [move(): return lax.ppermute(x, axis, [(i, to(i)) for i in range(n)])]
    ppermute x27 -> x26, waiting for transfers between devices: 44.2 us -> 44.5 us  [move(): return lax.ppermute(x, axis, [(i, to(i)) for i in range(n)])]
  transfers between devices with their start and end apart: 30 -> 29, of which waited for: 10 -> 10; matrix products, arithmetic and copies ran while one was open for 10% -> 4% of each run, Pallas kernels for 30% -> 32%
where the time goes in v4:
time: 202 us; the launch traced here: 201 us
  Pallas kernels  65.1 us (32%)
  waiting for transfers between devices  50.1 us (25%)
  starting transfers between devices  47.2 us (23%)
  local copies, waits for them, and re-layouts  18.1 us (9%)
  between operations  14.4 us (7%)
  other arithmetic  6.48 us (3%)
    ppermute x26, waiting for transfers between devices, move(): return lax.ppermute(x, axis, [(i, to(i)) for i in range(n)])  44.5 us
    ppermute x26, starting transfers between devices, move(): return lax.ppermute(x, axis, [(i, to(i)) for i in range(n)])  38.5 us
    pallas_call x3, Pallas kernels, weight_call(): pl.pallas_call(kernel, in_specs=[SMEM_SPEC, ANY_SPEC] + [VMEM_SPEC] * len...  15.3 us
    pallas_call x2, Pallas kernels, forward_call(): pl.pallas_call(kernel, grid=(HEADS,), in_specs=in_specs, out_specs=[OT_SP...  14.5 us
    unnamed x56, local copies, waits for them, and re-layouts  14.4 us
    pallas_call x1, Pallas kernels, backward_near(): pl.pallas_call(near_kernel, grid=(HEADS,), in_specs=COMMON_SPECS + [KV_SP...  10.5 us
    all_to_all x2, starting transfers between devices, exchange(): return lax.all_to_all(x, 'uly', split_axis=0, concat_axis=0, tiled=True)  8.68 us
    pallas_call x1, Pallas kernels, project(): pl.pallas_call(project_kernel, in_specs=[SMEM_SPEC] + [ANY_SPEC] * 6, out...  6.83 us
  transfers between devices with their start and end apart: 29, of which 10 were waited for; matrix products, arithmetic and copies ran while one was open for 4% of the time, Pallas kernels for 32%

profile of v4, /device:TPU:0, one launch (start us, length us, event | category | flops | bytes accessed | tf_op | source)
XLA Modules:
  0.0 201.4 jit_solution(4023650957177045713)
XLA Ops:
  11.3 4.5 %all-to-all-start = ((bf16[8,3,64,384]{3,2,1,0:T(8,128)(2,1)}), bf16[8,3,64,384]{3,2,1,0:T(8,128)(2,1)S(1)}, u32[]{:S(2)}, u32[]{:S(2)}) async-start(bf16[8,3,64,384]{3,2,1,0:T(8,128)(2,1)} %maximum_bitcast_fusion), calls=%async_computation | async-start | bytes 2359296 | tf_op jit(solution)/shard_map/all_to_all | solution.py:430
  15.8 3.3 %collective-permute-start.1 = (bf16[320,384]{1,0:T(8,128)(2,1)S(1)}, bf16[320,384]{1,0:T(8,128)(2,1)S(1)}, u32[]{:S(2)}, u32[]{:S(2)}) collective-permute-start(bf16[320,384]{1,0:T(8,128)(2,1)S(1)} %copy-done.6), channel_id=1, source_target_pairs={{0,16},{8,24},{16,0},{24,8},{32,48},{40,56},{48,32},{56,40},{1,17}... | collective-permute-start | bytes 737288 | tf_op jit(solution)/shard_map/ppermute | solution.py:409
  21.6 4.5 %collective-permute-done.1.refs_2_ = bf16[320,384]{1,0:T(8,128)(2,1)S(1)} collective-permute-done((bf16[320,384]{1,0:T(8,128)(2,1)S(1)}, bf16[320,384]{1,0:T(8,128)(2,1)S(1)}, u32[]{:S(2)}, u32[]{:S(2)}) %collective-permute-start.1) | collective-permute-done | bytes 245792 | tf_op jit(solution)/shard_map/ppermute | solution.py:409
  26.1 5.2 %collective-permute-done.refs_1_ = bf16[320,384]{1,0:T(8,128)(2,1)S(1)} collective-permute-done((bf16[320,384]{1,0:T(8,128)(2,1)S(1)}, bf16[320,384]{1,0:T(8,128)(2,1)S(1)}, u32[]{:S(2)}, u32[]{:S(2)}) %collective-permute-start) | collective-permute-done | bytes 245792 | tf_op jit(solution)/shard_map/ppermute | solution.py:409
  31.4 2.0 collective-permute-start.8
  33.4 2.2 %collective-permute-start.6 = (bf16[1280,384]{1,0:T(8,128)(2,1)S(1)}, bf16[1280,384]{1,0:T(8,128)(2,1)}, u32[]{:S(2)}, u32[]{:S(2)}) collective-permute-start(bf16[1280,384]{1,0:T(8,128)(2,1)S(1)} %stack_rows.1.w0), channel_id=1, source_target_pairs={{0,96},{8,104},{16,112},{24,120},{32,0},{40,8},{48,16},{56,24},{64... | collective-permute-start | bytes 2949128 | tf_op jit(solution)/shard_map/ppermute | solution.py:409
  35.6 4.8 %all-to-all-done = bf16[8,3,64,384]{3,2,1,0:T(8,128)(2,1)S(1)} async-done(((bf16[8,3,64,384]{3,2,1,0:T(8,128)(2,1)}), bf16[8,3,64,384]{3,2,1,0:T(8,128)(2,1)S(1)}, u32[]{:S(2)}, u32[]{:S(2)}) %all-to-all-start) | async-done | bytes 1179680 | tf_op jit(solution)/shard_map/all_to_all | solution.py:430
  44.1 2.4 %collective-permute-start.3 = (bf16[8,64,384]{2,1,0:T(8,128)(2,1)S(1)}, bf16[8,64,384]{2,1,0:T(8,128)(2,1)S(1)}, u32[]{:S(2)}, u32[]{:S(2)}) collective-permute-start(bf16[8,64,384]{2,1,0:T(8,128)(2,1)S(1)} %slice_bitcast_fusion.3.qa), channel_id=1, source_target_pairs={{0,32},{8,40},{16,48},{24,56},{32,0},{40,8},{48,16},{56,24},{1,33}... | collective-permute-start | bytes 1179656 | tf_op jit(solution)/shard_map/ppermute | solution.py:409
  46.4 10.8 %collective-permute-done.8.w3 = bf16[1280,384]{1,0:T(8,128)(2,1)S(1)} collective-permute-done((bf16[1280,384]{1,0:T(8,128)(2,1)S(1)}, bf16[1280,384]{1,0:T(8,128)(2,1)S(1)}, u32[]{:S(2)}, u32[]{:S(2)}) %collective-permute-start.8) | collective-permute-done | bytes 983072 | tf_op jit(solution)/shard_map/ppermute | solution.py:409
  59.3 2.4 %collective-permute-start.7 = (bf16[640,384]{1,0:T(8,128)(2,1)S(1)}, bf16[640,384]{1,0:T(8,128)(2,1)S(1)}, u32[]{:S(2)}, u32[]{:S(2)}) collective-permute-start(bf16[640,384]{1,0:T(8,128)(2,1)S(1)} %slice.28), channel_id=1, source_target_pairs={{0,96},{8,104},{16,112},{24,120},{32,0},{40,8},{48,16},{56,24},{64... | collective-permute-start | bytes 1474568 | tf_op jit(solution)/shard_map/ppermute | solution.py:409
  63.3 3.2 %collective-permute-done.3.qb = bf16[8,64,384]{2,1,0:T(8,128)(2,1)S(1)} collective-permute-done((bf16[8,64,384]{2,1,0:T(8,128)(2,1)S(1)}, bf16[8,64,384]{2,1,0:T(8,128)(2,1)S(1)}, u32[]{:S(2)}, u32[]{:S(2)}) %collective-permute-start.3) | collective-permute-done | bytes 393248 | tf_op jit(solution)/shard_map/ppermute | solution.py:409
  67.2 9.0 %forward_near.1 = (f32[384,1024]{1,0:T(8,128)}, f32[3,8,1024]{2,1,0:T(8,128)}) custom-call(bf16[8,64,384]{2,1,0:T(8,128)(2,1)} %copy-done.10, bf16[8,64,384]{2,1,0:T(8,128)(2,1)} %copy-done.20, bf16[8,2,64,384]{3,2,1,0:T(8,128)(2,1)} %copy-done.14, bf16[8,2,64,384]{3,2,1,0:T(8,128)(2,1)} %collective-permute-done.4.kv1, ...), custom_call_target="tpu_custom_call" | custom-call | flops 2415919104 | bytes 5242880 | tf_op jit(solution)/shard_map/forward_near/pallas_call | solution.py:89
  77.1 6.8 %project.1.da = bf16[512,384]{1,0:T(8,128)(2,1)} custom-call(s32[4]{0:T(128)} %pad_add_fusion.place, bf16[512,5120]{1,0:T(8,128)(2,1)} %all-gather.2.cloned.1.call-done.grad, bf16[1280,384]{1,0:T(8,128)(2,1)} %copy-done.2, bf16[1280,384]{1,0:T(8,128)(2,1)} %collective-permute-done.6.w1, bf16[640,384]{1,0:T(8,128)(2,1)} %copy-done.17, ...), custom_call_target="tpu_custom_call" | custom-call | flops 2013265920 | bytes 10485760 | tf_op jit(solution)/shard_map/project/pallas_call | solution.py:209
  84.9 5.5 %forward_far.1 = (f32[384,1024]{1,0:T(8,128)}, f32[3,8,1024]{2,1,0:T(8,128)}) custom-call(bf16[8,64,384]{2,1,0:T(8,128)(2,1)} %copy-done.10, bf16[8,64,384]{2,1,0:T(8,128)(2,1)} %copy-done.20, bf16[8,2,64,384]{3,2,1,0:T(8,128)(2,1)} %copy-done.16, f32[384,1024]{1,0:T(8,128)} %get-tuple-element.48.ot_in, f32[3,8,1024]{2,1,0:T(8,128)} %get-tuple-element.51.st_in), custom_call_target="tpu_custom_call" | custom-call | flops 805306368 | bytes 3145728 | tf_op jit(solution)/shard_map/forward_far/pallas_call | solution.py:89
  90.4 2.9 %collective-permute-done.10.db = bf16[512,384]{1,0:T(8,128)(2,1)S(1)} collective-permute-done((bf16[512,384]{1,0:T(8,128)(2,1)}, bf16[512,384]{1,0:T(8,128)(2,1)S(1)}, u32[]{:S(2)}, u32[]{:S(2)}) %collective-permute-start.10) | collective-permute-done | bytes 393248 | tf_op jit(solution)/shard_map/ppermute | solution.py:409
  96.8 4.3 %collective-permute-done.12.pst_ref = f32[3,8,1024]{2,1,0:T(8,128)S(1)} collective-permute-done((f32[3,8,1024]{2,1,0:T(8,128)S(1)}, f32[3,8,1024]{2,1,0:T(8,128)S(1)}, u32[]{:S(2)}, u32[]{:S(2)}) %collective-permute-start.12) | collective-permute-done | bytes 98336 | tf_op jit(solution)/shard_map/ppermute | solution.py:409
  103.8 6.4 %backward_far.1 = (bf16[4,2,64,384]{3,2,1,0:T(8,128)(2,1)}, bf16[4,2,64,384]{3,2,1,0:T(8,128)(2,1)}, f32[384,1024]{1,0:T(8,128)}) custom-call(bf16[8,64,384]{2,1,0:T(8,128)(2,1)} %copy-done.10, bf16[8,64,384]{2,1,0:T(8,128)(2,1)} %copy-done.20, bf16[512,384]{1,0:T(8,128)(2,1)} %project.1.da, bf16[512,384]{1,0:T(8,128)(2,1)} %copy-done.5, ...), custom_call_target="tpu_custom_call" | custom-call | flops 2013265920 | bytes 6291456 | tf_op jit(solution)/shard_map/backward_far/pallas_call | solution.py:370
  110.1 1.9 collective-permute-start.14
  114.5 4.4 %weight_far.1 = (bf16[640,384]{1,0:T(8,128)(2,1)}, bf16[640,384]{1,0:T(8,128)(2,1)}, bf16[512,384]{1,0:T(8,128)(2,1)}) custom-call(s32[4]{0:T(128)} %pad_add_fusion.place, bf16[512,5120]{1,0:T(8,128)(2,1)} %all-gather.2.cloned.1.call-done.grad, f32[512,384]{1,0:T(8,128)} %copy-done.4, bf16[512,384]{1,0:T(8,128)(2,1)} %copy-done.21), custom_call_target="tpu_custom_call" | custom-call | flops 503316480 | bytes 3145728 | tf_op jit(solution)/shard_map/weight_far/pallas_call | solution.py:277
  120.6 1.8 collective-permute-start.19
  124.0 10.5 %backward_near.1 = (bf16[8,2,64,384]{3,2,1,0:T(8,128)(2,1)}, bf16[8,2,64,384]{3,2,1,0:T(8,128)(2,1)}, f32[384,1024]{1,0:T(8,128)}) custom-call(bf16[8,64,384]{2,1,0:T(8,128)(2,1)} %copy-done.10, bf16[8,64,384]{2,1,0:T(8,128)(2,1)} %copy-done.20, bf16[512,384]{1,0:T(8,128)(2,1)} %project.1.da, bf16[512,384]{1,0:T(8,128)(2,1)} %copy-done.5, ...), custom_call_target="tpu_custom_call" | custom-call | flops 4026531840 | bytes 9437184 | tf_op jit(solution)/shard_map/backward_near/pallas_call | solution.py:383
  134.9 2.9 %collective-permute-start.17 = (bf16[8,2,64,384]{3,2,1,0:T(8,128)(2,1)}, bf16[8,2,64,384]{3,2,1,0:T(8,128)(2,1)}, u32[]{:S(2)}, u32[]{:S(2)}) collective-permute-start(bf16[8,2,64,384]{3,2,1,0:T(8,128)(2,1)} %get-tuple-element.67), channel_id=1, source_target_pairs={{0,24},{8,0},{16,8},{24,16},{32,56},{40,32},{48,40},{56,48},{1,25}... | collective-permute-start | bytes 2359304 | tf_op jit(solution)/shard_map/ppermute | solution.py:409
  137.8 6.8 %backward_own.1 = (f32[8,2,64,384]{3,2,1,0:T(8,128)}, f32[8,64,384]{2,1,0:T(8,128)}, bf16[8,64,384]{2,1,0:T(8,128)(2,1)}) custom-call(bf16[8,64,384]{2,1,0:T(8,128)(2,1)} %copy-done.10, bf16[8,64,384]{2,1,0:T(8,128)(2,1)} %copy-done.20, bf16[512,384]{1,0:T(8,128)(2,1)} %project.1.da, bf16[512,384]{1,0:T(8,128)(2,1)} %copy-done.5, f32[3,8,1024]{2,1,0:T(8,128)} %copy-done.8, ...), custom_call_target="tpu_custom_call" | custom-call | flops 2013265920 | bytes 8388608 | tf_op jit(solution)/shard_map/backward_own/pallas_call | solution.py:396
  146.4 6.4 %weight_near.1 = (bf16[1280,384]{1,0:T(8,128)(2,1)}, bf16[1280,384]{1,0:T(8,128)(2,1)}) custom-call(s32[4]{0:T(128)} %pad_add_fusion.place, bf16[512,5120]{1,0:T(8,128)(2,1)} %all-gather.2.cloned.1.call-done.grad, bf16[512,384]{1,0:T(8,128)(2,1)} %get-tuple-element.74.attn, bf16[640,384]{1,0:T(8,128)(2,1)} %copy-done.18, bf16[640,384]{1,0:T(8,128)(2,1)} %copy-done.19), custom_call_target="tpu_custom_call" | custom-call | flops 1006632960 | bytes 6291456 | tf_op jit(solution)/shard_map/weight_near/pallas_call | solution.py:277
  152.8 1.9 collective-permute-start.21
  159.0 4.2 %all-to-all-start.1 = ((bf16[8,3,64,384]{3,2,1,0:T(8,128)(2,1)}), bf16[8,3,64,384]{3,2,1,0:T(8,128)(2,1)S(1)}, u32[]{:S(2)}, u32[]{:S(2)}) async-start(bf16[8,3,64,384]{3,2,1,0:T(8,128)(2,1)} %pad_maximum_fusion), calls=%async_computation.1 | async-start | bytes 2359296 | tf_op jit(solution)/shard_map/all_to_all | solution.py:430
  163.2 4.5 %weight_own.1.mine = f32[1280,384]{1,0:T(8,128)} custom-call(s32[4]{0:T(128)} %pad_add_fusion.place, bf16[512,5120]{1,0:T(8,128)(2,1)} %all-gather.2.cloned.1.call-done.grad, bf16[512,384]{1,0:T(8,128)(2,1)} %get-tuple-element.74.attn), custom_call_target="tpu_custom_call" | custom-call | flops 503316480 | bytes 3145728 | tf_op jit(solution)/shard_map/weight_own/pallas_call | solution.py:277
  167.7 6.0 %collective-permute-done.22.above = bf16[1280,384]{1,0:T(8,128)(2,1)S(1)} collective-permute-done((bf16[1280,384]{1,0:T(8,128)(2,1)}, bf16[1280,384]{1,0:T(8,128)(2,1)S(1)}, u32[]{:S(2)}, u32[]{:S(2)}) %collective-permute-start.22) | collective-permute-done | bytes 983072 | tf_op jit(solution)/shard_map/ppermute | solution.py:409
  175.6 3.3 %weight_sum.1 = (f32[320,384]{1,0:T(8,128)}, bf16[320,384]{1,0:T(8,128)(2,1)}, bf16[320,384]{1,0:T(8,128)(2,1)}, bf16[320,384]{1,0:T(8,128)(2,1)}) custom-call(s32[4]{0:T(128)} %pad_add_fusion.place, f32[1280,384]{1,0:T(8,128)} %weight_own.1.mine, bf16[1280,384]{1,0:T(8,128)(2,1)} %copy-done.12, bf16[1280,384]{1,0:T(8,128)(2,1)} %copy-done.13), custom_call_target="tpu_custom_call" | custom-call | flops 1048576 | bytes 5242880 | tf_op jit(solution)/shard_map/weight_sum/pallas_call | solution.py:265
  179.0 2.2 %collective-permute-start.24 = (bf16[320,384]{1,0:T(8,128)(2,1)}, bf16[320,384]{1,0:T(8,128)(2,1)S(1)}, u32[]{:S(2)}, u32[]{:S(2)}) collective-permute-start(bf16[320,384]{1,0:T(8,128)(2,1)} %get-tuple-element.78), channel_id=1, source_target_pairs={{0,16},{8,24},{16,0},{24,8},{32,48},{40,56},{48,32},{56,40},{1,17}... | collective-permute-start | bytes 737288 | tf_op jit(solution)/shard_map/ppermute | solution.py:409
  182.5 6.8 %collective-permute-done.23 = bf16[320,384]{1,0:T(8,128)(2,1)S(1)} collective-permute-done((bf16[320,384]{1,0:T(8,128)(2,1)}, bf16[320,384]{1,0:T(8,128)(2,1)S(1)}, u32[]{:S(2)}, u32[]{:S(2)}) %collective-permute-start.23) | collective-permute-done | bytes 245792 | tf_op jit(solution)/shard_map/ppermute | solution.py:409
  190.1 1.9 convert_add_fusion
  (112 shorter events, 41.4 us)
Async XLA Ops:
  7.2 69.2 %all-gather.2.cloned.1.call-start = ((), (), s32[]{:S(2)}) async-start(), calls=%async_computation.2 | async-start | bytes 5898240 | tf_op jit(solution)/shard_map/all_gather | solution.py:446
  11.3 29.2 %all-to-all-start = ((bf16[8,3,64,384]{3,2,1,0:T(8,128)(2,1)}), bf16[8,3,64,384]{3,2,1,0:T(8,128)(2,1)S(1)}, u32[]{:S(2)}, u32[]{:S(2)}) async-start(bf16[8,3,64,384]{3,2,1,0:T(8,128)(2,1)} %maximum_bitcast_fusion), calls=%async_computation | async-start | bytes 2359296 | tf_op jit(solution)/shard_map/all_to_all | solution.py:430
  15.8 10.3 %collective-permute-start.1 = (bf16[320,384]{1,0:T(8,128)(2,1)S(1)}, bf16[320,384]{1,0:T(8,128)(2,1)S(1)}, u32[]{:S(2)}, u32[]{:S(2)}) collective-permute-start(bf16[320,384]{1,0:T(8,128)(2,1)S(1)} %copy-done.6), channel_id=1, source_target_pairs={{0,16},{8,24},{16,0},{24,8},{32,48},{40,56},{48,32},{56,40},{1,17}... | collective-permute-start | bytes 737288 | tf_op jit(solution)/shard_map/ppermute | solution.py:409
  19.0 12.3 %collective-permute-start = (bf16[320,384]{1,0:T(8,128)(2,1)S(1)}, bf16[320,384]{1,0:T(8,128)(2,1)S(1)}, u32[]{:S(2)}, u32[]{:S(2)}) collective-permute-start(bf16[320,384]{1,0:T(8,128)(2,1)S(1)} %copy-done.6), channel_id=1, source_target_pairs={{0,24},{8,0},{16,8},{24,16},{32,56},{40,32},{48,40},{56,48},{1,25}... | collective-permute-start | bytes 737288 | tf_op jit(solution)/shard_map/ppermute | solution.py:409
  20.1 11.2 %collective-permute-start.2 = (bf16[320,384]{1,0:T(8,128)(2,1)S(1)}, bf16[320,384]{1,0:T(8,128)(2,1)S(1)}, u32[]{:S(2)}, u32[]{:S(2)}) collective-permute-start(bf16[320,384]{1,0:T(8,128)(2,1)S(1)} %copy-done.6), channel_id=1, source_target_pairs={{0,8},{8,16},{16,24},{24,0},{32,40},{40,48},{48,56},{56,32},{1,9},... | collective-permute-start | bytes 737288 | tf_op jit(solution)/shard_map/ppermute | solution.py:409
  31.4 25.8 %collective-permute-start.8 = (bf16[1280,384]{1,0:T(8,128)(2,1)S(1)}, bf16[1280,384]{1,0:T(8,128)(2,1)S(1)}, u32[]{:S(2)}, u32[]{:S(2)}) collective-permute-start(bf16[1280,384]{1,0:T(8,128)(2,1)S(1)} %stack_rows.1.w0), channel_id=1, source_target_pairs={{0,32},{8,40},{16,48},{24,56},{32,64},{40,72},{48,80},{56,88},{64,... | collective-permute-start | bytes 2949128 | tf_op jit(solution)/shard_map/ppermute | solution.py:409
  33.4 24.8 %collective-permute-start.6 = (bf16[1280,384]{1,0:T(8,128)(2,1)S(1)}, bf16[1280,384]{1,0:T(8,128)(2,1)}, u32[]{:S(2)}, u32[]{:S(2)}) collective-permute-start(bf16[1280,384]{1,0:T(8,128)(2,1)S(1)} %stack_rows.1.w0), channel_id=1, source_target_pairs={{0,96},{8,104},{16,112},{24,120},{32,0},{40,8},{48,16},{56,24},{64... | collective-permute-start | bytes 2949128 | tf_op jit(solution)/shard_map/ppermute | solution.py:409
  40.5 18.7 %copy-start.14 = (bf16[8,2,64,384]{3,2,1,0:T(8,128)(2,1)}, bf16[8,2,64,384]{3,2,1,0:T(8,128)(2,1)S(1)}, u32[]{:S(2)}) copy-start(bf16[8,2,64,384]{3,2,1,0:T(8,128)(2,1)S(1)} %slice.22.kv0) | copy-start | bytes 2359300
  40.5 21.2 %collective-permute-start.4 = (bf16[8,2,64,384]{3,2,1,0:T(8,128)(2,1)S(1)}, bf16[8,2,64,384]{3,2,1,0:T(8,128)(2,1)}, u32[]{:S(2)}, u32[]{:S(2)}) collective-permute-start(bf16[8,2,64,384]{3,2,1,0:T(8,128)(2,1)S(1)} %slice.22.kv0), channel_id=1, source_target_pairs={{0,8},{8,16},{16,24},{24,0},{32,40},{40,48},{48,56},{56,32},{1,9},... | collective-permute-start | bytes 2359304 | tf_op jit(solution)/shard_map/ppermute | solution.py:409
  42.3 25.0 %collective-permute-start.5 = (bf16[8,2,64,384]{3,2,1,0:T(8,128)(2,1)S(1)}, bf16[8,2,64,384]{3,2,1,0:T(8,128)(2,1)}, u32[]{:S(2)}, u32[]{:S(2)}) collective-permute-start(bf16[8,2,64,384]{3,2,1,0:T(8,128)(2,1)S(1)} %slice.22.kv0), channel_id=1, source_target_pairs={{0,24},{8,0},{16,8},{24,16},{32,56},{40,32},{48,40},{56,48},{1,25}... | collective-permute-start | bytes 2359304 | tf_op jit(solution)/shard_map/ppermute | solution.py:409
  44.0 23.2 %copy-start.10 = (bf16[8,64,384]{2,1,0:T(8,128)(2,1)}, bf16[8,64,384]{2,1,0:T(8,128)(2,1)S(1)}, u32[]{:S(2)}) copy-start(bf16[8,64,384]{2,1,0:T(8,128)(2,1)S(1)} %slice_bitcast_fusion.3.qa) | copy-start | bytes 1179652
  44.1 22.4 %collective-permute-start.3 = (bf16[8,64,384]{2,1,0:T(8,128)(2,1)S(1)}, bf16[8,64,384]{2,1,0:T(8,128)(2,1)S(1)}, u32[]{:S(2)}, u32[]{:S(2)}) collective-permute-start(bf16[8,64,384]{2,1,0:T(8,128)(2,1)S(1)} %slice_bitcast_fusion.3.qa), channel_id=1, source_target_pairs={{0,32},{8,40},{16,48},{24,56},{32,0},{40,8},{48,16},{56,24},{1,33}... | collective-permute-start | bytes 1179656 | tf_op jit(solution)/shard_map/ppermute | solution.py:409
  57.2 19.1 %copy-start.9 = (bf16[1280,384]{1,0:T(8,128)(2,1)}, bf16[1280,384]{1,0:T(8,128)(2,1)S(1)}, u32[]{:S(2)}) copy-start(bf16[1280,384]{1,0:T(8,128)(2,1)S(1)} %collective-permute-done.8.w3) | copy-start | bytes 2949124
  57.2 19.0 %collective-permute-start.9 = (bf16[640,384]{1,0:T(8,128)(2,1)S(1)}, bf16[640,384]{1,0:T(8,128)(2,1)}, u32[]{:S(2)}, u32[]{:S(2)}) collective-permute-start(bf16[640,384]{1,0:T(8,128)(2,1)S(1)} %slice.29), channel_id=1, source_target_pairs={{0,32},{8,40},{16,48},{24,56},{32,64},{40,72},{48,80},{56,88},{64,... | collective-permute-start | bytes 1474568 | tf_op jit(solution)/shard_map/ppermute | solution.py:409
  59.3 17.0 %collective-permute-start.7 = (bf16[640,384]{1,0:T(8,128)(2,1)S(1)}, bf16[640,384]{1,0:T(8,128)(2,1)S(1)}, u32[]{:S(2)}, u32[]{:S(2)}) collective-permute-start(bf16[640,384]{1,0:T(8,128)(2,1)S(1)} %slice.28), channel_id=1, source_target_pairs={{0,96},{8,104},{16,112},{24,120},{32,0},{40,8},{48,16},{56,24},{64... | collective-permute-start | bytes 1474568 | tf_op jit(solution)/shard_map/ppermute | solution.py:409
  61.7 22.3 %collective-permute-start.11 = (bf16[8,2,64,384]{3,2,1,0:T(8,128)(2,1)}, bf16[8,2,64,384]{3,2,1,0:T(8,128)(2,1)S(1)}, u32[]{:S(2)}, u32[]{:S(2)}) collective-permute-start(bf16[8,2,64,384]{3,2,1,0:T(8,128)(2,1)} %collective-permute-done.4.kv1), channel_id=1, source_target_pairs={{0,8},{8,16},{16,24},{24,0},{32,40},{40,48},{48,56},{56,32},{1,9},... | collective-permute-start | bytes 2359304 | tf_op jit(solution)/shard_map/ppermute | solution.py:409
  83.9 9.4 %collective-permute-start.10 = (bf16[512,384]{1,0:T(8,128)(2,1)}, bf16[512,384]{1,0:T(8,128)(2,1)S(1)}, u32[]{:S(2)}, u32[]{:S(2)}) collective-permute-start(bf16[512,384]{1,0:T(8,128)(2,1)} %project.1.da), channel_id=1, source_target_pairs={{0,32},{8,40},{16,48},{24,56},{32,0},{40,8},{48,16},{56,24},{1,33}... | collective-permute-start | bytes 1179656 | tf_op jit(solution)/shard_map/ppermute | solution.py:409
  96.4 4.7 %collective-permute-start.12 = (f32[3,8,1024]{2,1,0:T(8,128)S(1)}, f32[3,8,1024]{2,1,0:T(8,128)S(1)}, u32[]{:S(2)}, u32[]{:S(2)}) collective-permute-start(f32[3,8,1024]{2,1,0:T(8,128)S(1)} %row_dots.1.st_ref), channel_id=1, source_target_pairs={{0,32},{8,40},{16,48},{24,56},{32,0},{40,8},{48,16},{56,24},{1,33}... | collective-permute-start | bytes 294920 | tf_op jit(solution)/shard_map/ppermute | solution.py:409
  103.4 10.2 %collective-permute-start.13 = (bf16[512,384]{1,0:T(8,128)(2,1)S(1)}, bf16[512,384]{1,0:T(8,128)(2,1)S(1)}, u32[]{:S(2)}, u32[]{:S(2)}) collective-permute-start(bf16[512,384]{1,0:T(8,128)(2,1)S(1)} %get-tuple-element.58), channel_id=1, source_target_pairs={{0,32},{8,40},{16,48},{24,56},{32,0},{40,8},{48,16},{56,24},{1,33}... | collective-permute-start | bytes 1179656 | tf_op jit(solution)/shard_map/ppermute | solution.py:409
  110.1 12.3 %collective-permute-start.14 = (bf16[4,2,64,384]{3,2,1,0:T(8,128)(2,1)}, bf16[4,2,64,384]{3,2,1,0:T(8,128)(2,1)S(1)}, u32[]{:S(2)}, u32[]{:S(2)}) collective-permute-start(bf16[4,2,64,384]{3,2,1,0:T(8,128)(2,1)} %get-tuple-element.62), channel_id=1, source_target_pairs={{0,8},{8,16},{16,24},{24,0},{32,40},{40,48},{48,56},{56,32},{1,9},... | collective-permute-start | bytes 1179656 | tf_op jit(solution)/shard_map/ppermute | solution.py:409
  112.0 10.4 %collective-permute-start.15 = (bf16[4,2,64,384]{3,2,1,0:T(8,128)(2,1)}, bf16[4,2,64,384]{3,2,1,0:T(8,128)(2,1)S(1)}, u32[]{:S(2)}, u32[]{:S(2)}) collective-permute-start(bf16[4,2,64,384]{3,2,1,0:T(8,128)(2,1)} %get-tuple-element.63), channel_id=1, source_target_pairs={{0,24},{8,0},{16,8},{24,16},{32,56},{40,32},{48,40},{56,48},{1,25}... | collective-permute-start | bytes 1179656 | tf_op jit(solution)/shard_map/ppermute | solution.py:409
  118.8 26.0 %collective-permute-start.18 = (bf16[640,384]{1,0:T(8,128)(2,1)}, bf16[640,384]{1,0:T(8,128)(2,1)S(1)}, u32[]{:S(2)}, u32[]{:S(2)}) collective-permute-start(bf16[640,384]{1,0:T(8,128)(2,1)} %get-tuple-element.59), channel_id=1, source_target_pairs={{0,32},{8,40},{16,48},{24,56},{32,64},{40,72},{48,80},{56,88},{64,... | collective-permute-start | bytes 1474568 | tf_op jit(solution)/shard_map/ppermute | solution.py:409
  120.6 24.2 %collective-permute-start.19 = (bf16[640,384]{1,0:T(8,128)(2,1)}, bf16[640,384]{1,0:T(8,128)(2,1)S(1)}, u32[]{:S(2)}, u32[]{:S(2)}) collective-permute-start(bf16[640,384]{1,0:T(8,128)(2,1)} %get-tuple-element.60), channel_id=1, source_target_pairs={{0,96},{8,104},{16,112},{24,120},{32,0},{40,8},{48,16},{56,24},{64... | collective-permute-start | bytes 1474568 | tf_op jit(solution)/shard_map/ppermute | solution.py:409
  134.5 21.7 %collective-permute-start.16 = (bf16[8,2,64,384]{3,2,1,0:T(8,128)(2,1)}, bf16[8,2,64,384]{3,2,1,0:T(8,128)(2,1)S(1)}, u32[]{:S(2)}, u32[]{:S(2)}) collective-permute-start(bf16[8,2,64,384]{3,2,1,0:T(8,128)(2,1)} %get-tuple-element.66), channel_id=1, source_target_pairs={{0,8},{8,16},{16,24},{24,0},{32,40},{40,48},{48,56},{56,32},{1,9},... | collective-permute-start | bytes 2359304 | tf_op jit(solution)/shard_map/ppermute | solution.py:409
  134.9 21.3 %collective-permute-start.17 = (bf16[8,2,64,384]{3,2,1,0:T(8,128)(2,1)}, bf16[8,2,64,384]{3,2,1,0:T(8,128)(2,1)}, u32[]{:S(2)}, u32[]{:S(2)}) collective-permute-start(bf16[8,2,64,384]{3,2,1,0:T(8,128)(2,1)} %get-tuple-element.67), channel_id=1, source_target_pairs={{0,24},{8,0},{16,8},{24,16},{32,56},{40,32},{48,40},{56,48},{1,25}... | collective-permute-start | bytes 2359304 | tf_op jit(solution)/shard_map/ppermute | solution.py:409
  144.6 11.5 %collective-permute-start.20 = (bf16[8,64,384]{2,1,0:T(8,128)(2,1)}, bf16[8,64,384]{2,1,0:T(8,128)(2,1)S(1)}, u32[]{:S(2)}, u32[]{:S(2)}) collective-permute-start(bf16[8,64,384]{2,1,0:T(8,128)(2,1)} %get-tuple-element.70), channel_id=1, source_target_pairs={{0,32},{8,40},{16,48},{24,56},{32,0},{40,8},{48,16},{56,24},{1,33}... | collective-permute-start | bytes 1179656 | tf_op jit(solution)/shard_map/ppermute | solution.py:409
  152.8 20.9 %collective-permute-start.21 = (bf16[1280,384]{1,0:T(8,128)(2,1)}, bf16[1280,384]{1,0:T(8,128)(2,1)S(1)}, u32[]{:S(2)}, u32[]{:S(2)}) collective-permute-start(bf16[1280,384]{1,0:T(8,128)(2,1)} %get-tuple-element.72), channel_id=1, source_target_pairs={{0,32},{8,40},{16,48},{24,56},{32,64},{40,72},{48,80},{56,88},{64,... | collective-permute-start | bytes 2949128 | tf_op jit(solution)/shard_map/ppermute | solution.py:409
  154.7 18.9 %collective-permute-start.22 = (bf16[1280,384]{1,0:T(8,128)(2,1)}, bf16[1280,384]{1,0:T(8,128)(2,1)S(1)}, u32[]{:S(2)}, u32[]{:S(2)}) collective-permute-start(bf16[1280,384]{1,0:T(8,128)(2,1)} %get-tuple-element.75), channel_id=1, source_target_pairs={{0,96},{8,104},{16,112},{24,120},{32,0},{40,8},{48,16},{56,24},{64... | collective-permute-start | bytes 2949128 | tf_op jit(solution)/shard_map/ppermute | solution.py:409
  159.0 33.0 %all-to-all-start.1 = ((bf16[8,3,64,384]{3,2,1,0:T(8,128)(2,1)}), bf16[8,3,64,384]{3,2,1,0:T(8,128)(2,1)S(1)}, u32[]{:S(2)}, u32[]{:S(2)}) async-start(bf16[8,3,64,384]{3,2,1,0:T(8,128)(2,1)} %pad_maximum_fusion), calls=%async_computation.1 | async-start | bytes 2359296 | tf_op jit(solution)/shard_map/all_to_all | solution.py:430
  179.0 10.3 %collective-permute-start.23 = (bf16[320,384]{1,0:T(8,128)(2,1)}, bf16[320,384]{1,0:T(8,128)(2,1)S(1)}, u32[]{:S(2)}, u32[]{:S(2)}) collective-permute-start(bf16[320,384]{1,0:T(8,128)(2,1)} %get-tuple-element.77), channel_id=1, source_target_pairs={{0,8},{8,16},{16,24},{24,0},{32,40},{40,48},{48,56},{56,32},{1,9},... | collective-permute-start | bytes 737288 | tf_op jit(solution)/shard_map/ppermute | solution.py:409
  179.0 10.3 %collective-permute-start.24 = (bf16[320,384]{1,0:T(8,128)(2,1)}, bf16[320,384]{1,0:T(8,128)(2,1)S(1)}, u32[]{:S(2)}, u32[]{:S(2)}) collective-permute-start(bf16[320,384]{1,0:T(8,128)(2,1)} %get-tuple-element.78), channel_id=1, source_target_pairs={{0,16},{8,24},{16,0},{24,8},{32,48},{40,56},{48,32},{56,40},{1,17}... | collective-permute-start | bytes 737288 | tf_op jit(solution)/shard_map/ppermute | solution.py:409
  181.2 9.0 %collective-permute-start.25 = (bf16[320,384]{1,0:T(8,128)(2,1)}, bf16[320,384]{1,0:T(8,128)(2,1)S(1)}, u32[]{:S(2)}, u32[]{:S(2)}) collective-permute-start(bf16[320,384]{1,0:T(8,128)(2,1)} %get-tuple-element.79), channel_id=1, source_target_pairs={{0,24},{8,0},{16,8},{24,16},{32,56},{40,32},{48,40},{56,48},{1,25}... | collective-permute-start | bytes 737288 | tf_op jit(solution)/shard_map/ppermute | solution.py:409
  (23 other events, 64.0 us)
Sparse Core Ops, SparseCore 0:
  9.7 45.8 all-gather.1

commit v5 on v4

--- a/solution.py
+++ b/solution.py
@@ -234,9 +234,8 @@
     return tn(held[...], attn[...])
 
 
-def weight_far_kernel(place, grad, keep, got, a_ref, b_ref, attn_ref, held, sem):
-    attn_ref[...] = (keep[...] + got[...].astype(F32)).astype(BF)
-    part = weight_part(place, 2, grad, attn_ref, held, sem).astype(BF)
+def weight_far_kernel(place, grad, attn, a_ref, b_ref, held, sem):
+    part = weight_part(place, 2, grad, attn, held, sem).astype(BF)
     a_ref[...] = part[: QUARTER // 2]
     b_ref[...] = part[QUARTER // 2 :]
 
@@ -462,14 +461,13 @@
     ot, st = forward_far(after(qa, da), qb, kv_far, ot, st)
     st = row_dots(ot, st, da, db)
     o_keep, o_send, fin = merge(ot, st, z_swap(st))
-    o_got = z_swap(o_send)
+    attn_out = (o_keep + z_swap(o_send).astype(F32)).astype(BF)
     common = (qa, qb, da, db, fin)
 
     low, high, dqt = backward_far(common, kv_far)
     low_got, high_got = y_shift(low, 1), y_shift(high, -1)
     half = struct((QUARTER // 2, W), BF)
-    outs = [half, half, struct((ROWS, W), BF)]
-    a, b, attn_out = weight_call(weight_far_kernel, "weight_far", 1, outs, [], place, grad_block, after(o_keep, dqt), o_got)
+    a, b = weight_call(weight_far_kernel, "weight_far", 1, [half, half], [], place, grad_block, after(attn_out, dqt))
     a_got, b_got = z_shift(a, 1), z_shift(b, -1)
     to_prev, to_next, dqt = backward_near(common, kv_prev, kv_next, after(dqt, a, b), low_got, high_got)
     from_below, from_above = y_shift(to_next, 1), y_shift(to_prev, -1)

time: 202 us -> 201 us (level)
    unnamed x56 -> x54, local copies, waits for them, and re-layouts: 14.4 us -> 12.7 us
  transfers between devices with their start and end apart: 29 -> 29, of which waited for: 10 -> 10; matrix products, arithmetic and copies ran while one was open for 4% -> 5% of each run, Pallas kernels for 32% -> 32%
where the time goes in v5:
time: 201 us
  Pallas kernels  64.9 us (32%)
  waiting for transfers between devices  49.6 us (25%)
  starting transfers between devices  47 us (23%)
  local copies, waits for them, and re-layouts  17.3 us (9%)
  between operations  14.4 us (7%)
  other arithmetic  7.37 us (4%)
    ppermute x26, waiting for transfers between devices, move(): return lax.ppermute(x, axis, [(i, to(i)) for i in range(n)])  44.1 us
    ppermute x26, starting transfers between devices, move(): return lax.ppermute(x, axis, [(i, to(i)) for i in range(n)])  38.1 us
    pallas_call x3, Pallas kernels, weight_call(): pl.pallas_call(kernel, in_specs=[SMEM_SPEC, ANY_SPEC] + [VMEM_SPEC] * len...  14.9 us
    pallas_call x2, Pallas kernels, forward_call(): pl.pallas_call(kernel, grid=(HEADS,), in_specs=in_specs, out_specs=[OT_SP...  14.6 us
    unnamed x54, local copies, waits for them, and re-layouts  12.7 us
    pallas_call x1, Pallas kernels, backward_near(): pl.pallas_call(near_kernel, grid=(HEADS,), in_specs=COMMON_SPECS + [KV_SP...  10.5 us
    all_to_all x2, starting transfers between devices, exchange(): return lax.all_to_all(x, 'uly', split_axis=0, concat_axis=0, tiled=True)  8.87 us
    pallas_call x1, Pallas kernels, project(): pl.pallas_call(project_kernel, in_specs=[SMEM_SPEC] + [ANY_SPEC] * 6, out...  6.96 us
  transfers between devices with their start and end apart: 29, of which 10 were waited for; matrix products, arithmetic and copies ran while one was open for 5% of the time, Pallas kernels for 32%

profile of v5, /device:TPU:0, one launch (start us, length us, event | category | flops | bytes accessed | tf_op | source)
XLA Modules:
  0.0 200.6 jit_solution(13779758768366352237)
XLA Ops:
  11.3 4.5 %all-to-all-start = ((bf16[8,3,64,384]{3,2,1,0:T(8,128)(2,1)}), bf16[8,3,64,384]{3,2,1,0:T(8,128)(2,1)S(1)}, u32[]{:S(2)}, u32[]{:S(2)}) async-start(bf16[8,3,64,384]{3,2,1,0:T(8,128)(2,1)} %maximum_bitcast_fusion), calls=%async_computation | async-start | bytes 2359296 | tf_op jit(solution)/shard_map/all_to_all | solution.py:429
  15.8 3.3 %collective-permute-start.1 = (bf16[320,384]{1,0:T(8,128)(2,1)S(1)}, bf16[320,384]{1,0:T(8,128)(2,1)S(1)}, u32[]{:S(2)}, u32[]{:S(2)}) collective-permute-start(bf16[320,384]{1,0:T(8,128)(2,1)S(1)} %copy-done.5), channel_id=1, source_target_pairs={{0,16},{8,24},{16,0},{24,8},{32,48},{40,56},{48,32},{56,40},{1,17}... | collective-permute-start | bytes 737288 | tf_op jit(solution)/shard_map/ppermute | solution.py:408
  21.7 4.4 %collective-permute-done.1.refs_2_ = bf16[320,384]{1,0:T(8,128)(2,1)S(1)} collective-permute-done((bf16[320,384]{1,0:T(8,128)(2,1)S(1)}, bf16[320,384]{1,0:T(8,128)(2,1)S(1)}, u32[]{:S(2)}, u32[]{:S(2)}) %collective-permute-start.1) | collective-permute-done | bytes 245792 | tf_op jit(solution)/shard_map/ppermute | solution.py:408
  26.1 5.2 %collective-permute-done.refs_1_ = bf16[320,384]{1,0:T(8,128)(2,1)S(1)} collective-permute-done((bf16[320,384]{1,0:T(8,128)(2,1)S(1)}, bf16[320,384]{1,0:T(8,128)(2,1)S(1)}, u32[]{:S(2)}, u32[]{:S(2)}) %collective-permute-start) | collective-permute-done | bytes 245792 | tf_op jit(solution)/shard_map/ppermute | solution.py:408
  31.4 2.0 collective-permute-start.8
  33.4 2.2 %collective-permute-start.6 = (bf16[1280,384]{1,0:T(8,128)(2,1)S(1)}, bf16[1280,384]{1,0:T(8,128)(2,1)}, u32[]{:S(2)}, u32[]{:S(2)}) collective-permute-start(bf16[1280,384]{1,0:T(8,128)(2,1)S(1)} %stack_rows.1.w0), channel_id=1, source_target_pairs={{0,96},{8,104},{16,112},{24,120},{32,0},{40,8},{48,16},{56,24},{64... | collective-permute-start | bytes 2949128 | tf_op jit(solution)/shard_map/ppermute | solution.py:408
  35.6 4.9 %all-to-all-done = bf16[8,3,64,384]{3,2,1,0:T(8,128)(2,1)S(1)} async-done(((bf16[8,3,64,384]{3,2,1,0:T(8,128)(2,1)}), bf16[8,3,64,384]{3,2,1,0:T(8,128)(2,1)S(1)}, u32[]{:S(2)}, u32[]{:S(2)}) %all-to-all-start) | async-done | bytes 1179680 | tf_op jit(solution)/shard_map/all_to_all | solution.py:429
  44.1 2.4 %collective-permute-start.3 = (bf16[8,64,384]{2,1,0:T(8,128)(2,1)S(1)}, bf16[8,64,384]{2,1,0:T(8,128)(2,1)S(1)}, u32[]{:S(2)}, u32[]{:S(2)}) collective-permute-start(bf16[8,64,384]{2,1,0:T(8,128)(2,1)S(1)} %slice_bitcast_fusion.3.qa), channel_id=1, source_target_pairs={{0,32},{8,40},{16,48},{24,56},{32,0},{40,8},{48,16},{56,24},{1,33}... | collective-permute-start | bytes 1179656 | tf_op jit(solution)/shard_map/ppermute | solution.py:408
  46.4 10.8 %collective-permute-done.8.w3 = bf16[1280,384]{1,0:T(8,128)(2,1)S(1)} collective-permute-done((bf16[1280,384]{1,0:T(8,128)(2,1)S(1)}, bf16[1280,384]{1,0:T(8,128)(2,1)S(1)}, u32[]{:S(2)}, u32[]{:S(2)}) %collective-permute-start.8) | collective-permute-done | bytes 983072 | tf_op jit(solution)/shard_map/ppermute | solution.py:408
  58.2 1.9 slice.28
  60.0 2.4 %collective-permute-start.7 = (bf16[640,384]{1,0:T(8,128)(2,1)}, bf16[640,384]{1,0:T(8,128)(2,1)S(1)}, u32[]{:S(2)}, u32[]{:S(2)}) collective-permute-start(bf16[640,384]{1,0:T(8,128)(2,1)} %slice.28), channel_id=1, source_target_pairs={{0,96},{8,104},{16,112},{24,120},{32,0},{40,8},{48,16},{56,24},{64... | collective-permute-start | bytes 1474568 | tf_op jit(solution)/shard_map/ppermute | solution.py:408
  64.0 2.5 %collective-permute-done.3.qb = bf16[8,64,384]{2,1,0:T(8,128)(2,1)S(1)} collective-permute-done((bf16[8,64,384]{2,1,0:T(8,128)(2,1)S(1)}, bf16[8,64,384]{2,1,0:T(8,128)(2,1)S(1)}, u32[]{:S(2)}, u32[]{:S(2)}) %collective-permute-start.3) | collective-permute-done | bytes 393248 | tf_op jit(solution)/shard_map/ppermute | solution.py:408
  67.3 9.0 %forward_near.1 = (f32[384,1024]{1,0:T(8,128)}, f32[3,8,1024]{2,1,0:T(8,128)}) custom-call(bf16[8,64,384]{2,1,0:T(8,128)(2,1)} %copy-done.9, bf16[8,64,384]{2,1,0:T(8,128)(2,1)} %copy-done.20, bf16[8,2,64,384]{3,2,1,0:T(8,128)(2,1)} %copy-done.13, bf16[8,2,64,384]{3,2,1,0:T(8,128)(2,1)} %collective-permute-done.4.kv1, ...), custom_call_target="tpu_custom_call" | custom-call | flops 2415919104 | bytes 5242880 | tf_op jit(solution)/shard_map/forward_near/pallas_call | solution.py:89
  77.2 7.0 %project.1.da = bf16[512,384]{1,0:T(8,128)(2,1)} custom-call(s32[4]{0:T(128)} %pad_add_fusion.place, bf16[512,5120]{1,0:T(8,128)(2,1)} %all-gather.2.cloned.1.call-done.grad, bf16[1280,384]{1,0:T(8,128)(2,1)} %copy-done.2, bf16[1280,384]{1,0:T(8,128)(2,1)} %collective-permute-done.6.w1, bf16[640,384]{1,0:T(8,128)(2,1)} %copy-done.17, ...), custom_call_target="tpu_custom_call" | custom-call | flops 2013265920 | bytes 10485760 | tf_op jit(solution)/shard_map/project/pallas_call | solution.py:209
  85.2 5.5 %forward_far.1 = (f32[384,1024]{1,0:T(8,128)}, f32[3,8,1024]{2,1,0:T(8,128)}) custom-call(bf16[8,64,384]{2,1,0:T(8,128)(2,1)} %copy-done.9, bf16[8,64,384]{2,1,0:T(8,128)(2,1)} %copy-done.20, bf16[8,2,64,384]{3,2,1,0:T(8,128)(2,1)} %copy-done.15, f32[384,1024]{1,0:T(8,128)} %get-tuple-element.47.ot_in, f32[3,8,1024]{2,1,0:T(8,128)} %get-tuple-element.50.st_in), custom_call_target="tpu_custom_call" | custom-call | flops 805306368 | bytes 3145728 | tf_op jit(solution)/shard_map/forward_far/pallas_call | solution.py:89
  90.7 2.7 %collective-permute-done.10.db = bf16[512,384]{1,0:T(8,128)(2,1)S(1)} collective-permute-done((bf16[512,384]{1,0:T(8,128)(2,1)}, bf16[512,384]{1,0:T(8,128)(2,1)S(1)}, u32[]{:S(2)}, u32[]{:S(2)}) %collective-permute-start.10) | collective-permute-done | bytes 393248 | tf_op jit(solution)/shard_map/ppermute | solution.py:408
  96.9 4.5 %collective-permute-done.12.pst_ref = f32[3,8,1024]{2,1,0:T(8,128)S(1)} collective-permute-done((f32[3,8,1024]{2,1,0:T(8,128)S(1)}, f32[3,8,1024]{2,1,0:T(8,128)S(1)}, u32[]{:S(2)}, u32[]{:S(2)}) %collective-permute-start.12) | collective-permute-done | bytes 98336 | tf_op jit(solution)/shard_map/ppermute | solution.py:408
  102.9 6.4 %backward_far.1 = (bf16[4,2,64,384]{3,2,1,0:T(8,128)(2,1)}, bf16[4,2,64,384]{3,2,1,0:T(8,128)(2,1)}, f32[384,1024]{1,0:T(8,128)}) custom-call(bf16[8,64,384]{2,1,0:T(8,128)(2,1)} %copy-done.9, bf16[8,64,384]{2,1,0:T(8,128)(2,1)} %copy-done.20, bf16[512,384]{1,0:T(8,128)(2,1)} %project.1.da, bf16[512,384]{1,0:T(8,128)(2,1)} %copy-done.4, ...), custom_call_target="tpu_custom_call" | custom-call | flops 2013265920 | bytes 6291456 | tf_op jit(solution)/shard_map/backward_far/pallas_call | solution.py:369
  109.3 1.9 collective-permute-start.14
  113.7 4.0 %weight_far.1 = (bf16[640,384]{1,0:T(8,128)(2,1)}, bf16[640,384]{1,0:T(8,128)(2,1)}) custom-call(s32[4]{0:T(128)} %pad_add_fusion.place, bf16[512,5120]{1,0:T(8,128)(2,1)} %all-gather.2.cloned.1.call-done.grad, bf16[512,384]{1,0:T(8,128)(2,1)} %add_convert_fusion.2.attn), custom_call_target="tpu_custom_call" | custom-call | flops 503316480 | bytes 3145728 | tf_op jit(solution)/shard_map/weight_far/pallas_call | solution.py:276
  119.5 2.1 %collective-permute-start.19 = (bf16[640,384]{1,0:T(8,128)(2,1)}, bf16[640,384]{1,0:T(8,128)(2,1)S(1)}, u32[]{:S(2)}, u32[]{:S(2)}) collective-permute-start(bf16[640,384]{1,0:T(8,128)(2,1)} %get-tuple-element.59), channel_id=1, source_target_pairs={{0,96},{8,104},{16,112},{24,120},{32,0},{40,8},{48,16},{56,24},{64... | collective-permute-start | bytes 1474568 | tf_op jit(solution)/shard_map/ppermute | solution.py:408
  123.1 10.5 %backward_near.1 = (bf16[8,2,64,384]{3,2,1,0:T(8,128)(2,1)}, bf16[8,2,64,384]{3,2,1,0:T(8,128)(2,1)}, f32[384,1024]{1,0:T(8,128)}) custom-call(bf16[8,64,384]{2,1,0:T(8,128)(2,1)} %copy-done.9, bf16[8,64,384]{2,1,0:T(8,128)(2,1)} %copy-done.20, bf16[512,384]{1,0:T(8,128)(2,1)} %project.1.da, bf16[512,384]{1,0:T(8,128)(2,1)} %copy-done.4, ...), custom_call_target="tpu_custom_call" | custom-call | flops 4026531840 | bytes 9437184 | tf_op jit(solution)/shard_map/backward_near/pallas_call | solution.py:382
  133.7 3.2 %collective-permute-start.17 = (bf16[8,2,64,384]{3,2,1,0:T(8,128)(2,1)}, bf16[8,2,64,384]{3,2,1,0:T(8,128)(2,1)}, u32[]{:S(2)}, u32[]{:S(2)}) collective-permute-start(bf16[8,2,64,384]{3,2,1,0:T(8,128)(2,1)} %get-tuple-element.66), channel_id=1, source_target_pairs={{0,24},{8,0},{16,8},{24,16},{32,56},{40,32},{48,40},{56,48},{1,25}... | collective-permute-start | bytes 2359304 | tf_op jit(solution)/shard_map/ppermute | solution.py:408
  136.9 6.8 %backward_own.1 = (f32[8,2,64,384]{3,2,1,0:T(8,128)}, f32[8,64,384]{2,1,0:T(8,128)}, bf16[8,64,384]{2,1,0:T(8,128)(2,1)}) custom-call(bf16[8,64,384]{2,1,0:T(8,128)(2,1)} %copy-done.9, bf16[8,64,384]{2,1,0:T(8,128)(2,1)} %copy-done.20, bf16[512,384]{1,0:T(8,128)(2,1)} %project.1.da, bf16[512,384]{1,0:T(8,128)(2,1)} %copy-done.4, f32[3,8,1024]{2,1,0:T(8,128)} %copy-done.7, ...), custom_call_target="tpu_custom_call" | custom-call | flops 2013265920 | bytes 8388608 | tf_op jit(solution)/shard_map/backward_own/pallas_call | solution.py:395
  145.4 6.4 %weight_near.1 = (bf16[1280,384]{1,0:T(8,128)(2,1)}, bf16[1280,384]{1,0:T(8,128)(2,1)}) custom-call(s32[4]{0:T(128)} %pad_add_fusion.place, bf16[512,5120]{1,0:T(8,128)(2,1)} %all-gather.2.cloned.1.call-done.grad, bf16[512,384]{1,0:T(8,128)(2,1)} %add_convert_fusion.2.attn, bf16[640,384]{1,0:T(8,128)(2,1)} %copy-done.18, bf16[640,384]{1,0:T(8,128)(2,1)} %copy-done.19), custom_call_target="tpu_custom_call" | custom-call | flops 1006632960 | bytes 6291456 | tf_op jit(solution)/shard_map/weight_near/pallas_call | solution.py:276
  151.8 2.1 %collective-permute-start.21 = (bf16[1280,384]{1,0:T(8,128)(2,1)}, bf16[1280,384]{1,0:T(8,128)(2,1)S(1)}, u32[]{:S(2)}, u32[]{:S(2)}) collective-permute-start(bf16[1280,384]{1,0:T(8,128)(2,1)} %get-tuple-element.70), channel_id=1, source_target_pairs={{0,32},{8,40},{16,48},{24,56},{32,64},{40,72},{48,80},{56,88},{64,... | collective-permute-start | bytes 2949128 | tf_op jit(solution)/shard_map/ppermute | solution.py:408
  158.0 4.4 %all-to-all-start.1 = ((bf16[8,3,64,384]{3,2,1,0:T(8,128)(2,1)}), bf16[8,3,64,384]{3,2,1,0:T(8,128)(2,1)S(1)}, u32[]{:S(2)}, u32[]{:S(2)}) async-start(bf16[8,3,64,384]{3,2,1,0:T(8,128)(2,1)} %pad_maximum_fusion), calls=%async_computation.1 | async-start | bytes 2359296 | tf_op jit(solution)/shard_map/all_to_all | solution.py:429
  162.4 4.5 %weight_own.1.mine = f32[1280,384]{1,0:T(8,128)} custom-call(s32[4]{0:T(128)} %pad_add_fusion.place, bf16[512,5120]{1,0:T(8,128)(2,1)} %all-gather.2.cloned.1.call-done.grad, bf16[512,384]{1,0:T(8,128)(2,1)} %add_convert_fusion.2.attn), custom_call_target="tpu_custom_call" | custom-call | flops 503316480 | bytes 3145728 | tf_op jit(solution)/shard_map/weight_own/pallas_call | solution.py:276
  166.9 6.0 %collective-permute-done.22.above = bf16[1280,384]{1,0:T(8,128)(2,1)S(1)} collective-permute-done((bf16[1280,384]{1,0:T(8,128)(2,1)}, bf16[1280,384]{1,0:T(8,128)(2,1)S(1)}, u32[]{:S(2)}, u32[]{:S(2)}) %collective-permute-start.22) | collective-permute-done | bytes 983072 | tf_op jit(solution)/shard_map/ppermute | solution.py:408
  174.9 3.3 %weight_sum.1 = (f32[320,384]{1,0:T(8,128)}, bf16[320,384]{1,0:T(8,128)(2,1)}, bf16[320,384]{1,0:T(8,128)(2,1)}, bf16[320,384]{1,0:T(8,128)(2,1)}) custom-call(s32[4]{0:T(128)} %pad_add_fusion.place, f32[1280,384]{1,0:T(8,128)} %weight_own.1.mine, bf16[1280,384]{1,0:T(8,128)(2,1)} %copy-done.11, bf16[1280,384]{1,0:T(8,128)(2,1)} %copy-done.12), custom_call_target="tpu_custom_call" | custom-call | flops 1048576 | bytes 5242880 | tf_op jit(solution)/shard_map/weight_sum/pallas_call | solution.py:264
  181.5 7.0 %collective-permute-done.23 = bf16[320,384]{1,0:T(8,128)(2,1)S(1)} collective-permute-done((bf16[320,384]{1,0:T(8,128)(2,1)}, bf16[320,384]{1,0:T(8,128)(2,1)S(1)}, u32[]{:S(2)}, u32[]{:S(2)}) %collective-permute-start.23) | collective-permute-done | bytes 245792 | tf_op jit(solution)/shard_map/ppermute | solution.py:408
  189.4 1.9 convert_add_fusion
  (111 shorter events, 40.6 us)
Async XLA Ops:
  7.2 69.2 %all-gather.2.cloned.1.call-start = ((), (), s32[]{:S(2)}) async-start(), calls=%async_computation.2 | async-start | bytes 5898240 | tf_op jit(solution)/shard_map/all_gather | solution.py:445
  11.3 29.2 %all-to-all-start = ((bf16[8,3,64,384]{3,2,1,0:T(8,128)(2,1)}), bf16[8,3,64,384]{3,2,1,0:T(8,128)(2,1)S(1)}, u32[]{:S(2)}, u32[]{:S(2)}) async-start(bf16[8,3,64,384]{3,2,1,0:T(8,128)(2,1)} %maximum_bitcast_fusion), calls=%async_computation | async-start | bytes 2359296 | tf_op jit(solution)/shard_map/all_to_all | solution.py:429
  15.8 10.3 %collective-permute-start.1 = (bf16[320,384]{1,0:T(8,128)(2,1)S(1)}, bf16[320,384]{1,0:T(8,128)(2,1)S(1)}, u32[]{:S(2)}, u32[]{:S(2)}) collective-permute-start(bf16[320,384]{1,0:T(8,128)(2,1)S(1)} %copy-done.5), channel_id=1, source_target_pairs={{0,16},{8,24},{16,0},{24,8},{32,48},{40,56},{48,32},{56,40},{1,17}... | collective-permute-start | bytes 737288 | tf_op jit(solution)/shard_map/ppermute | solution.py:408
  19.1 12.3 %collective-permute-start = (bf16[320,384]{1,0:T(8,128)(2,1)S(1)}, bf16[320,384]{1,0:T(8,128)(2,1)S(1)}, u32[]{:S(2)}, u32[]{:S(2)}) collective-permute-start(bf16[320,384]{1,0:T(8,128)(2,1)S(1)} %copy-done.5), channel_id=1, source_target_pairs={{0,24},{8,0},{16,8},{24,16},{32,56},{40,32},{48,40},{56,48},{1,25}... | collective-permute-start | bytes 737288 | tf_op jit(solution)/shard_map/ppermute | solution.py:408
  20.1 11.2 %collective-permute-start.2 = (bf16[320,384]{1,0:T(8,128)(2,1)S(1)}, bf16[320,384]{1,0:T(8,128)(2,1)S(1)}, u32[]{:S(2)}, u32[]{:S(2)}) collective-permute-start(bf16[320,384]{1,0:T(8,128)(2,1)S(1)} %copy-done.5), channel_id=1, source_target_pairs={{0,8},{8,16},{16,24},{24,0},{32,40},{40,48},{48,56},{56,32},{1,9},... | collective-permute-start | bytes 737288 | tf_op jit(solution)/shard_map/ppermute | solution.py:408
  31.4 25.8 %collective-permute-start.8 = (bf16[1280,384]{1,0:T(8,128)(2,1)S(1)}, bf16[1280,384]{1,0:T(8,128)(2,1)S(1)}, u32[]{:S(2)}, u32[]{:S(2)}) collective-permute-start(bf16[1280,384]{1,0:T(8,128)(2,1)S(1)} %stack_rows.1.w0), channel_id=1, source_target_pairs={{0,32},{8,40},{16,48},{24,56},{32,64},{40,72},{48,80},{56,88},{64,... | collective-permute-start | bytes 2949128 | tf_op jit(solution)/shard_map/ppermute | solution.py:408
  33.4 24.8 %collective-permute-start.6 = (bf16[1280,384]{1,0:T(8,128)(2,1)S(1)}, bf16[1280,384]{1,0:T(8,128)(2,1)}, u32[]{:S(2)}, u32[]{:S(2)}) collective-permute-start(bf16[1280,384]{1,0:T(8,128)(2,1)S(1)} %stack_rows.1.w0), channel_id=1, source_target_pairs={{0,96},{8,104},{16,112},{24,120},{32,0},{40,8},{48,16},{56,24},{64... | collective-permute-start | bytes 2949128 | tf_op jit(solution)/shard_map/ppermute | solution.py:408
  40.6 19.5 %copy-start.13 = (bf16[8,2,64,384]{3,2,1,0:T(8,128)(2,1)}, bf16[8,2,64,384]{3,2,1,0:T(8,128)(2,1)S(1)}, u32[]{:S(2)}) copy-start(bf16[8,2,64,384]{3,2,1,0:T(8,128)(2,1)S(1)} %slice.22.kv0) | copy-start | bytes 2359300
  40.6 21.9 %collective-permute-start.4 = (bf16[8,2,64,384]{3,2,1,0:T(8,128)(2,1)S(1)}, bf16[8,2,64,384]{3,2,1,0:T(8,128)(2,1)}, u32[]{:S(2)}, u32[]{:S(2)}) collective-permute-start(bf16[8,2,64,384]{3,2,1,0:T(8,128)(2,1)S(1)} %slice.22.kv0), channel_id=1, source_target_pairs={{0,8},{8,16},{16,24},{24,0},{32,40},{40,48},{48,56},{56,32},{1,9},... | collective-permute-start | bytes 2359304 | tf_op jit(solution)/shard_map/ppermute | solution.py:408
  42.3 25.0 %collective-permute-start.5 = (bf16[8,2,64,384]{3,2,1,0:T(8,128)(2,1)S(1)}, bf16[8,2,64,384]{3,2,1,0:T(8,128)(2,1)}, u32[]{:S(2)}, u32[]{:S(2)}) collective-permute-start(bf16[8,2,64,384]{3,2,1,0:T(8,128)(2,1)S(1)} %slice.22.kv0), channel_id=1, source_target_pairs={{0,24},{8,0},{16,8},{24,16},{32,56},{40,32},{48,40},{56,48},{1,25}... | collective-permute-start | bytes 2359304 | tf_op jit(solution)/shard_map/ppermute | solution.py:408
  44.1 23.2 %copy-start.9 = (bf16[8,64,384]{2,1,0:T(8,128)(2,1)}, bf16[8,64,384]{2,1,0:T(8,128)(2,1)S(1)}, u32[]{:S(2)}) copy-start(bf16[8,64,384]{2,1,0:T(8,128)(2,1)S(1)} %slice_bitcast_fusion.3.qa) | copy-start | bytes 1179652
  44.1 22.4 %collective-permute-start.3 = (bf16[8,64,384]{2,1,0:T(8,128)(2,1)S(1)}, bf16[8,64,384]{2,1,0:T(8,128)(2,1)S(1)}, u32[]{:S(2)}, u32[]{:S(2)}) collective-permute-start(bf16[8,64,384]{2,1,0:T(8,128)(2,1)S(1)} %slice_bitcast_fusion.3.qa), channel_id=1, source_target_pairs={{0,32},{8,40},{16,48},{24,56},{32,0},{40,8},{48,16},{56,24},{1,33}... | collective-permute-start | bytes 1179656 | tf_op jit(solution)/shard_map/ppermute | solution.py:408
  57.2 19.1 %copy-start.8 = (bf16[1280,384]{1,0:T(8,128)(2,1)}, bf16[1280,384]{1,0:T(8,128)(2,1)S(1)}, u32[]{:S(2)}) copy-start(bf16[1280,384]{1,0:T(8,128)(2,1)S(1)} %collective-permute-done.8.w3) | copy-start | bytes 2949124
  57.2 19.0 %collective-permute-start.9 = (bf16[640,384]{1,0:T(8,128)(2,1)S(1)}, bf16[640,384]{1,0:T(8,128)(2,1)S(1)}, u32[]{:S(2)}, u32[]{:S(2)}) collective-permute-start(bf16[640,384]{1,0:T(8,128)(2,1)S(1)} %slice.29), channel_id=1, source_target_pairs={{0,32},{8,40},{16,48},{24,56},{32,64},{40,72},{48,80},{56,88},{64,... | collective-permute-start | bytes 1474568 | tf_op jit(solution)/shard_map/ppermute | solution.py:408
  60.0 16.3 %collective-permute-start.7 = (bf16[640,384]{1,0:T(8,128)(2,1)}, bf16[640,384]{1,0:T(8,128)(2,1)S(1)}, u32[]{:S(2)}, u32[]{:S(2)}) collective-permute-start(bf16[640,384]{1,0:T(8,128)(2,1)} %slice.28), channel_id=1, source_target_pairs={{0,96},{8,104},{16,112},{24,120},{32,0},{40,8},{48,16},{56,24},{64... | collective-permute-start | bytes 1474568 | tf_op jit(solution)/shard_map/ppermute | solution.py:408
  62.4 21.9 %collective-permute-start.11 = (bf16[8,2,64,384]{3,2,1,0:T(8,128)(2,1)}, bf16[8,2,64,384]{3,2,1,0:T(8,128)(2,1)S(1)}, u32[]{:S(2)}, u32[]{:S(2)}) collective-permute-start(bf16[8,2,64,384]{3,2,1,0:T(8,128)(2,1)} %collective-permute-done.4.kv1), channel_id=1, source_target_pairs={{0,8},{8,16},{16,24},{24,0},{32,40},{40,48},{48,56},{56,32},{1,9},... | collective-permute-start | bytes 2359304 | tf_op jit(solution)/shard_map/ppermute | solution.py:408
  84.2 9.3 %collective-permute-start.10 = (bf16[512,384]{1,0:T(8,128)(2,1)}, bf16[512,384]{1,0:T(8,128)(2,1)S(1)}, u32[]{:S(2)}, u32[]{:S(2)}) collective-permute-start(bf16[512,384]{1,0:T(8,128)(2,1)} %project.1.da), channel_id=1, source_target_pairs={{0,32},{8,40},{16,48},{24,56},{32,0},{40,8},{48,16},{56,24},{1,33}... | collective-permute-start | bytes 1179656 | tf_op jit(solution)/shard_map/ppermute | solution.py:408
  96.6 4.9 %collective-permute-start.12 = (f32[3,8,1024]{2,1,0:T(8,128)S(1)}, f32[3,8,1024]{2,1,0:T(8,128)S(1)}, u32[]{:S(2)}, u32[]{:S(2)}) collective-permute-start(f32[3,8,1024]{2,1,0:T(8,128)S(1)} %row_dots.1.st_ref), channel_id=1, source_target_pairs={{0,32},{8,40},{16,48},{24,56},{32,0},{40,8},{48,16},{56,24},{1,33}... | collective-permute-start | bytes 294920 | tf_op jit(solution)/shard_map/ppermute | solution.py:408
  102.8 10.1 %collective-permute-start.13 = (bf16[512,384]{1,0:T(8,128)(2,1)S(1)}, bf16[512,384]{1,0:T(8,128)(2,1)S(1)}, u32[]{:S(2)}, u32[]{:S(2)}) collective-permute-start(bf16[512,384]{1,0:T(8,128)(2,1)S(1)} %get-tuple-element.56), channel_id=1, source_target_pairs={{0,32},{8,40},{16,48},{24,56},{32,0},{40,8},{48,16},{56,24},{1,33}... | collective-permute-start | bytes 1179656 | tf_op jit(solution)/shard_map/ppermute | solution.py:408
  109.3 12.3 %collective-permute-start.14 = (bf16[4,2,64,384]{3,2,1,0:T(8,128)(2,1)}, bf16[4,2,64,384]{3,2,1,0:T(8,128)(2,1)S(1)}, u32[]{:S(2)}, u32[]{:S(2)}) collective-permute-start(bf16[4,2,64,384]{3,2,1,0:T(8,128)(2,1)} %get-tuple-element.61), channel_id=1, source_target_pairs={{0,8},{8,16},{16,24},{24,0},{32,40},{40,48},{48,56},{56,32},{1,9},... | collective-permute-start | bytes 1179656 | tf_op jit(solution)/shard_map/ppermute | solution.py:408
  111.2 10.4 %collective-permute-start.15 = (bf16[4,2,64,384]{3,2,1,0:T(8,128)(2,1)}, bf16[4,2,64,384]{3,2,1,0:T(8,128)(2,1)S(1)}, u32[]{:S(2)}, u32[]{:S(2)}) collective-permute-start(bf16[4,2,64,384]{3,2,1,0:T(8,128)(2,1)} %get-tuple-element.62), channel_id=1, source_target_pairs={{0,24},{8,0},{16,8},{24,16},{32,56},{40,32},{48,40},{56,48},{1,25}... | collective-permute-start | bytes 1179656 | tf_op jit(solution)/shard_map/ppermute | solution.py:408
  117.7 26.1 %collective-permute-start.18 = (bf16[640,384]{1,0:T(8,128)(2,1)}, bf16[640,384]{1,0:T(8,128)(2,1)S(1)}, u32[]{:S(2)}, u32[]{:S(2)}) collective-permute-start(bf16[640,384]{1,0:T(8,128)(2,1)} %get-tuple-element.58), channel_id=1, source_target_pairs={{0,32},{8,40},{16,48},{24,56},{32,64},{40,72},{48,80},{56,88},{64,... | collective-permute-start | bytes 1474568 | tf_op jit(solution)/shard_map/ppermute | solution.py:408
  119.5 24.4 %collective-permute-start.19 = (bf16[640,384]{1,0:T(8,128)(2,1)}, bf16[640,384]{1,0:T(8,128)(2,1)S(1)}, u32[]{:S(2)}, u32[]{:S(2)}) collective-permute-start(bf16[640,384]{1,0:T(8,128)(2,1)} %get-tuple-element.59), channel_id=1, source_target_pairs={{0,96},{8,104},{16,112},{24,120},{32,0},{40,8},{48,16},{56,24},{64... | collective-permute-start | bytes 1474568 | tf_op jit(solution)/shard_map/ppermute | solution.py:408
  133.6 21.6 %collective-permute-start.16 = (bf16[8,2,64,384]{3,2,1,0:T(8,128)(2,1)}, bf16[8,2,64,384]{3,2,1,0:T(8,128)(2,1)S(1)}, u32[]{:S(2)}, u32[]{:S(2)}) collective-permute-start(bf16[8,2,64,384]{3,2,1,0:T(8,128)(2,1)} %get-tuple-element.65), channel_id=1, source_target_pairs={{0,8},{8,16},{16,24},{24,0},{32,40},{40,48},{48,56},{56,32},{1,9},... | collective-permute-start | bytes 2359304 | tf_op jit(solution)/shard_map/ppermute | solution.py:408
  133.7 21.5 %collective-permute-start.17 = (bf16[8,2,64,384]{3,2,1,0:T(8,128)(2,1)}, bf16[8,2,64,384]{3,2,1,0:T(8,128)(2,1)}, u32[]{:S(2)}, u32[]{:S(2)}) collective-permute-start(bf16[8,2,64,384]{3,2,1,0:T(8,128)(2,1)} %get-tuple-element.66), channel_id=1, source_target_pairs={{0,24},{8,0},{16,8},{24,16},{32,56},{40,32},{48,40},{56,48},{1,25}... | collective-permute-start | bytes 2359304 | tf_op jit(solution)/shard_map/ppermute | solution.py:408
  143.8 11.4 %collective-permute-start.20 = (bf16[8,64,384]{2,1,0:T(8,128)(2,1)}, bf16[8,64,384]{2,1,0:T(8,128)(2,1)S(1)}, u32[]{:S(2)}, u32[]{:S(2)}) collective-permute-start(bf16[8,64,384]{2,1,0:T(8,128)(2,1)} %get-tuple-element.68), channel_id=1, source_target_pairs={{0,32},{8,40},{16,48},{24,56},{32,0},{40,8},{48,16},{56,24},{1,33}... | collective-permute-start | bytes 1179656 | tf_op jit(solution)/shard_map/ppermute | solution.py:408
  151.8 21.1 %collective-permute-start.21 = (bf16[1280,384]{1,0:T(8,128)(2,1)}, bf16[1280,384]{1,0:T(8,128)(2,1)S(1)}, u32[]{:S(2)}, u32[]{:S(2)}) collective-permute-start(bf16[1280,384]{1,0:T(8,128)(2,1)} %get-tuple-element.70), channel_id=1, source_target_pairs={{0,32},{8,40},{16,48},{24,56},{32,64},{40,72},{48,80},{56,88},{64,... | collective-permute-start | bytes 2949128 | tf_op jit(solution)/shard_map/ppermute | solution.py:408
  153.9 19.0 %collective-permute-start.22 = (bf16[1280,384]{1,0:T(8,128)(2,1)}, bf16[1280,384]{1,0:T(8,128)(2,1)S(1)}, u32[]{:S(2)}, u32[]{:S(2)}) collective-permute-start(bf16[1280,384]{1,0:T(8,128)(2,1)} %get-tuple-element.73), channel_id=1, source_target_pairs={{0,96},{8,104},{16,112},{24,120},{32,0},{40,8},{48,16},{56,24},{64... | collective-permute-start | bytes 2949128 | tf_op jit(solution)/shard_map/ppermute | solution.py:408
  158.0 33.2 %all-to-all-start.1 = ((bf16[8,3,64,384]{3,2,1,0:T(8,128)(2,1)}), bf16[8,3,64,384]{3,2,1,0:T(8,128)(2,1)S(1)}, u32[]{:S(2)}, u32[]{:S(2)}) async-start(bf16[8,3,64,384]{3,2,1,0:T(8,128)(2,1)} %pad_maximum_fusion), calls=%async_computation.1 | async-start | bytes 2359296 | tf_op jit(solution)/shard_map/all_to_all | solution.py:429
  178.2 10.3 %collective-permute-start.23 = (bf16[320,384]{1,0:T(8,128)(2,1)}, bf16[320,384]{1,0:T(8,128)(2,1)S(1)}, u32[]{:S(2)}, u32[]{:S(2)}) collective-permute-start(bf16[320,384]{1,0:T(8,128)(2,1)} %get-tuple-element.75), channel_id=1, source_target_pairs={{0,8},{8,16},{16,24},{24,0},{32,40},{40,48},{48,56},{56,32},{1,9},... | collective-permute-start | bytes 737288 | tf_op jit(solution)/shard_map/ppermute | solution.py:408
  178.2 10.3 %collective-permute-start.24 = (bf16[320,384]{1,0:T(8,128)(2,1)}, bf16[320,384]{1,0:T(8,128)(2,1)S(1)}, u32[]{:S(2)}, u32[]{:S(2)}) collective-permute-start(bf16[320,384]{1,0:T(8,128)(2,1)} %get-tuple-element.76), channel_id=1, source_target_pairs={{0,16},{8,24},{16,0},{24,8},{32,48},{40,56},{48,32},{56,40},{1,17}... | collective-permute-start | bytes 737288 | tf_op jit(solution)/shard_map/ppermute | solution.py:408
  180.1 9.3 %collective-permute-start.25 = (bf16[320,384]{1,0:T(8,128)(2,1)}, bf16[320,384]{1,0:T(8,128)(2,1)S(1)}, u32[]{:S(2)}, u32[]{:S(2)}) collective-permute-start(bf16[320,384]{1,0:T(8,128)(2,1)} %get-tuple-element.77), channel_id=1, source_target_pairs={{0,24},{8,0},{16,8},{24,16},{32,56},{40,32},{48,40},{56,48},{1,25}... | collective-permute-start | bytes 737288 | tf_op jit(solution)/shard_map/ppermute | solution.py:408
  (22 other events, 63.3 us)
Sparse Core Ops, SparseCore 0:
  9.7 45.8 all-gather.1
